TPU v7x, 256 devices: a whole 4x4x8 slice. The times are simulated.
256 devices in a mesh: gx: 32 (over x, z_lo, core), gy: 8 (over y, z_hi).
Axes of the slice: x: 4, y: 4, z: 8 (z_hi: 2, z_lo: 4; z = z_hi * 4 + z_lo), core: 2. Of those that a mesh axis runs over, the one named last changes fastest.
Arguments:
- temp_old: float32 [512, 256, 1024], P('gx', 'gy'), may hold values from -6 to 6
- capacity: float32 [512, 256, 1024], P('gx', 'gy'), may hold values from 0.05 to 0.5
- soil_class: int32 [512, 256, 1024], P('gx', 'gy'), may hold values from 0 to 7
- cond_table: float32 [8], replicated, may hold values from 0.3 to 3
- losses: float32 [65536, 128], P(('gx', 'gy')), may hold values from 0.1 to 10
- owner: int32 [65536, 1], P(('gx', 'gy')), may hold values from 0 to 7; in each aligned block of 256 rows (0 to 255, 256 to 511, ...) at most 64 rows name the same one
- column: int32 [65536], P(('gx', 'gy')), may hold values from 0 to 511
- injection: float32 [128, 1024], replicated, may hold values from -0.5 to 0.5
Outputs:
- temp_new: float32 [512, 256, 1024], P('gx', 'gy')
Inputs may be any that keep to these rules, and one draw needn't show every extreme that they name: In each device's block of 256 rows no owner is named by more than 64 rows, a bound that some block reaches.
All inputs are finite; a program needn't handle non-finite values.
Results may differ from a plain program's by a relative error of at most 0.000061.
Values sent between devices are 32-bit elements; how exact they have to be, the bound alone decides.
No kernel may reach another device: no remote copies, remote signals or barrier semaphores. Data moves between devices by JAX's collectives and lax.ppermute only.
A program may use at most 64 MiB of HBM per device.

v0:
```python
import jax
import jax.numpy as jnp
from jax import lax
from jax.experimental import pallas as pl
from jax.experimental.pallas import tpu as pltpu
from jax.sharding import PartitionSpec as P

SWEEPS = 4
NCLS = 8
CX, CY, NZ = 16, 32, 1024
LW = 128
SEG = 256
CAP = 64
NGX, NGY = 32, 8
CHUNK = CAP + 8
YT = 8
NT = CY // YT
PARTS = 4
F32, BF16 = jnp.float32, jnp.bfloat16
HIGH = lax.Precision.HIGHEST
VM = pl.BlockSpec(memory_space=pltpu.VMEM)
SM = pl.BlockSpec(memory_space=pltpu.SMEM)
HB = pl.BlockSpec(memory_space=pltpu.HBM)


def local(*dims, dtype=F32):
    return pltpu.VMEM(dims, dtype)


def near(*arrays):
    return [pltpu.with_memory_space_constraint(a, pltpu.VMEM) for a in arrays]


def far(*arrays):
    return [pltpu.with_memory_space_constraint(a, pltpu.HBM) for a in arrays]


def lookup(klass, table):
    cond = jnp.where(klass == 0, table[0], F32(0.0))
    for k in range(1, NCLS):
        cond = jnp.where(klass == k, table[k], cond)
    return cond


def load(pairs, sems):
    copies = [pltpu.make_async_copy(src, dst, sems.at[i]) for i, (src, dst) in enumerate(pairs)]
    for copy in copies:
        copy.start()
    for copy in copies:
        copy.wait()


def even(axis):
    return lax.rem(lax.axis_index(axis), 2) == 0


def split(a, b, is_even):
    return jnp.where(is_even, b, a), jnp.where(is_even, a, b)


def start_kernel(t_hbm, soil_hbm, loss_hbm, owner_hbm, col_hbm, send_ref, xa, xb, ya, yb,
                 t_lo, t_hi, s_lo, s_hi, tx, sx, loss_ref, owner_ref, col_ref, sems):
    pairs = [(loss_hbm, loss_ref), (owner_hbm, owner_ref), (col_hbm, col_ref),
             (t_hbm.at[:, 0:YT], t_lo), (t_hbm.at[:, CY - YT:CY], t_hi),
             (soil_hbm.at[:, 0:YT], s_lo), (soil_hbm.at[:, CY - YT:CY], s_hi),
             (t_hbm.at[0], tx.at[0]), (t_hbm.at[CX - 1], tx.at[1]),
             (soil_hbm.at[0], sx.at[0]), (soil_hbm.at[CX - 1], sx.at[1])]
    copies = [pltpu.make_async_copy(src, dst, sems.at[i]) for i, (src, dst) in enumerate(pairs)]
    for copy in copies:
        copy.start()
    for copy in copies[:3]:
        copy.wait()
    own = owner_ref[...]
    mine = lax.broadcasted_iota(jnp.int32, (NGY, SEG), 0) == own
    before = lax.broadcasted_iota(jnp.int32, (SEG, SEG), 0) < lax.broadcasted_iota(jnp.int32, (SEG, SEG), 1)
    count = jnp.dot(mine.astype(F32).astype(BF16), before.astype(F32).astype(BF16), preferred_element_type=F32)
    rank = jnp.sum(jnp.where(mine, count, 0.0), axis=0, keepdims=True).astype(jnp.int32)
    slot = own * CAP + rank
    pick = (lax.broadcasted_iota(jnp.int32, (NGY * CAP, SEG), 0) == slot).astype(F32).astype(BF16)
    loss = loss_ref[...]
    sent = jnp.zeros((NGY * CAP, LW), F32)
    for _ in range(3):
        part = loss.astype(BF16)
        loss = loss - part.astype(F32)
        sent = sent + jnp.dot(pick, part, preferred_element_type=F32)
    col = jnp.broadcast_to(col_ref[...], (8, SEG))
    low = lax.rem(col, 128)
    by_lane = (((1,), (1,)), ((), ()))
    cols = lax.dot_general(low.astype(F32).astype(BF16), pick, by_lane, preferred_element_type=F32)
    cols = cols + lax.dot_general((col - low).astype(F32).astype(BF16), pick, by_lane, preferred_element_type=F32)
    for o in range(NGY):
        send_ref[o * CHUNK:o * CHUNK + CAP, :] = sent[o * CAP:(o + 1) * CAP, :]
        crow = cols[:, o * CAP:(o + 1) * CAP]
        send_ref[o * CHUNK + CAP:(o + 1) * CHUNK, :] = jnp.concatenate([crow, crow], axis=1)
    for copy in copies[3:]:
        copy.wait()
    even_x, even_y = even("gx"), even("gy")
    for x in range(CX):
        ya[x:x + 1, :], yb[x:x + 1, :] = split(t_lo[x, 0:1, :], t_hi[x, YT - 1:YT, :], even_y)
        s_a, s_b = split(s_lo[x, 0:1, :], s_hi[x, YT - 1:YT, :], even_y)
        ya[CX + x:CX + x + 1, :] = s_a.astype(F32)
        yb[CX + x:CX + x + 1, :] = s_b.astype(F32)
    xa[0:CY, :], xb[0:CY, :] = split(tx[0], tx[1], even_x)
    s_a, s_b = split(sx[0], sx[1], even_x)
    xa[CY:, :] = s_a.astype(F32)
    xb[CY:, :] = s_b.astype(F32)


def add_source(recv_ref, inj, out_ref):
    lane = lax.broadcasted_iota(jnp.int32, (1, 2 * CAP), 1)
    cell = lax.broadcasted_iota(jnp.int32, (CX * CY, 2 * CAP), 0)
    pick, loss = [], []
    for g in range(0, NGY, 2):
        a, b = g * CHUNK, (g + 1) * CHUNK
        crow = jnp.where(lane < CAP, recv_ref[a + CAP:a + CAP + 1, :], recv_ref[b + CAP:b + CAP + 1, :])
        pick.append((cell == crow.astype(jnp.int32)).astype(F32).astype(BF16))
        loss += [recv_ref[a:a + CAP, :], recv_ref[b:b + CAP, :]]
    pick = jnp.concatenate(pick, axis=1)
    loss = jnp.concatenate(loss, axis=0)
    gathered = jnp.zeros((CX * CY, LW), F32)
    for _ in range(3):
        part = loss.astype(BF16)
        loss = loss - part.astype(F32)
        gathered = gathered + jnp.dot(pick, part, preferred_element_type=F32)
    high = gathered.astype(BF16)
    low = (gathered - high.astype(F32)).astype(BF16)
    left = jnp.concatenate([high, low, high], axis=1)
    width = 256
    for n in range(0, NZ, width):
        cut = slice(n, n + width)
        both = inj[:, cut]
        top = both.astype(BF16)
        right = jnp.concatenate([top, top, (both - top.astype(F32)).astype(BF16)], axis=0)
        out_ref[:, :, cut] = jnp.dot(left, right, preferred_element_type=F32).reshape(CX, CY, width)


def tile_sides(ref, x, yt):
    mid = ref[x, yt * YT:(yt + 1) * YT, :]
    row = lax.broadcasted_iota(jnp.int32, (YT, NZ), 0)
    up, down = pltpu.roll(mid, YT - 1, 0), pltpu.roll(mid, 1, 0)
    if yt < NT - 1:
        up = jnp.where(row == YT - 1, ref[x, (yt + 1) * YT:(yt + 1) * YT + 1, :], up)
    if yt > 0:
        down = jnp.where(row == 0, ref[x, yt * YT - 1:yt * YT, :], down)
    return mid, up, down


def prepare_kernel(recv_ref, table_ref, t_hbm, cap_hbm, soil_hbm, inj_hbm,
                   fx_ref, fy_ref, fz_ref, w_ref, rhs_ref, tn_ref, cx_ref, ey_ref, t_ref, cond, soil, cap, inj, sems):
    copies = []
    step = CX // PARTS
    for part in range(PARTS):
        span = pl.ds(part * step, step)
        for k, (src, dst) in enumerate(((soil_hbm, soil), (t_hbm, t_ref), (cap_hbm, cap))):
            copies.append(pltpu.make_async_copy(src.at[span], dst.at[span], sems.at[3 * part + k]))
    copies.append(pltpu.make_async_copy(inj_hbm, inj, sems.at[3 * PARTS]))
    for copy in copies:
        copy.start()
    table = [table_ref[k] for k in range(NCLS)]

    def fill(x, carry):
        cond[x] = lookup(soil[x], table)
        return carry

    copies[-1].wait()
    add_source(recv_ref, inj, rhs_ref)
    for part in range(PARTS):
        copies[3 * part].wait()
        lax.fori_loop(part * step, (part + 1) * step, fill, 0)
    for part in range(PARTS):
        copies[3 * part + 1].wait()
        copies[3 * part + 2].wait()
    cx_ref[0] = cond[0]
    cx_ref[1] = cond[CX - 1]
    row = lax.broadcasted_iota(jnp.int32, (YT, NZ), 0)
    lane = lax.broadcasted_iota(jnp.int32, (YT, NZ), 1)

    def plane(x, first, last):
        for yt in range(NT):
            rows = slice(yt * YT, (yt + 1) * YT)
            low, high = yt == 0, yt == NT - 1
            c, cyp, cym = tile_sides(cond, x, yt)
            half = 0.5 * c
            fxp = half if last else 0.5 * (c + cond[x + 1, rows, :])
            fxm = half if first else 0.5 * (c + cond[x - 1, rows, :])
            fyp, fym = 0.5 * (c + cyp), 0.5 * (c + cym)
            if high:
                fyp = jnp.where(row == YT - 1, half, fyp)
            if low:
                fym = jnp.where(row == 0, half, fym)
            fzp = jnp.where(lane == NZ - 1, half, 0.5 * (c + pltpu.roll(c, NZ - 1, 1)))
            fzm = jnp.where(lane == 0, half, 0.5 * (c + pltpu.roll(c, 1, 1)))
            cp = cap[x, rows, :]
            diag = cp + fxp + fxm + fyp + fym + fzp + fzm
            t, typ, tym = tile_sides(t_ref, x, yt)
            rhs = rhs_ref[x, rows, :] + cp * t
            rhs_ref[x, rows, :] = rhs
            total = rhs
            if not last:
                total = total + fxp * t_ref[x + 1, rows, :]
                fx_ref[x, rows, :] = fxp
            if not first:
                total = total + fxm * t_ref[x - 1, rows, :]
            if high:
                fyp = jnp.where(row == YT - 1, F32(0.0), fyp)
            if low:
                fym = jnp.where(row == 0, F32(0.0), fym)
            fzp = jnp.where(lane == NZ - 1, F32(0.0), fzp)
            fzm = jnp.where(lane == 0, F32(0.0), fzm)
            fy_ref[x, rows, :] = fyp
            fz_ref[x, rows, :] = fzp
            total = total + fyp * typ + fym * tym
            total = total + fzp * pltpu.roll(t, NZ - 1, 1) + fzm * pltpu.roll(t, 1, 1)
            if first or last:
                w_ref[x, rows, :] = diag
                tn_ref[x, rows, :] = total
            else:
                w = 0.8 / diag
                w_ref[x, rows, :] = w
                tn_ref[x, rows, :] = (1.0 - 0.8) * t + w * total
            if low or high:
                at = slice(0, 1) if low else slice(YT - 1, YT)
                side = 0 if low else 1
                for k, value in enumerate((total, diag, c, t)):
                    ey_ref[side, k, pl.ds(x, 1), :] = value[at, :]

    def inner(x, carry):
        plane(x, False, False)
        return carry

    plane(0, True, False)
    lax.fori_loop(1, CX - 1, inner, 0)
    plane(CX - 1, False, True)


def at_row(shape, index, value):
    return jnp.where(lax.broadcasted_iota(jnp.int32, shape, 0) == index, value, F32(0.0))


def with_corners(xlo, xhi, ylo, yhi):
    xs, ys = xlo.shape, ylo.shape
    return (xlo + at_row(xs, 0, ylo[0:1]) + at_row(xs, CY - 1, yhi[0:1]),
            xhi + at_row(xs, 0, ylo[CX - 1:CX]) + at_row(xs, CY - 1, yhi[CX - 1:CX]),
            ylo + at_row(ys, 0, xlo[0:1]) + at_row(ys, CX - 1, xhi[0:1]),
            yhi + at_row(ys, 0, xlo[CY - 1:CY]) + at_row(ys, CX - 1, xhi[CY - 1:CY]))


def fix_kernel(table_ref, hxa, hxb, hya, hyb, t_hbm, w_ref, tn_ref, cx_ref, ey_ref,
               xa, xb, ya, yb, wx_ref, wy_ref, ax_ref, ay_ref, t_edge, sems):
    copies = [pltpu.make_async_copy(t_hbm.at[x], t_edge.at[k], sems.at[k]) for k, x in enumerate((0, CX - 1))]
    for copy in copies:
        copy.start()
    table = [table_ref[k] for k in range(NCLS)]
    gx, gy = lax.axis_index("gx"), lax.axis_index("gy")
    within = [jnp.where(q, F32(1.0), F32(0.0)) for q in (gx > 0, gx < NGX - 1, gy > 0, gy < NGY - 1)]
    t_halo = split(hxa[0:CY, :], hxb[0:CY, :], even("gx")) + split(hya[0:CX, :], hyb[0:CX, :], even("gy"))
    klass = split(hxa[CY:, :], hxb[CY:, :], even("gx")) + split(hya[CX:, :], hyb[CX:, :], even("gy"))
    conds = (cx_ref[0], cx_ref[1], ey_ref[0, 2], ey_ref[1, 2])
    more = [0.5 * lookup(k.astype(jnp.int32), table) * q for k, q in zip(klass, within)]
    face = [(0.5 * c + m) * q for c, m, q in zip(conds, more, within)]
    diag = with_corners(*more)
    total = with_corners(*[f * t for f, t in zip(face, t_halo)])
    for copy in copies:
        copy.wait()
    total = [a + b for a, b in zip(total, (tn_ref[0], tn_ref[CX - 1], ey_ref[0, 0], ey_ref[1, 0]))]
    w = [0.8 / (a + b) for a, b in zip(diag, (w_ref[0], w_ref[CX - 1], ey_ref[0, 1], ey_ref[1, 1]))]
    old = (t_edge[0], t_edge[1], ey_ref[0, 3], ey_ref[1, 3])
    new = [(1.0 - 0.8) * t + a * b for t, a, b in zip(old, w, total)]
    xa[...], xb[...] = split(new[0], new[1], even("gx"))
    ya[...], yb[...] = split(new[2], new[3], even("gy"))
    for k in range(2):
        wx_ref[k], wy_ref[k] = w[k], w[2 + k]
        ax_ref[k], ay_ref[k] = w[k] * face[k], w[2 + k] * face[2 + k]


def faces_of(tn_ref, py_ref, ax_ref, ay_ref, hxa, hxb, hya, hyb):
    halo = split(hxa[...], hxb[...], even("gx")) + split(hya[...], hyb[...], even("gy"))
    terms = with_corners(ax_ref[0] * halo[0], ax_ref[1] * halo[1], ay_ref[0] * halo[2], ay_ref[1] * halo[3])
    return [a + b for a, b in zip(terms, (tn_ref[0], tn_ref[CX - 1], py_ref[0], py_ref[1]))]


def edge_kernel(tn_ref, py_ref, ax_ref, ay_ref, hxa, hxb, hya, hyb, xa, xb, ya, yb):
    new = faces_of(tn_ref, py_ref, ax_ref, ay_ref, hxa, hxb, hya, hyb)
    xa[...], xb[...] = split(new[0], new[1], even("gx"))
    ya[...], yb[...] = split(new[2], new[3], even("gy"))


def put_edges(ref, xlo, xhi, ylo, yhi):
    ref[0] = xlo
    ref[CX - 1] = xhi
    for x in range(1, CX - 1):
        ref[x, 0:1, :] = ylo[x:x + 1]
        ref[x, CY - 1:CY, :] = yhi[x:x + 1]


def sweep_plane(x, first, last, t_ref, fx_ref, fy_ref, fz_ref, w_ref, rhs_ref, tn_ref, py_ref):
    row = lax.broadcasted_iota(jnp.int32, (YT, NZ), 0)
    lane = lax.broadcasted_iota(jnp.int32, (YT, NZ), 1)
    for yt in range(NT):
        rows = slice(yt * YT, (yt + 1) * YT)
        t, typ, tym = tile_sides(t_ref, x, yt)
        fy, _, fym = tile_sides(fy_ref, x, yt)
        if yt == 0:
            fym = jnp.where(row == 0, F32(0.0), fym)
        fz = fz_ref[x, rows, :]
        total = rhs_ref[x, rows, :] + fy * typ + fym * tym
        if not last:
            total = total + fx_ref[x, rows, :] * t_ref[x + 1, rows, :]
        if not first:
            total = total + fx_ref[x - 1, rows, :] * t_ref[x - 1, rows, :]
        total = total + fz * pltpu.roll(t, NZ - 1, 1)
        total = total + jnp.where(lane == 0, F32(0.0), pltpu.roll(fz * t, 1, 1))
        tn = (1.0 - 0.8) * t + w_ref[x, rows, :] * total
        tn_ref[x, rows, :] = tn
        if yt == 0:
            py_ref[0, pl.ds(x, 1), :] = tn[0:1, :]
        if yt == NT - 1:
            py_ref[1, pl.ds(x, 1), :] = tn[YT - 1:YT, :]


def sweep_inside(refs, start=1, stop=CX - 1):
    def inner(x, carry):
        sweep_plane(x, False, False, *refs)
        return carry

    lax.fori_loop(start, stop, inner, 0)


def first_sweep_kernel(fx_ref, fy_ref, fz_ref, rhs_ref, xa, xb, ya, yb, wx_ref, wy_ref, w_in, t_in,
                       w_ref, t_ref, tn_ref, py_ref):
    put_edges(w_ref, wx_ref[0], wx_ref[1], wy_ref[0], wy_ref[1])
    sweep(fx_ref, fy_ref, fz_ref, rhs_ref, w_ref, xa, xb, ya, yb, t_ref, tn_ref, py_ref)


def sweep(fx_ref, fy_ref, fz_ref, rhs_ref, w_ref, xa, xb, ya, yb, t_ref, tn_ref, py_ref):
    put_edges(t_ref, *split(xa[...], xb[...], even("gx")), *split(ya[...], yb[...], even("gy")))
    refs = (t_ref, fx_ref, fy_ref, fz_ref, w_ref, rhs_ref, tn_ref, py_ref)
    sweep_plane(0, True, False, *refs)
    sweep_inside(refs)
    sweep_plane(CX - 1, False, True, *refs)


def sweep_kernel(fx_ref, fy_ref, fz_ref, rhs_ref, w_ref, xa, xb, ya, yb, t_in, t_ref, tn_ref, py_ref):
    sweep(fx_ref, fy_ref, fz_ref, rhs_ref, w_ref, xa, xb, ya, yb, t_ref, tn_ref, py_ref)


def last_sweep_kernel(fx_ref, fy_ref, fz_ref, rhs_ref, w_ref, xa, xb, ya, yb, t_in, t_ref, tn_ref, py_ref, out_ref, sems):
    put_edges(t_ref, *split(xa[...], xb[...], even("gx")), *split(ya[...], yb[...], even("gy")))
    refs = (t_ref, fx_ref, fy_ref, fz_ref, w_ref, rhs_ref, tn_ref, py_ref)
    bounds = list(range(1, CX - 1, 4)) + [CX - 1]
    copies = []
    for k, (start, stop) in enumerate(zip(bounds[:-1], bounds[1:])):
        sweep_inside(refs, start, stop)
        part = (pl.ds(start, stop - start), pl.ds(YT, CY - 2 * YT))
        copies.append(pltpu.make_async_copy(tn_ref.at[part], out_ref.at[part], sems.at[k]))
        copies[-1].start()
    sweep_plane(0, True, False, *refs)
    sweep_plane(CX - 1, False, True, *refs)
    for copy in copies:
        copy.wait()


def finish_kernel(tn_ref, py_ref, ax_ref, ay_ref, hxa, hxb, hya, hyb, out_in, out_ref, x_out, lo_out, hi_out, sems):
    xlo, xhi, ylo, yhi = faces_of(tn_ref, py_ref, ax_ref, ay_ref, hxa, hxb, hya, hyb)
    x_out[0] = xlo
    x_out[1] = xhi
    row = lax.broadcasted_iota(jnp.int32, (YT, NZ), 0)
    for x in range(1, CX - 1):
        lo_out[x - 1] = jnp.where(row == 0, ylo[x:x + 1], tn_ref[x, 0:YT, :])
        hi_out[x - 1] = jnp.where(row == YT - 1, yhi[x:x + 1], tn_ref[x, CY - YT:CY, :])
    inside = pl.ds(1, CX - 2)
    load([(x_out.at[0], out_ref.at[0]), (x_out.at[1], out_ref.at[CX - 1]),
          (lo_out, out_ref.at[inside, 0:YT]), (hi_out, out_ref.at[inside, CY - YT:CY])], sems)


def swaps(axis, count, a, b):
    one = [(i, i + 1) for i in range(0, count, 2)]
    two = [(i, (i + 1) % count) for i in range(1, count, 2)]
    return [lax.ppermute(v, axis, p + [(j, i) for i, j in p]) for v, p in ((a, one), (b, two))]


def exchange(xa, xb, ya, yb):
    return near(*swaps("gx", NGX, xa, xb), *swaps("gy", NGY, ya, yb))


def call(kernel, outs, specs, scratch=(), alias={}, mib=1, us=0.1, out_specs=None):
    return pl.pallas_call(
        kernel,
        out_shape=outs,
        in_specs=specs,
        out_specs=out_specs or [VM] * len(outs),
        scratch_shapes=scratch,
        input_output_aliases=alias,
        compiler_params=pltpu.CompilerParams(vmem_limit_bytes=mib * 1024 * 1024),
        cost_estimate=pl.CostEstimate(flops=0, bytes_accessed=int(us * 3e6), transcendentals=0),
    )


SLAB = local(CX, CY, NZ)
FACES = (local(CY, NZ), local(CY, NZ), local(CX, NZ), local(CX, NZ))
XX, YY = local(2, CY, NZ), local(2, CX, NZ)
DMA = pltpu.SemaphoreType.DMA
I32 = jnp.int32


def shards(temp_old, capacity, soil_class, cond_table, losses, owner, column, injection):
    rows, rows_int = local(CX, YT, NZ), local(CX, YT, NZ, dtype=I32)
    send, *faces = call(
        start_kernel, (local(NGY * CHUNK, LW),) + (local(2 * CY, NZ),) * 2 + (local(2 * CX, NZ),) * 2, [HB] * 5,
        [rows, rows, rows_int, rows_int, XX, local(2, CY, NZ, dtype=I32), local(SEG, LW), local(1, SEG, dtype=I32),
         local(1, SEG, dtype=I32), DMA((11,))], mib=6)(
        *far(temp_old, soil_class, losses, owner.reshape(1, SEG), column.reshape(1, SEG)))
    recv = lax.all_to_all(send, "gy", 0, 0, tiled=True)
    halo = exchange(*faces)
    fx, fy, fz, w, rhs, new, cx, ey = call(
        prepare_kernel, (SLAB,) * 6 + (XX, local(2, 4, CX, NZ)), [VM, SM] + [HB] * 4,
        [SLAB, SLAB, local(CX, CY, NZ, dtype=I32), SLAB, local(LW, NZ), DMA((3 * PARTS + 1,))], mib=16, us=5.0)(
        *near(recv), cond_table, *far(temp_old, capacity, soil_class, injection))
    *faces, wx, wy, ax, ay = call(
        fix_kernel, FACES + (XX, YY, XX, YY), [SM] + [VM] * 4 + [HB] + [VM] * 4, [XX, DMA((2,))], mib=4)(
        cond_table, *halo, *far(temp_old), *near(w, new, cx, ey))
    for number in range(1, SWEEPS):
        halo = exchange(*faces)
        coefs = near(fx, fy, fz, rhs)
        if number == 1:
            w, temp, new, py = call(
                first_sweep_kernel, (SLAB, SLAB, SLAB, YY), [VM] * 12, alias={10: 0, 11: 1}, mib=2)(
                *coefs, *near(*faces, wx, wy, w, new))
        elif number < SWEEPS - 1:
            temp, new, py = call(sweep_kernel, (SLAB, SLAB, YY), [VM] * 10, alias={9: 0}, mib=2)(
                *coefs, *near(w, *faces, new))
        else:
            temp, new, py, out = call(
                last_sweep_kernel, (SLAB, SLAB, YY, pltpu.HBM((CX, CY, NZ), F32)), [VM] * 10, [DMA((4,))],
                alias={9: 0}, mib=2, out_specs=[VM] * 3 + [HB])(*coefs, *near(w, *faces, new))
        args = near(new, py, ax, ay) + halo
        if number < SWEEPS - 1:
            faces = call(edge_kernel, FACES, [VM] * 8, mib=2)(*args)
    return call(finish_kernel, (pltpu.HBM((CX, CY, NZ), F32),), [VM] * 8 + [HB],
                [XX, local(CX - 2, YT, NZ), local(CX - 2, YT, NZ), DMA((4,))], alias={8: 0}, mib=4, out_specs=[HB])(*args, out)[0]


def solution(mesh):
    return jax.shard_map(
        shards,
        mesh=mesh,
        in_specs=(
            P("gx", "gy", None),
            P("gx", "gy", None),
            P("gx", "gy", None),
            P(),
            P(("gx", "gy"), None),
            P(("gx", "gy"), None),
            P(("gx", "gy")),
            P(),
        ),
        out_specs=P("gx", "gy", None),
        check_vma=False,
    )
```

profile of v0, /device:TPU:24, one launch (start us, length us, event | category | flops | bytes accessed | tf_op | source)
XLA Modules:
  0.0 92.7 jit_solution(14241843281533415964)
XLA Ops:
  0.0 0.0 copy-start
  0.0 2.6 %shard_map.82 = (f32[576,128]{1,0:T(8,128)}, f32[64,1024]{1,0:T(8,128)S(1)}, f32[64,1024]{1,0:T(8,128)S(1)}, f32[32,1024]{1,0:T(8,128)S(1)}, f32[32,1024]{1,0:T(8,128)S(1)}) custom-call(f32[16,32,1024]{2,1,0:T(8,128)} %t_hbm.5, s32[16,32,1024]{2,1,0:T(8,128)} %soil_hbm.3, f32[256,128]{1,0:T(8,128)} %loss_hbm.1, s32[1,256]{1,0:T(1,128)} %bitcast.5, ...), custom_call_target="tpu_custom_call" | custom-call | bytes 300000 | tf_op jit(solution)/shard_map/pallas_call | solution.py:408
  2.6 11.3 %all-to-all-start = ((f32[8,72,128]{2,1,0:T(8,128)}), f32[8,72,128]{2,1,0:T(8,128)S(1)}, u32[]{:S(2)}, u32[]{:S(2)}) async-start(f32[8,72,128]{2,1,0:T(8,128)} %bitcast.2), calls=%async_computation | async-start | bytes 589824 | tf_op jit(solution)/shard_map/all_to_all | solution.py:413
  13.9 0.0 collective-permute-start
  13.9 4.2 %collective-permute-start.1 = (f32[64,1024]{1,0:T(8,128)S(1)}, f32[64,1024]{1,0:T(8,128)S(1)}, u32[]{:S(2)}, u32[]{:S(2)}) collective-permute-start(f32[64,1024]{1,0:T(8,128)S(1)} %get-tuple-element.48), channel_id=1, source_target_pairs={{8,16},{24,32},{40,48},{56,64},{72,80},{88,96},{104,112},{120,128}... | collective-permute-start | bytes 786440 | tf_op jit(solution)/shard_map/ppermute | solution.py:379
  18.2 5.4 %collective-permute-start.2 = (f32[32,1024]{1,0:T(8,128)S(1)}, f32[32,1024]{1,0:T(8,128)S(1)}, u32[]{:S(2)}, u32[]{:S(2)}) collective-permute-start(f32[32,1024]{1,0:T(8,128)S(1)} %get-tuple-element.49), channel_id=1, source_target_pairs={{0,1},{2,3},{4,5},{6,7},{1,0},{3,2},{5,4},{7,6},{8,9},{10,11},{12,... | collective-permute-start | bytes 393224 | tf_op jit(solution)/shard_map/ppermute | solution.py:379
  23.5 0.9 collective-permute-start.3
  24.4 2.2 %all-to-all-done = f32[8,72,128]{2,1,0:T(8,128)S(1)} async-done(((f32[8,72,128]{2,1,0:T(8,128)}), f32[8,72,128]{2,1,0:T(8,128)S(1)}, u32[]{:S(2)}, u32[]{:S(2)}) %all-to-all-start) | async-done | bytes 294944 | tf_op jit(solution)/shard_map/all_to_all | solution.py:413
  26.6 0.0 copy-done
  26.6 10.8 %shard_map.83 = (f32[16,32,1024]{2,1,0:T(8,128)S(1)}, f32[16,32,1024]{2,1,0:T(8,128)S(1)}, f32[16,32,1024]{2,1,0:T(8,128)S(1)}, f32[16,32,1024]{2,1,0:T(8,128)S(...) custom-call(f32[576,128]{1,0:T(8,128)S(1)} %bitcast.4, ...), custom_call_target="tpu_custom_call" | custom-call | bytes 15000000 | tf_op jit(solution)/shard_map/pallas_call | solution.py:415
  37.4 0.1 collective-permute-done.2.hya
  37.5 2.2 %collective-permute-done.3.hyb = f32[32,1024]{1,0:T(8,128)S(1)} collective-permute-done((f32[32,1024]{1,0:T(8,128)S(1)}, f32[32,1024]{1,0:T(8,128)S(1)}, u32[]{:S(2)}, u32[]{:S(2)}) %collective-permute-start.3) | collective-permute-done | bytes 131104 | tf_op jit(solution)/shard_map/ppermute | solution.py:379
  39.7 0.0 collective-permute-done.hxa
  39.7 0.0 collective-permute-done.1.hxb
  39.7 1.7 %shard_map.84 = (f32[32,1024]{1,0:T(8,128)S(1)}, f32[32,1024]{1,0:T(8,128)S(1)}, f32[16,1024]{1,0:T(8,128)S(1)}, f32[16,1024]{1,0:T(8,128)S(1)}, f32[2,32,1024]{...) custom-call(f32[8]{0:T(128)S(1)} %copy-done, ...), custom_call_target="tpu_custom_call" | custom-call | bytes 300000 | tf_op jit(solution)/shard_map/pallas_call | solution.py:419
  41.5 0.1 collective-permute-start.4
  41.6 5.4 %collective-permute-start.5 = (f32[32,1024]{1,0:T(8,128)S(1)}, f32[32,1024]{1,0:T(8,128)S(1)}, u32[]{:S(2)}, u32[]{:S(2)}) collective-permute-start(f32[32,1024]{1,0:T(8,128)S(1)} %get-tuple-element.56.xb), channel_id=1, source_target_pairs={{8,16},{24,32},{40,48},{56,64},{72,80},{88,96},{104,112},{120,128}... | collective-permute-start | bytes 393224 | tf_op jit(solution)/shard_map/ppermute | solution.py:379
  47.0 0.0 collective-permute-start.6
  47.0 5.9 %collective-permute-start.7 = (f32[16,1024]{1,0:T(8,128)S(1)}, f32[16,1024]{1,0:T(8,128)S(1)}, u32[]{:S(2)}, u32[]{:S(2)}) collective-permute-start(f32[16,1024]{1,0:T(8,128)S(1)} %get-tuple-element.58.yb), channel_id=1, source_target_pairs={{1,2},{3,4},{5,6},{7,0},{2,1},{4,3},{6,5},{0,7},{9,10},{11,12},{13... | collective-permute-start | bytes 196616 | tf_op jit(solution)/shard_map/ppermute | solution.py:379
  52.9 2.7 %shard_map.85 = (f32[16,32,1024]{2,1,0:T(8,128)S(1)}, f32[16,32,1024]{2,1,0:T(8,128)S(1)}, f32[16,32,1024]{2,1,0:T(8,128)S(1)}, f32[2,16,1024]{2,1,0:T(8,128)S(1)}) custom-call(f32[16,32,1024]{2,1,0:T(8,128)S(1)} %get-tuple-element.43.fx_ref, f32[16,32,1024]{2,1,0:T(8,128)S(1)} %get-tuple-element.44.fy_ref, ...), custom_call_target="tpu_custom_call", output_to_operand_aliasing={{0}: (10, {}), {1}: (11, {})} | custom-call | bytes 300000 | tf_op jit(solution)/shard_map/pallas_call | solution.py:426
  55.7 1.0 %collective-permute-done.6.hya = f32[16,1024]{1,0:T(8,128)S(1)} collective-permute-done((f32[16,1024]{1,0:T(8,128)S(1)}, f32[16,1024]{1,0:T(8,128)S(1)}, u32[]{:S(2)}, u32[]{:S(2)}) %collective-permute-start.6) | collective-permute-done | bytes 65568 | tf_op jit(solution)/shard_map/ppermute | solution.py:379
  56.6 0.3 collective-permute-done.7.hyb
  56.9 0.0 collective-permute-done.4.hxa
  56.9 0.0 collective-permute-done.5.hxb
  56.9 0.1 shard_map.86
  57.0 0.1 collective-permute-start.8
  57.1 2.0 %collective-permute-start.9 = (f32[32,1024]{1,0:T(8,128)S(1)}, f32[32,1024]{1,0:T(8,128)S(1)}, u32[]{:S(2)}, u32[]{:S(2)}) collective-permute-start(f32[32,1024]{1,0:T(8,128)S(1)} %get-tuple-element.67.xb), channel_id=1, source_target_pairs={{8,16},{24,32},{40,48},{56,64},{72,80},{88,96},{104,112},{120,128}... | collective-permute-start | bytes 393224 | tf_op jit(solution)/shard_map/ppermute | solution.py:379
  59.2 7.0 %collective-permute-start.10 = (f32[16,1024]{1,0:T(8,128)S(1)}, f32[16,1024]{1,0:T(8,128)S(1)}, u32[]{:S(2)}, u32[]{:S(2)}) collective-permute-start(f32[16,1024]{1,0:T(8,128)S(1)} %get-tuple-element.68.ya), channel_id=1, source_target_pairs={{0,1},{2,3},{4,5},{6,7},{1,0},{3,2},{5,4},{7,6},{8,9},{10,11},{12,... | collective-permute-start | bytes 196616 | tf_op jit(solution)/shard_map/ppermute | solution.py:379
  66.1 1.0 %collective-permute-start.11 = (f32[16,1024]{1,0:T(8,128)S(1)}, f32[16,1024]{1,0:T(8,128)S(1)}, u32[]{:S(2)}, u32[]{:S(2)}) collective-permute-start(f32[16,1024]{1,0:T(8,128)S(1)} %get-tuple-element.69.yb), channel_id=1, source_target_pairs={{1,2},{3,4},{5,6},{7,0},{2,1},{4,3},{6,5},{0,7},{9,10},{11,12},{13... | collective-permute-start | bytes 196616 | tf_op jit(solution)/shard_map/ppermute | solution.py:379
  67.1 2.6 %shard_map.87 = (f32[16,32,1024]{2,1,0:T(8,128)S(1)}, f32[16,32,1024]{2,1,0:T(8,128)S(1)}, f32[2,16,1024]{2,1,0:T(8,128)S(1)}) custom-call(f32[16,32,1024]{2,1,0:T(8,128)S(1)} %get-tuple-element.43.fx_ref, f32[16,32,1024]{2,1,0:T(8,128)S(1)} %get-tuple-element.44.fy_ref, ...), custom_call_target="tpu_custom_call", output_to_operand_aliasing={{0}: (9, {})} | custom-call | bytes 300000 | tf_op jit(solution)/shard_map/pallas_call | solution.py:430
  69.7 3.1 %collective-permute-done.10.hya = f32[16,1024]{1,0:T(8,128)S(1)} collective-permute-done((f32[16,1024]{1,0:T(8,128)S(1)}, f32[16,1024]{1,0:T(8,128)S(1)}, u32[]{:S(2)}, u32[]{:S(2)}) %collective-permute-start.10) | collective-permute-done | bytes 65568 | tf_op jit(solution)/shard_map/ppermute | solution.py:379
  72.9 2.9 %collective-permute-done.11.hyb = f32[16,1024]{1,0:T(8,128)S(1)} collective-permute-done((f32[16,1024]{1,0:T(8,128)S(1)}, f32[16,1024]{1,0:T(8,128)S(1)}, u32[]{:S(2)}, u32[]{:S(2)}) %collective-permute-start.11) | collective-permute-done | bytes 65568 | tf_op jit(solution)/shard_map/ppermute | solution.py:379
  75.8 0.0 collective-permute-done.8.hxa
  75.8 0.0 collective-permute-done.9.hxb
  75.8 0.1 shard_map.88
  75.9 0.3 collective-permute-start.12
  76.2 3.8 %collective-permute-start.13 = (f32[32,1024]{1,0:T(8,128)S(1)}, f32[32,1024]{1,0:T(8,128)S(1)}, u32[]{:S(2)}, u32[]{:S(2)}) collective-permute-start(f32[32,1024]{1,0:T(8,128)S(1)} %get-tuple-element.73.xb), channel_id=1, source_target_pairs={{8,16},{24,32},{40,48},{56,64},{72,80},{88,96},{104,112},{120,128}... | collective-permute-start | bytes 393224 | tf_op jit(solution)/shard_map/ppermute | solution.py:379
  80.0 1.9 %collective-permute-start.14 = (f32[16,1024]{1,0:T(8,128)S(1)}, f32[16,1024]{1,0:T(8,128)S(1)}, u32[]{:S(2)}, u32[]{:S(2)}) collective-permute-start(f32[16,1024]{1,0:T(8,128)S(1)} %get-tuple-element.74.ya), channel_id=1, source_target_pairs={{0,1},{2,3},{4,5},{6,7},{1,0},{3,2},{5,4},{7,6},{8,9},{10,11},{12,... | collective-permute-start | bytes 196616 | tf_op jit(solution)/shard_map/ppermute | solution.py:379
  81.9 2.5 %collective-permute-start.15 = (f32[16,1024]{1,0:T(8,128)S(1)}, f32[16,1024]{1,0:T(8,128)S(1)}, u32[]{:S(2)}, u32[]{:S(2)}) collective-permute-start(f32[16,1024]{1,0:T(8,128)S(1)} %get-tuple-element.75.yb), channel_id=1, source_target_pairs={{1,2},{3,4},{5,6},{7,0},{2,1},{4,3},{6,5},{0,7},{9,10},{11,12},{13... | collective-permute-start | bytes 196616 | tf_op jit(solution)/shard_map/ppermute | solution.py:379
  84.4 3.1 %shard_map.89 = (f32[16,32,1024]{2,1,0:T(8,128)S(1)}, f32[16,32,1024]{2,1,0:T(8,128)S(1)}, f32[2,16,1024]{2,1,0:T(8,128)S(1)}, f32[16,32,1024]{2,1,0:T(8,128)}) custom-call(f32[16,32,1024]{2,1,0:T(8,128)S(1)} %get-tuple-element.43.fx_ref, f32[16,32,1024]{2,1,0:T(8,128)S(1)} %get-tuple-element.44.fy_ref, ...), custom_call_target="tpu_custom_call", output_to_operand_aliasing={{0}: (9, {})} | custom-call | bytes 300000 | tf_op jit(solution)/shard_map/pallas_call | solution.py:433
  87.5 1.6 %collective-permute-done.14.hya = f32[16,1024]{1,0:T(8,128)S(1)} collective-permute-done((f32[16,1024]{1,0:T(8,128)S(1)}, f32[16,1024]{1,0:T(8,128)S(1)}, u32[]{:S(2)}, u32[]{:S(2)}) %collective-permute-start.14) | collective-permute-done | bytes 65568 | tf_op jit(solution)/shard_map/ppermute | solution.py:379
  89.1 2.2 %collective-permute-done.15.hyb = f32[16,1024]{1,0:T(8,128)S(1)} collective-permute-done((f32[16,1024]{1,0:T(8,128)S(1)}, f32[16,1024]{1,0:T(8,128)S(1)}, u32[]{:S(2)}, u32[]{:S(2)}) %collective-permute-start.15) | collective-permute-done | bytes 65568 | tf_op jit(solution)/shard_map/ppermute | solution.py:379
  91.4 0.0 collective-permute-done.12.hxa
  91.4 0.0 collective-permute-done.13.hxb
  91.4 1.1 %shard_map.90 = f32[16,32,1024]{2,1,0:T(8,128)} custom-call(f32[16,32,1024]{2,1,0:T(8,128)S(1)} %get-tuple-element.76.tn_ref, f32[2,16,1024]{2,1,0:T(8,128)S(1)} %get-tuple-element.77.py_ref, f32[2,32,1024]{2,1,0:T(8,128)S(1)} %get-tuple-element.64.ax_ref, f32[2,16,1024]{2,1,0:T(8,128)S(1)} %get-tuple-element.65.ay_ref, ...), custom_call_target="tpu_custom_call", output_to_operand_aliasing={{}: (8, {})} | custom-call | bytes 300000 | tf_op jit(solution)/shard_map/pallas_call | solution.py:439
Async XLA Ops:
  0.0 26.6 %copy-start = (f32[8]{0:T(128)S(1)}, f32[8]{0:T(128)}, u32[]{:S(2)}) copy-start(f32[8]{0:T(128)} %table_ref.3) | copy-start | bytes 100
  2.6 24.0 %all-to-all-start = ((f32[8,72,128]{2,1,0:T(8,128)}), f32[8,72,128]{2,1,0:T(8,128)S(1)}, u32[]{:S(2)}, u32[]{:S(2)}) async-start(f32[8,72,128]{2,1,0:T(8,128)} %bitcast.2), calls=%async_computation | async-start | bytes 589824 | tf_op jit(solution)/shard_map/all_to_all | solution.py:413
  13.9 25.8 %collective-permute-start = (f32[64,1024]{1,0:T(8,128)S(1)}, f32[64,1024]{1,0:T(8,128)S(1)}, u32[]{:S(2)}, u32[]{:S(2)}) collective-permute-start(f32[64,1024]{1,0:T(8,128)S(1)} %get-tuple-element.47), channel_id=1, source_target_pairs={{0,8},{16,24},{32,40},{48,56},{64,72},{80,88},{96,104},{112,120},{... | collective-permute-start | bytes 786440 | tf_op jit(solution)/shard_map/ppermute | solution.py:379
  13.9 25.8 %collective-permute-start.1 = (f32[64,1024]{1,0:T(8,128)S(1)}, f32[64,1024]{1,0:T(8,128)S(1)}, u32[]{:S(2)}, u32[]{:S(2)}) collective-permute-start(f32[64,1024]{1,0:T(8,128)S(1)} %get-tuple-element.48), channel_id=1, source_target_pairs={{8,16},{24,32},{40,48},{56,64},{72,80},{88,96},{104,112},{120,128}... | collective-permute-start | bytes 786440 | tf_op jit(solution)/shard_map/ppermute | solution.py:379
  18.2 19.3 %collective-permute-start.2 = (f32[32,1024]{1,0:T(8,128)S(1)}, f32[32,1024]{1,0:T(8,128)S(1)}, u32[]{:S(2)}, u32[]{:S(2)}) collective-permute-start(f32[32,1024]{1,0:T(8,128)S(1)} %get-tuple-element.49), channel_id=1, source_target_pairs={{0,1},{2,3},{4,5},{6,7},{1,0},{3,2},{5,4},{7,6},{8,9},{10,11},{12,... | collective-permute-start | bytes 393224 | tf_op jit(solution)/shard_map/ppermute | solution.py:379
  23.5 16.2 %collective-permute-start.3 = (f32[32,1024]{1,0:T(8,128)S(1)}, f32[32,1024]{1,0:T(8,128)S(1)}, u32[]{:S(2)}, u32[]{:S(2)}) collective-permute-start(f32[32,1024]{1,0:T(8,128)S(1)} %get-tuple-element.50), channel_id=1, source_target_pairs={{1,2},{3,4},{5,6},{7,0},{2,1},{4,3},{6,5},{0,7},{9,10},{11,12},{13... | collective-permute-start | bytes 393224 | tf_op jit(solution)/shard_map/ppermute | solution.py:379
  41.5 15.4 %collective-permute-start.4 = (f32[32,1024]{1,0:T(8,128)S(1)}, f32[32,1024]{1,0:T(8,128)S(1)}, u32[]{:S(2)}, u32[]{:S(2)}) collective-permute-start(f32[32,1024]{1,0:T(8,128)S(1)} %get-tuple-element.55.xa), channel_id=1, source_target_pairs={{0,8},{16,24},{32,40},{48,56},{64,72},{80,88},{96,104},{112,120},{... | collective-permute-start | bytes 393224 | tf_op jit(solution)/shard_map/ppermute | solution.py:379
  41.6 15.3 %collective-permute-start.5 = (f32[32,1024]{1,0:T(8,128)S(1)}, f32[32,1024]{1,0:T(8,128)S(1)}, u32[]{:S(2)}, u32[]{:S(2)}) collective-permute-start(f32[32,1024]{1,0:T(8,128)S(1)} %get-tuple-element.56.xb), channel_id=1, source_target_pairs={{8,16},{24,32},{40,48},{56,64},{72,80},{88,96},{104,112},{120,128}... | collective-permute-start | bytes 393224 | tf_op jit(solution)/shard_map/ppermute | solution.py:379
  47.0 9.6 %collective-permute-start.6 = (f32[16,1024]{1,0:T(8,128)S(1)}, f32[16,1024]{1,0:T(8,128)S(1)}, u32[]{:S(2)}, u32[]{:S(2)}) collective-permute-start(f32[16,1024]{1,0:T(8,128)S(1)} %get-tuple-element.57.ya), channel_id=1, source_target_pairs={{0,1},{2,3},{4,5},{6,7},{1,0},{3,2},{5,4},{7,6},{8,9},{10,11},{12,... | collective-permute-start | bytes 196616 | tf_op jit(solution)/shard_map/ppermute | solution.py:379
  47.0 9.9 %collective-permute-start.7 = (f32[16,1024]{1,0:T(8,128)S(1)}, f32[16,1024]{1,0:T(8,128)S(1)}, u32[]{:S(2)}, u32[]{:S(2)}) collective-permute-start(f32[16,1024]{1,0:T(8,128)S(1)} %get-tuple-element.58.yb), channel_id=1, source_target_pairs={{1,2},{3,4},{5,6},{7,0},{2,1},{4,3},{6,5},{0,7},{9,10},{11,12},{13... | collective-permute-start | bytes 196616 | tf_op jit(solution)/shard_map/ppermute | solution.py:379
  57.0 18.8 %collective-permute-start.8 = (f32[32,1024]{1,0:T(8,128)S(1)}, f32[32,1024]{1,0:T(8,128)S(1)}, u32[]{:S(2)}, u32[]{:S(2)}) collective-permute-start(f32[32,1024]{1,0:T(8,128)S(1)} %get-tuple-element.66.xa), channel_id=1, source_target_pairs={{0,8},{16,24},{32,40},{48,56},{64,72},{80,88},{96,104},{112,120},{... | collective-permute-start | bytes 393224 | tf_op jit(solution)/shard_map/ppermute | solution.py:379
  57.1 18.7 %collective-permute-start.9 = (f32[32,1024]{1,0:T(8,128)S(1)}, f32[32,1024]{1,0:T(8,128)S(1)}, u32[]{:S(2)}, u32[]{:S(2)}) collective-permute-start(f32[32,1024]{1,0:T(8,128)S(1)} %get-tuple-element.67.xb), channel_id=1, source_target_pairs={{8,16},{24,32},{40,48},{56,64},{72,80},{88,96},{104,112},{120,128}... | collective-permute-start | bytes 393224 | tf_op jit(solution)/shard_map/ppermute | solution.py:379
  59.2 13.7 %collective-permute-start.10 = (f32[16,1024]{1,0:T(8,128)S(1)}, f32[16,1024]{1,0:T(8,128)S(1)}, u32[]{:S(2)}, u32[]{:S(2)}) collective-permute-start(f32[16,1024]{1,0:T(8,128)S(1)} %get-tuple-element.68.ya), channel_id=1, source_target_pairs={{0,1},{2,3},{4,5},{6,7},{1,0},{3,2},{5,4},{7,6},{8,9},{10,11},{12,... | collective-permute-start | bytes 196616 | tf_op jit(solution)/shard_map/ppermute | solution.py:379
  66.1 9.7 %collective-permute-start.11 = (f32[16,1024]{1,0:T(8,128)S(1)}, f32[16,1024]{1,0:T(8,128)S(1)}, u32[]{:S(2)}, u32[]{:S(2)}) collective-permute-start(f32[16,1024]{1,0:T(8,128)S(1)} %get-tuple-element.69.yb), channel_id=1, source_target_pairs={{1,2},{3,4},{5,6},{7,0},{2,1},{4,3},{6,5},{0,7},{9,10},{11,12},{13... | collective-permute-start | bytes 196616 | tf_op jit(solution)/shard_map/ppermute | solution.py:379
  75.9 15.5 %collective-permute-start.12 = (f32[32,1024]{1,0:T(8,128)S(1)}, f32[32,1024]{1,0:T(8,128)S(1)}, u32[]{:S(2)}, u32[]{:S(2)}) collective-permute-start(f32[32,1024]{1,0:T(8,128)S(1)} %get-tuple-element.72.xa), channel_id=1, source_target_pairs={{0,8},{16,24},{32,40},{48,56},{64,72},{80,88},{96,104},{112,120},{... | collective-permute-start | bytes 393224 | tf_op jit(solution)/shard_map/ppermute | solution.py:379
  76.2 15.2 %collective-permute-start.13 = (f32[32,1024]{1,0:T(8,128)S(1)}, f32[32,1024]{1,0:T(8,128)S(1)}, u32[]{:S(2)}, u32[]{:S(2)}) collective-permute-start(f32[32,1024]{1,0:T(8,128)S(1)} %get-tuple-element.73.xb), channel_id=1, source_target_pairs={{8,16},{24,32},{40,48},{56,64},{72,80},{88,96},{104,112},{120,128}... | collective-permute-start | bytes 393224 | tf_op jit(solution)/shard_map/ppermute | solution.py:379
  80.0 9.1 %collective-permute-start.14 = (f32[16,1024]{1,0:T(8,128)S(1)}, f32[16,1024]{1,0:T(8,128)S(1)}, u32[]{:S(2)}, u32[]{:S(2)}) collective-permute-start(f32[16,1024]{1,0:T(8,128)S(1)} %get-tuple-element.74.ya), channel_id=1, source_target_pairs={{0,1},{2,3},{4,5},{6,7},{1,0},{3,2},{5,4},{7,6},{8,9},{10,11},{12,... | collective-permute-start | bytes 196616 | tf_op jit(solution)/shard_map/ppermute | solution.py:379
  81.9 9.5 %collective-permute-start.15 = (f32[16,1024]{1,0:T(8,128)S(1)}, f32[16,1024]{1,0:T(8,128)S(1)}, u32[]{:S(2)}, u32[]{:S(2)}) collective-permute-start(f32[16,1024]{1,0:T(8,128)S(1)} %get-tuple-element.75.yb), channel_id=1, source_target_pairs={{1,2},{3,4},{5,6},{7,0},{2,1},{4,3},{6,5},{0,7},{9,10},{11,12},{13... | collective-permute-start | bytes 196616 | tf_op jit(solution)/shard_map/ppermute | solution.py:379
where the time goes:
time: 94.6 us; the launch traced here: 92.7 us
  starting transfers between devices  51.8 us (55%)
  Pallas kernels  24.8 us (26%)
  waiting for transfers between devices  15.7 us (17%)
    ppermute x16, starting transfers between devices, swaps(): lax.ppermute(v, axis, p + [(j, i) for i, j in p])  40.5 us
    ppermute x16, waiting for transfers between devices, swaps(): lax.ppermute(v, axis, p + [(j, i) for i, j in p])  13.6 us
    all_to_all x1, starting transfers between devices, shards(): recv = lax.all_to_all(send, 'gy', 0, 0, tiled=True)  11.3 us
    pallas_call x1, Pallas kernels, shards(): call(prepare_kernel, (SLAB,) * 6 + (XX, local(2, 4, CX, NZ)), [VM, SM] +...  10.8 us
    pallas_call x1, Pallas kernels, shards(): call(last_sweep_kernel, (SLAB, SLAB, YY, pltpu.HBM((CX, CY, NZ), F32)), [...  3.06 us
    pallas_call x1, Pallas kernels, shards(): call(first_sweep_kernel, (SLAB, SLAB, SLAB, YY), [VM] * 12, alias={10: 0,...  2.71 us
    pallas_call x1, Pallas kernels, shards(): call(sweep_kernel, (SLAB, SLAB, YY), [VM] * 10, alias={9: 0}, mib=2)  2.61 us
    pallas_call x1, Pallas kernels, shards(): call(start_kernel, (local(NGY * CHUNK, LW),) + (local(2 * CY, NZ),) * 2 +...  2.58 us
  transfers between devices with their start and end apart: 17, of which 9 were waited for; matrix products, arithmetic and copies ran while one was open for 0% of the time, Pallas kernels for 21%

commit v1 on v0

--- a/solution.py
+++ b/solution.py
@@ -146,7 +146,7 @@
 
 
 def prepare_kernel(recv_ref, table_ref, t_hbm, cap_hbm, soil_hbm, inj_hbm,
-                   fx_ref, fy_ref, fz_ref, w_ref, rhs_ref, tn_ref, cx_ref, ey_ref, t_ref, cond, soil, cap, inj, sems):
+                   fx_ref, fy_ref, fz_ref, w_ref, rhs_ref, tn_ref, ex_ref, ey_ref, t_ref, cond, soil, cap, inj, sems):
     copies = []
     step = CX // PARTS
     for part in range(PARTS):
@@ -170,8 +170,9 @@
     for part in range(PARTS):
         copies[3 * part + 1].wait()
         copies[3 * part + 2].wait()
-    cx_ref[0] = cond[0]
-    cx_ref[1] = cond[CX - 1]
+    for side, x in enumerate((0, CX - 1)):
+        ex_ref[side, 0] = cond[x]
+        ex_ref[side, 1] = t_ref[x]
     row = lax.broadcasted_iota(jnp.int32, (YT, NZ), 0)
     lane = lax.broadcasted_iota(jnp.int32, (YT, NZ), 1)
 
@@ -245,26 +246,33 @@
             yhi + at_row(ys, 0, xlo[CY - 1:CY]) + at_row(ys, CX - 1, xhi[CY - 1:CY]))
 
 
-def fix_kernel(table_ref, hxa, hxb, hya, hyb, t_hbm, w_ref, tn_ref, cx_ref, ey_ref,
-               xa, xb, ya, yb, wx_ref, wy_ref, ax_ref, ay_ref, t_edge, sems):
-    copies = [pltpu.make_async_copy(t_hbm.at[x], t_edge.at[k], sems.at[k]) for k, x in enumerate((0, CX - 1))]
-    for copy in copies:
-        copy.start()
+def fix_y_kernel(table_ref, hya, hyb, ey_ref, more_ref, face_ref, term_ref):
     table = [table_ref[k] for k in range(NCLS)]
-    gx, gy = lax.axis_index("gx"), lax.axis_index("gy")
-    within = [jnp.where(q, F32(1.0), F32(0.0)) for q in (gx > 0, gx < NGX - 1, gy > 0, gy < NGY - 1)]
-    t_halo = split(hxa[0:CY, :], hxb[0:CY, :], even("gx")) + split(hya[0:CX, :], hyb[0:CX, :], even("gy"))
-    klass = split(hxa[CY:, :], hxb[CY:, :], even("gx")) + split(hya[CX:, :], hyb[CX:, :], even("gy"))
-    conds = (cx_ref[0], cx_ref[1], ey_ref[0, 2], ey_ref[1, 2])
+    gy = lax.axis_index("gy")
+    halo = split(hya[...], hyb[...], even("gy"))
+    for k, inside in enumerate((gy > 0, gy < NGY - 1)):
+        inside = jnp.where(inside, F32(1.0), F32(0.0))
+        more = 0.5 * lookup(halo[k][CX:].astype(jnp.int32), table) * inside
+        face = (0.5 * ey_ref[k, 2] + more) * inside
+        more_ref[k] = more
+        face_ref[k] = face
+        term_ref[k] = face * halo[k][0:CX]
+
+
+def fix_kernel(table_ref, hxa, hxb, my_ref, fy_ref, gy_ref, w_ref, tn_ref, ex_ref, ey_ref,
+               xa, xb, ya, yb, wx_ref, wy_ref, ax_ref, ay_ref):
+    table = [table_ref[k] for k in range(NCLS)]
+    gx = lax.axis_index("gx")
+    within = [jnp.where(q, F32(1.0), F32(0.0)) for q in (gx > 0, gx < NGX - 1)]
+    t_halo = split(hxa[0:CY, :], hxb[0:CY, :], even("gx"))
+    klass = split(hxa[CY:, :], hxb[CY:, :], even("gx"))
     more = [0.5 * lookup(k.astype(jnp.int32), table) * q for k, q in zip(klass, within)]
-    face = [(0.5 * c + m) * q for c, m, q in zip(conds, more, within)]
-    diag = with_corners(*more)
-    total = with_corners(*[f * t for f, t in zip(face, t_halo)])
-    for copy in copies:
-        copy.wait()
+    face = [(0.5 * ex_ref[k, 0] + more[k]) * within[k] for k in range(2)] + [fy_ref[0], fy_ref[1]]
+    diag = with_corners(*more, my_ref[0], my_ref[1])
+    total = with_corners(face[0] * t_halo[0], face[1] * t_halo[1], gy_ref[0], gy_ref[1])
     total = [a + b for a, b in zip(total, (tn_ref[0], tn_ref[CX - 1], ey_ref[0, 0], ey_ref[1, 0]))]
     w = [0.8 / (a + b) for a, b in zip(diag, (w_ref[0], w_ref[CX - 1], ey_ref[0, 1], ey_ref[1, 1]))]
-    old = (t_edge[0], t_edge[1], ey_ref[0, 3], ey_ref[1, 3])
+    old = (ex_ref[0, 1], ex_ref[1, 1], ey_ref[0, 3], ey_ref[1, 3])
     new = [(1.0 - 0.8) * t + a * b for t, a, b in zip(old, w, total)]
     xa[...], xb[...] = split(new[0], new[1], even("gx"))
     ya[...], yb[...] = split(new[2], new[3], even("gy"))
@@ -273,14 +281,20 @@
         ax_ref[k], ay_ref[k] = w[k] * face[k], w[2 + k] * face[2 + k]
 
 
-def faces_of(tn_ref, py_ref, ax_ref, ay_ref, hxa, hxb, hya, hyb):
-    halo = split(hxa[...], hxb[...], even("gx")) + split(hya[...], hyb[...], even("gy"))
-    terms = with_corners(ax_ref[0] * halo[0], ax_ref[1] * halo[1], ay_ref[0] * halo[2], ay_ref[1] * halo[3])
+def y_term_kernel(ay_ref, hya, hyb, gy_ref):
+    lo, hi = split(hya[...], hyb[...], even("gy"))
+    gy_ref[0] = ay_ref[0] * lo
+    gy_ref[1] = ay_ref[1] * hi
+
+
+def faces_of(tn_ref, py_ref, ax_ref, gy_ref, hxa, hxb):
+    lo, hi = split(hxa[...], hxb[...], even("gx"))
+    terms = with_corners(ax_ref[0] * lo, ax_ref[1] * hi, gy_ref[0], gy_ref[1])
     return [a + b for a, b in zip(terms, (tn_ref[0], tn_ref[CX - 1], py_ref[0], py_ref[1]))]
 
 
-def edge_kernel(tn_ref, py_ref, ax_ref, ay_ref, hxa, hxb, hya, hyb, xa, xb, ya, yb):
-    new = faces_of(tn_ref, py_ref, ax_ref, ay_ref, hxa, hxb, hya, hyb)
+def edge_kernel(tn_ref, py_ref, ax_ref, gy_ref, hxa, hxb, xa, xb, ya, yb):
+    new = faces_of(tn_ref, py_ref, ax_ref, gy_ref, hxa, hxb)
     xa[...], xb[...] = split(new[0], new[1], even("gx"))
     ya[...], yb[...] = split(new[2], new[3], even("gy"))
 
@@ -360,8 +374,8 @@
         copy.wait()
 
 
-def finish_kernel(tn_ref, py_ref, ax_ref, ay_ref, hxa, hxb, hya, hyb, out_in, out_ref, x_out, lo_out, hi_out, sems):
-    xlo, xhi, ylo, yhi = faces_of(tn_ref, py_ref, ax_ref, ay_ref, hxa, hxb, hya, hyb)
+def finish_kernel(tn_ref, py_ref, ax_ref, gy_ref, hxa, hxb, out_in, out_ref, x_out, lo_out, hi_out, sems):
+    xlo, xhi, ylo, yhi = faces_of(tn_ref, py_ref, ax_ref, gy_ref, hxa, hxb)
     x_out[0] = xlo
     x_out[1] = xhi
     row = lax.broadcasted_iota(jnp.int32, (YT, NZ), 0)
@@ -392,7 +406,7 @@
         scratch_shapes=scratch,
         input_output_aliases=alias,
         compiler_params=pltpu.CompilerParams(vmem_limit_bytes=mib * 1024 * 1024),
-        cost_estimate=pl.CostEstimate(flops=0, bytes_accessed=int(us * 3e6), transcendentals=0),
+        cost_estimate=pl.CostEstimate(flops=int(us * 1e9), bytes_accessed=int(us * 3e6), transcendentals=0),
     )
 
 
@@ -412,13 +426,15 @@
         *far(temp_old, soil_class, losses, owner.reshape(1, SEG), column.reshape(1, SEG)))
     recv = lax.all_to_all(send, "gy", 0, 0, tiled=True)
     halo = exchange(*faces)
-    fx, fy, fz, w, rhs, new, cx, ey = call(
-        prepare_kernel, (SLAB,) * 6 + (XX, local(2, 4, CX, NZ)), [VM, SM] + [HB] * 4,
-        [SLAB, SLAB, local(CX, CY, NZ, dtype=I32), SLAB, local(LW, NZ), DMA((3 * PARTS + 1,))], mib=16, us=5.0)(
+    fx, fy, fz, w, rhs, new, ex, ey = call(
+        prepare_kernel, (SLAB,) * 6 + (local(2, 2, CY, NZ), local(2, 4, CX, NZ)), [VM, SM] + [HB] * 4,
+        [SLAB, SLAB, local(CX, CY, NZ, dtype=I32), SLAB, local(LW, NZ), DMA((3 * PARTS + 1,))], mib=16, us=0.1)(
         *near(recv), cond_table, *far(temp_old, capacity, soil_class, injection))
+    hxa, hxb, hya, hyb = halo
+    my, fyh, gy = call(fix_y_kernel, (YY, YY, YY), [SM] + [VM] * 3, us=8.0)(cond_table, hya, hyb, *near(ey))
     *faces, wx, wy, ax, ay = call(
-        fix_kernel, FACES + (XX, YY, XX, YY), [SM] + [VM] * 4 + [HB] + [VM] * 4, [XX, DMA((2,))], mib=4)(
-        cond_table, *halo, *far(temp_old), *near(w, new, cx, ey))
+        fix_kernel, FACES + (XX, YY, XX, YY), [SM] + [VM] * 9, mib=2)(
+        cond_table, hxa, hxb, *near(my, fyh, gy, w, new, ex, ey))
     for number in range(1, SWEEPS):
         halo = exchange(*faces)
         coefs = near(fx, fy, fz, rhs)
@@ -433,11 +449,13 @@
             temp, new, py, out = call(
                 last_sweep_kernel, (SLAB, SLAB, YY, pltpu.HBM((CX, CY, NZ), F32)), [VM] * 10, [DMA((4,))],
                 alias={9: 0}, mib=2, out_specs=[VM] * 3 + [HB])(*coefs, *near(w, *faces, new))
-        args = near(new, py, ax, ay) + halo
+        hxa, hxb, hya, hyb = halo
+        (gy,) = call(y_term_kernel, (YY,), [VM] * 3, us=8.0)(*near(ay), hya, hyb)
+        args = near(new, py, ax, gy) + [hxa, hxb]
         if number < SWEEPS - 1:
-            faces = call(edge_kernel, FACES, [VM] * 8, mib=2)(*args)
-    return call(finish_kernel, (pltpu.HBM((CX, CY, NZ), F32),), [VM] * 8 + [HB],
-                [XX, local(CX - 2, YT, NZ), local(CX - 2, YT, NZ), DMA((4,))], alias={8: 0}, mib=4, out_specs=[HB])(*args, out)[0]
+            faces = call(edge_kernel, FACES, [VM] * 6, mib=2)(*args)
+    return call(finish_kernel, (pltpu.HBM((CX, CY, NZ), F32),), [VM] * 6 + [HB],
+                [XX, local(CX - 2, YT, NZ), local(CX - 2, YT, NZ), DMA((4,))], alias={6: 0}, mib=4, out_specs=[HB])(*args, out)[0]
 
 
 def solution(mesh):

time: 94.6 us -> 91.6 us (0.968)
  the two profiles are of different devices: /device:TPU:24 before, /device:TPU:8 now
where the time goes in v1:
time: 91.6 us; the launch traced here: 91.4 us
  starting transfers between devices  49.7 us (54%)
  Pallas kernels  24.8 us (27%)
  waiting for transfers between devices  16.6 us (18%)
    ppermute x16, starting transfers between devices, swaps(): lax.ppermute(v, axis, p + [(j, i) for i, j in p])  38.2 us
    ppermute x16, waiting for transfers between devices, swaps(): lax.ppermute(v, axis, p + [(j, i) for i, j in p])  13.6 us
    all_to_all x1, starting transfers between devices, shards(): recv = lax.all_to_all(send, 'gy', 0, 0, tiled=True)  11.6 us
    pallas_call x1, Pallas kernels, shards(): call(prepare_kernel, (SLAB,) * 6 + (local(2, 2, CY, NZ), local(2, 4, CX,...  10.8 us
    pallas_call x1, Pallas kernels, shards(): call(last_sweep_kernel, (SLAB, SLAB, YY, pltpu.HBM((CX, CY, NZ), F32)), [...  3.06 us
    all_to_all x1, waiting for transfers between devices, shards(): recv = lax.all_to_all(send, 'gy', 0, 0, tiled=True)  2.97 us
    pallas_call x1, Pallas kernels, shards(): call(first_sweep_kernel, (SLAB, SLAB, SLAB, YY), [VM] * 12, alias={10: 0,...  2.71 us
    pallas_call x1, Pallas kernels, shards(): call(start_kernel, (local(NGY * CHUNK, LW),) + (local(2 * CY, NZ),) * 2 +...  2.58 us
  transfers between devices with their start and end apart: 17, of which 9 were waited for; matrix products, arithmetic and copies ran while one was open for 0% of the time, Pallas kernels for 22%

profile of v1, /device:TPU:8, one launch (start us, length us, event | category | flops | bytes accessed | tf_op | source)
XLA Modules:
  0.0 91.4 jit_solution(14410700578011533183)
XLA Ops:
  0.0 0.0 copy-start
  0.0 2.6 %shard_map.82 = (f32[576,128]{1,0:T(8,128)}, f32[64,1024]{1,0:T(8,128)S(1)}, f32[64,1024]{1,0:T(8,128)S(1)}, f32[32,1024]{1,0:T(8,128)S(1)}, f32[32,1024]{1,0:T(8,128)S(1)}) custom-call(f32[16,32,1024]{2,1,0:T(8,128)} %t_hbm.3, s32[16,32,1024]{2,1,0:T(8,128)} %soil_hbm.3, f32[256,128]{1,0:T(8,128)} %loss_hbm.1, s32[1,256]{1,0:T(1,128)} %bitcast.5, ...), custom_call_target="tpu_custom_call" | custom-call | flops 100000000 | bytes 300000 | tf_op jit(solution)/shard_map/pallas_call | solution.py:422
  2.6 11.6 %all-to-all-start = ((f32[8,72,128]{2,1,0:T(8,128)}), f32[8,72,128]{2,1,0:T(8,128)S(1)}, u32[]{:S(2)}, u32[]{:S(2)}) async-start(f32[8,72,128]{2,1,0:T(8,128)} %bitcast.2), calls=%async_computation | async-start | bytes 589824 | tf_op jit(solution)/shard_map/all_to_all | solution.py:427
  14.1 5.4 %collective-permute-start.2 = (f32[32,1024]{1,0:T(8,128)S(1)}, f32[32,1024]{1,0:T(8,128)S(1)}, u32[]{:S(2)}, u32[]{:S(2)}) collective-permute-start(f32[32,1024]{1,0:T(8,128)S(1)} %get-tuple-element.52), channel_id=1, source_target_pairs={{0,1},{2,3},{4,5},{6,7},{1,0},{3,2},{5,4},{7,6},{8,9},{10,11},{12,... | collective-permute-start | bytes 393224 | tf_op jit(solution)/shard_map/ppermute | solution.py:393
  19.5 0.0 collective-permute-start.3
  19.5 0.0 collective-permute-start
  19.5 4.2 %collective-permute-start.1 = (f32[64,1024]{1,0:T(8,128)S(1)}, f32[64,1024]{1,0:T(8,128)S(1)}, u32[]{:S(2)}, u32[]{:S(2)}) collective-permute-start(f32[64,1024]{1,0:T(8,128)S(1)} %get-tuple-element.51), channel_id=1, source_target_pairs={{8,16},{24,32},{40,48},{56,64},{72,80},{88,96},{104,112},{120,128}... | collective-permute-start | bytes 786440 | tf_op jit(solution)/shard_map/ppermute | solution.py:393
  23.8 3.0 %all-to-all-done = f32[8,72,128]{2,1,0:T(8,128)S(1)} async-done(((f32[8,72,128]{2,1,0:T(8,128)}), f32[8,72,128]{2,1,0:T(8,128)S(1)}, u32[]{:S(2)}, u32[]{:S(2)}) %all-to-all-start) | async-done | bytes 294944 | tf_op jit(solution)/shard_map/all_to_all | solution.py:427
  26.7 0.0 copy-done
  26.8 10.8 %shard_map.83 = (f32[16,32,1024]{2,1,0:T(8,128)S(1)}, f32[16,32,1024]{2,1,0:T(8,128)S(1)}, f32[16,32,1024]{2,1,0:T(8,128)S(1)}, f32[16,32,1024]{2,1,0:T(8,128)S(...) custom-call(f32[576,128]{1,0:T(8,128)S(1)} %bitcast.4, ...), custom_call_target="tpu_custom_call" | custom-call | flops 100000000 | bytes 300000 | tf_op jit(solution)/shard_map/pallas_call | solution.py:429
  37.6 0.0 collective-permute-done.2.hya
  37.6 0.4 collective-permute-done.3.hyb
  38.0 0.7 shard_map.84
  38.7 0.0 collective-permute-done.hxa
  38.7 0.8 collective-permute-done.1.hxb
  39.5 1.0 %shard_map.85 = (f32[32,1024]{1,0:T(8,128)S(1)}, f32[32,1024]{1,0:T(8,128)S(1)}, f32[16,1024]{1,0:T(8,128)S(1)}, f32[16,1024]{1,0:T(8,128)S(1)}, f32[2,32,1024]{...) custom-call(f32[8]{0:T(128)S(1)} %copy-done, ...), custom_call_target="tpu_custom_call" | custom-call | flops 100000000 | bytes 300000 | tf_op jit(solution)/shard_map/pallas_call | solution.py:435
  40.5 5.6 %collective-permute-start.4 = (f32[16,1024]{1,0:T(8,128)S(1)}, f32[16,1024]{1,0:T(8,128)S(1)}, u32[]{:S(2)}, u32[]{:S(2)}) collective-permute-start(f32[16,1024]{1,0:T(8,128)S(1)} %get-tuple-element.63.ya), channel_id=1, source_target_pairs={{0,1},{2,3},{4,5},{6,7},{1,0},{3,2},{5,4},{7,6},{8,9},{10,11},{12,... | collective-permute-start | bytes 196616 | tf_op jit(solution)/shard_map/ppermute | solution.py:393
  46.1 3.0 %collective-permute-start.5 = (f32[16,1024]{1,0:T(8,128)S(1)}, f32[16,1024]{1,0:T(8,128)S(1)}, u32[]{:S(2)}, u32[]{:S(2)}) collective-permute-start(f32[16,1024]{1,0:T(8,128)S(1)} %get-tuple-element.64.yb), channel_id=1, source_target_pairs={{1,2},{3,4},{5,6},{7,0},{2,1},{4,3},{6,5},{0,7},{9,10},{11,12},{13... | collective-permute-start | bytes 196616 | tf_op jit(solution)/shard_map/ppermute | solution.py:393
  49.1 0.0 collective-permute-start.6
  49.1 2.2 %collective-permute-start.7 = (f32[32,1024]{1,0:T(8,128)S(1)}, f32[32,1024]{1,0:T(8,128)S(1)}, u32[]{:S(2)}, u32[]{:S(2)}) collective-permute-start(f32[32,1024]{1,0:T(8,128)S(1)} %get-tuple-element.62.xb), channel_id=1, source_target_pairs={{8,16},{24,32},{40,48},{56,64},{72,80},{88,96},{104,112},{120,128}... | collective-permute-start | bytes 393224 | tf_op jit(solution)/shard_map/ppermute | solution.py:393
  51.3 2.7 %shard_map.86 = (f32[16,32,1024]{2,1,0:T(8,128)S(1)}, f32[16,32,1024]{2,1,0:T(8,128)S(1)}, f32[16,32,1024]{2,1,0:T(8,128)S(1)}, f32[2,16,1024]{2,1,0:T(8,128)S(1)}) custom-call(f32[16,32,1024]{2,1,0:T(8,128)S(1)} %get-tuple-element.46.fx_ref, f32[16,32,1024]{2,1,0:T(8,128)S(1)} %get-tuple-element.47.fy_ref, ...), custom_call_target="tpu_custom_call", output_to_operand_aliasing={{0}: (10, {}), {1}: (11, {})} | custom-call | flops 100000000 | bytes 300000 | tf_op jit(solution)/shard_map/pallas_call | solution.py:442
  54.0 0.0 collective-permute-done.4.hya
  54.0 2.5 %collective-permute-done.5.hyb = f32[16,1024]{1,0:T(8,128)S(1)} collective-permute-done((f32[16,1024]{1,0:T(8,128)S(1)}, f32[16,1024]{1,0:T(8,128)S(1)}, u32[]{:S(2)}, u32[]{:S(2)}) %collective-permute-start.5) | collective-permute-done | bytes 65568 | tf_op jit(solution)/shard_map/ppermute | solution.py:393
  56.5 0.0 collective-permute-done.6.hxa
  56.5 1.0 %collective-permute-done.7.hxb = f32[32,1024]{1,0:T(8,128)S(1)} collective-permute-done((f32[32,1024]{1,0:T(8,128)S(1)}, f32[32,1024]{1,0:T(8,128)S(1)}, u32[]{:S(2)}, u32[]{:S(2)}) %collective-permute-start.7) | collective-permute-done | bytes 131104 | tf_op jit(solution)/shard_map/ppermute | solution.py:393
  57.5 0.1 shard_map.88
  57.6 3.8 %collective-permute-start.8 = (f32[16,1024]{1,0:T(8,128)S(1)}, f32[16,1024]{1,0:T(8,128)S(1)}, u32[]{:S(2)}, u32[]{:S(2)}) collective-permute-start(f32[16,1024]{1,0:T(8,128)S(1)} %get-tuple-element.74.ya), channel_id=1, source_target_pairs={{0,1},{2,3},{4,5},{6,7},{1,0},{3,2},{5,4},{7,6},{8,9},{10,11},{12,... | collective-permute-start | bytes 196616 | tf_op jit(solution)/shard_map/ppermute | solution.py:393
  61.4 3.1 %collective-permute-start.9 = (f32[16,1024]{1,0:T(8,128)S(1)}, f32[16,1024]{1,0:T(8,128)S(1)}, u32[]{:S(2)}, u32[]{:S(2)}) collective-permute-start(f32[16,1024]{1,0:T(8,128)S(1)} %get-tuple-element.75.yb), channel_id=1, source_target_pairs={{1,2},{3,4},{5,6},{7,0},{2,1},{4,3},{6,5},{0,7},{9,10},{11,12},{13... | collective-permute-start | bytes 196616 | tf_op jit(solution)/shard_map/ppermute | solution.py:393
  64.5 0.0 collective-permute-start.10
  64.5 3.2 %collective-permute-start.11 = (f32[32,1024]{1,0:T(8,128)S(1)}, f32[32,1024]{1,0:T(8,128)S(1)}, u32[]{:S(2)}, u32[]{:S(2)}) collective-permute-start(f32[32,1024]{1,0:T(8,128)S(1)} %get-tuple-element.73.xb), channel_id=1, source_target_pairs={{8,16},{24,32},{40,48},{56,64},{72,80},{88,96},{104,112},{120,128}... | collective-permute-start | bytes 393224 | tf_op jit(solution)/shard_map/ppermute | solution.py:393
  67.7 2.6 %shard_map.89 = (f32[16,32,1024]{2,1,0:T(8,128)S(1)}, f32[16,32,1024]{2,1,0:T(8,128)S(1)}, f32[2,16,1024]{2,1,0:T(8,128)S(1)}) custom-call(f32[16,32,1024]{2,1,0:T(8,128)S(1)} %get-tuple-element.46.fx_ref, f32[16,32,1024]{2,1,0:T(8,128)S(1)} %get-tuple-element.47.fy_ref, ...), custom_call_target="tpu_custom_call", output_to_operand_aliasing={{0}: (9, {})} | custom-call | flops 100000000 | bytes 300000 | tf_op jit(solution)/shard_map/pallas_call | solution.py:446
  70.2 0.0 collective-permute-done.8.hya
  70.2 2.2 %collective-permute-done.9.hyb = f32[16,1024]{1,0:T(8,128)S(1)} collective-permute-done((f32[16,1024]{1,0:T(8,128)S(1)}, f32[16,1024]{1,0:T(8,128)S(1)}, u32[]{:S(2)}, u32[]{:S(2)}) %collective-permute-start.9) | collective-permute-done | bytes 65568 | tf_op jit(solution)/shard_map/ppermute | solution.py:393
  72.5 0.0 collective-permute-done.10.hxa
  72.5 2.0 %collective-permute-done.11.hxb = f32[32,1024]{1,0:T(8,128)S(1)} collective-permute-done((f32[32,1024]{1,0:T(8,128)S(1)}, f32[32,1024]{1,0:T(8,128)S(1)}, u32[]{:S(2)}, u32[]{:S(2)}) %collective-permute-start.11) | collective-permute-done | bytes 131104 | tf_op jit(solution)/shard_map/ppermute | solution.py:393
  74.4 0.1 shard_map.91
  74.5 2.9 %collective-permute-start.12 = (f32[16,1024]{1,0:T(8,128)S(1)}, f32[16,1024]{1,0:T(8,128)S(1)}, u32[]{:S(2)}, u32[]{:S(2)}) collective-permute-start(f32[16,1024]{1,0:T(8,128)S(1)} %get-tuple-element.80.ya), channel_id=1, source_target_pairs={{0,1},{2,3},{4,5},{6,7},{1,0},{3,2},{5,4},{7,6},{8,9},{10,11},{12,... | collective-permute-start | bytes 196616 | tf_op jit(solution)/shard_map/ppermute | solution.py:393
  77.4 3.2 %collective-permute-start.13 = (f32[16,1024]{1,0:T(8,128)S(1)}, f32[16,1024]{1,0:T(8,128)S(1)}, u32[]{:S(2)}, u32[]{:S(2)}) collective-permute-start(f32[16,1024]{1,0:T(8,128)S(1)} %get-tuple-element.81.yb), channel_id=1, source_target_pairs={{1,2},{3,4},{5,6},{7,0},{2,1},{4,3},{6,5},{0,7},{9,10},{11,12},{13... | collective-permute-start | bytes 196616 | tf_op jit(solution)/shard_map/ppermute | solution.py:393
  80.6 0.0 collective-permute-start.14
  80.6 1.7 %collective-permute-start.15 = (f32[32,1024]{1,0:T(8,128)S(1)}, f32[32,1024]{1,0:T(8,128)S(1)}, u32[]{:S(2)}, u32[]{:S(2)}) collective-permute-start(f32[32,1024]{1,0:T(8,128)S(1)} %get-tuple-element.79.xb), channel_id=1, source_target_pairs={{8,16},{24,32},{40,48},{56,64},{72,80},{88,96},{104,112},{120,128}... | collective-permute-start | bytes 393224 | tf_op jit(solution)/shard_map/ppermute | solution.py:393
  82.3 3.1 %shard_map.92 = (f32[16,32,1024]{2,1,0:T(8,128)S(1)}, f32[16,32,1024]{2,1,0:T(8,128)S(1)}, f32[2,16,1024]{2,1,0:T(8,128)S(1)}, f32[16,32,1024]{2,1,0:T(8,128)}) custom-call(f32[16,32,1024]{2,1,0:T(8,128)S(1)} %get-tuple-element.46.fx_ref, f32[16,32,1024]{2,1,0:T(8,128)S(1)} %get-tuple-element.47.fy_ref, ...), custom_call_target="tpu_custom_call", output_to_operand_aliasing={{0}: (9, {})} | custom-call | flops 100000000 | bytes 300000 | tf_op jit(solution)/shard_map/pallas_call | solution.py:449
  85.4 0.0 collective-permute-done.12.hya
  85.4 2.5 %collective-permute-done.13.hyb = f32[16,1024]{1,0:T(8,128)S(1)} collective-permute-done((f32[16,1024]{1,0:T(8,128)S(1)}, f32[16,1024]{1,0:T(8,128)S(1)}, u32[]{:S(2)}, u32[]{:S(2)}) %collective-permute-start.13) | collective-permute-done | bytes 65568 | tf_op jit(solution)/shard_map/ppermute | solution.py:393
  87.9 0.0 collective-permute-done.14.hxa
  87.9 2.2 %collective-permute-done.15.hxb = f32[32,1024]{1,0:T(8,128)S(1)} collective-permute-done((f32[32,1024]{1,0:T(8,128)S(1)}, f32[32,1024]{1,0:T(8,128)S(1)}, u32[]{:S(2)}, u32[]{:S(2)}) %collective-permute-start.15) | collective-permute-done | bytes 131104 | tf_op jit(solution)/shard_map/ppermute | solution.py:393
  90.1 1.1 %shard_map.94 = f32[16,32,1024]{2,1,0:T(8,128)} custom-call(f32[16,32,1024]{2,1,0:T(8,128)S(1)} %get-tuple-element.82.tn_ref, f32[2,16,1024]{2,1,0:T(8,128)S(1)} %get-tuple-element.83.py_ref, f32[2,32,1024]{2,1,0:T(8,128)S(1)} %get-tuple-element.70.ax_ref, f32[2,16,1024]{2,1,0:T(8,128)S(1)} %shard_map.93.gy_ref, ...), custom_call_target="tpu_custom_call", output_to_operand_aliasing={{}: (6, {})} | custom-call | flops 100000000 | bytes 300000 | tf_op jit(solution)/shard_map/pallas_call | solution.py:457
  (3 shorter events, 0.1 us)
Async XLA Ops:
  0.0 26.7 %copy-start = (f32[8]{0:T(128)S(1)}, f32[8]{0:T(128)}, u32[]{:S(2)}) copy-start(f32[8]{0:T(128)} %table_ref.5) | copy-start | bytes 100
  2.6 24.2 %all-to-all-start = ((f32[8,72,128]{2,1,0:T(8,128)}), f32[8,72,128]{2,1,0:T(8,128)S(1)}, u32[]{:S(2)}, u32[]{:S(2)}) async-start(f32[8,72,128]{2,1,0:T(8,128)} %bitcast.2), calls=%async_computation | async-start | bytes 589824 | tf_op jit(solution)/shard_map/all_to_all | solution.py:427
  14.1 23.4 %collective-permute-start.2 = (f32[32,1024]{1,0:T(8,128)S(1)}, f32[32,1024]{1,0:T(8,128)S(1)}, u32[]{:S(2)}, u32[]{:S(2)}) collective-permute-start(f32[32,1024]{1,0:T(8,128)S(1)} %get-tuple-element.52), channel_id=1, source_target_pairs={{0,1},{2,3},{4,5},{6,7},{1,0},{3,2},{5,4},{7,6},{8,9},{10,11},{12,... | collective-permute-start | bytes 393224 | tf_op jit(solution)/shard_map/ppermute | solution.py:393
  19.5 18.5 %collective-permute-start.3 = (f32[32,1024]{1,0:T(8,128)S(1)}, f32[32,1024]{1,0:T(8,128)S(1)}, u32[]{:S(2)}, u32[]{:S(2)}) collective-permute-start(f32[32,1024]{1,0:T(8,128)S(1)} %get-tuple-element.53), channel_id=1, source_target_pairs={{1,2},{3,4},{5,6},{7,0},{2,1},{4,3},{6,5},{0,7},{9,10},{11,12},{13... | collective-permute-start | bytes 393224 | tf_op jit(solution)/shard_map/ppermute | solution.py:393
  19.5 19.1 %collective-permute-start = (f32[64,1024]{1,0:T(8,128)S(1)}, f32[64,1024]{1,0:T(8,128)S(1)}, u32[]{:S(2)}, u32[]{:S(2)}) collective-permute-start(f32[64,1024]{1,0:T(8,128)S(1)} %get-tuple-element.50), channel_id=1, source_target_pairs={{0,8},{16,24},{32,40},{48,56},{64,72},{80,88},{96,104},{112,120},{... | collective-permute-start | bytes 786440 | tf_op jit(solution)/shard_map/ppermute | solution.py:393
  19.5 20.0 %collective-permute-start.1 = (f32[64,1024]{1,0:T(8,128)S(1)}, f32[64,1024]{1,0:T(8,128)S(1)}, u32[]{:S(2)}, u32[]{:S(2)}) collective-permute-start(f32[64,1024]{1,0:T(8,128)S(1)} %get-tuple-element.51), channel_id=1, source_target_pairs={{8,16},{24,32},{40,48},{56,64},{72,80},{88,96},{104,112},{120,128}... | collective-permute-start | bytes 786440 | tf_op jit(solution)/shard_map/ppermute | solution.py:393
  40.5 13.4 %collective-permute-start.4 = (f32[16,1024]{1,0:T(8,128)S(1)}, f32[16,1024]{1,0:T(8,128)S(1)}, u32[]{:S(2)}, u32[]{:S(2)}) collective-permute-start(f32[16,1024]{1,0:T(8,128)S(1)} %get-tuple-element.63.ya), channel_id=1, source_target_pairs={{0,1},{2,3},{4,5},{6,7},{1,0},{3,2},{5,4},{7,6},{8,9},{10,11},{12,... | collective-permute-start | bytes 196616 | tf_op jit(solution)/shard_map/ppermute | solution.py:393
  46.1 10.4 %collective-permute-start.5 = (f32[16,1024]{1,0:T(8,128)S(1)}, f32[16,1024]{1,0:T(8,128)S(1)}, u32[]{:S(2)}, u32[]{:S(2)}) collective-permute-start(f32[16,1024]{1,0:T(8,128)S(1)} %get-tuple-element.64.yb), channel_id=1, source_target_pairs={{1,2},{3,4},{5,6},{7,0},{2,1},{4,3},{6,5},{0,7},{9,10},{11,12},{13... | collective-permute-start | bytes 196616 | tf_op jit(solution)/shard_map/ppermute | solution.py:393
  49.1 7.4 %collective-permute-start.6 = (f32[32,1024]{1,0:T(8,128)S(1)}, f32[32,1024]{1,0:T(8,128)S(1)}, u32[]{:S(2)}, u32[]{:S(2)}) collective-permute-start(f32[32,1024]{1,0:T(8,128)S(1)} %get-tuple-element.61.xa), channel_id=1, source_target_pairs={{0,8},{16,24},{32,40},{48,56},{64,72},{80,88},{96,104},{112,120},{... | collective-permute-start | bytes 393224 | tf_op jit(solution)/shard_map/ppermute | solution.py:393
  49.1 8.4 %collective-permute-start.7 = (f32[32,1024]{1,0:T(8,128)S(1)}, f32[32,1024]{1,0:T(8,128)S(1)}, u32[]{:S(2)}, u32[]{:S(2)}) collective-permute-start(f32[32,1024]{1,0:T(8,128)S(1)} %get-tuple-element.62.xb), channel_id=1, source_target_pairs={{8,16},{24,32},{40,48},{56,64},{72,80},{88,96},{104,112},{120,128}... | collective-permute-start | bytes 393224 | tf_op jit(solution)/shard_map/ppermute | solution.py:393
  57.6 12.6 %collective-permute-start.8 = (f32[16,1024]{1,0:T(8,128)S(1)}, f32[16,1024]{1,0:T(8,128)S(1)}, u32[]{:S(2)}, u32[]{:S(2)}) collective-permute-start(f32[16,1024]{1,0:T(8,128)S(1)} %get-tuple-element.74.ya), channel_id=1, source_target_pairs={{0,1},{2,3},{4,5},{6,7},{1,0},{3,2},{5,4},{7,6},{8,9},{10,11},{12,... | collective-permute-start | bytes 196616 | tf_op jit(solution)/shard_map/ppermute | solution.py:393
  61.4 11.0 %collective-permute-start.9 = (f32[16,1024]{1,0:T(8,128)S(1)}, f32[16,1024]{1,0:T(8,128)S(1)}, u32[]{:S(2)}, u32[]{:S(2)}) collective-permute-start(f32[16,1024]{1,0:T(8,128)S(1)} %get-tuple-element.75.yb), channel_id=1, source_target_pairs={{1,2},{3,4},{5,6},{7,0},{2,1},{4,3},{6,5},{0,7},{9,10},{11,12},{13... | collective-permute-start | bytes 196616 | tf_op jit(solution)/shard_map/ppermute | solution.py:393
  64.5 8.0 %collective-permute-start.10 = (f32[32,1024]{1,0:T(8,128)S(1)}, f32[32,1024]{1,0:T(8,128)S(1)}, u32[]{:S(2)}, u32[]{:S(2)}) collective-permute-start(f32[32,1024]{1,0:T(8,128)S(1)} %get-tuple-element.72.xa), channel_id=1, source_target_pairs={{0,8},{16,24},{32,40},{48,56},{64,72},{80,88},{96,104},{112,120},{... | collective-permute-start | bytes 393224 | tf_op jit(solution)/shard_map/ppermute | solution.py:393
  64.5 9.9 %collective-permute-start.11 = (f32[32,1024]{1,0:T(8,128)S(1)}, f32[32,1024]{1,0:T(8,128)S(1)}, u32[]{:S(2)}, u32[]{:S(2)}) collective-permute-start(f32[32,1024]{1,0:T(8,128)S(1)} %get-tuple-element.73.xb), channel_id=1, source_target_pairs={{8,16},{24,32},{40,48},{56,64},{72,80},{88,96},{104,112},{120,128}... | collective-permute-start | bytes 393224 | tf_op jit(solution)/shard_map/ppermute | solution.py:393
  74.5 10.8 %collective-permute-start.12 = (f32[16,1024]{1,0:T(8,128)S(1)}, f32[16,1024]{1,0:T(8,128)S(1)}, u32[]{:S(2)}, u32[]{:S(2)}) collective-permute-start(f32[16,1024]{1,0:T(8,128)S(1)} %get-tuple-element.80.ya), channel_id=1, source_target_pairs={{0,1},{2,3},{4,5},{6,7},{1,0},{3,2},{5,4},{7,6},{8,9},{10,11},{12,... | collective-permute-start | bytes 196616 | tf_op jit(solution)/shard_map/ppermute | solution.py:393
  77.4 10.4 %collective-permute-start.13 = (f32[16,1024]{1,0:T(8,128)S(1)}, f32[16,1024]{1,0:T(8,128)S(1)}, u32[]{:S(2)}, u32[]{:S(2)}) collective-permute-start(f32[16,1024]{1,0:T(8,128)S(1)} %get-tuple-element.81.yb), channel_id=1, source_target_pairs={{1,2},{3,4},{5,6},{7,0},{2,1},{4,3},{6,5},{0,7},{9,10},{11,12},{13... | collective-permute-start | bytes 196616 | tf_op jit(solution)/shard_map/ppermute | solution.py:393
  80.6 7.2 %collective-permute-start.14 = (f32[32,1024]{1,0:T(8,128)S(1)}, f32[32,1024]{1,0:T(8,128)S(1)}, u32[]{:S(2)}, u32[]{:S(2)}) collective-permute-start(f32[32,1024]{1,0:T(8,128)S(1)} %get-tuple-element.78.xa), channel_id=1, source_target_pairs={{0,8},{16,24},{32,40},{48,56},{64,72},{80,88},{96,104},{112,120},{... | collective-permute-start | bytes 393224 | tf_op jit(solution)/shard_map/ppermute | solution.py:393
  80.6 9.5 %collective-permute-start.15 = (f32[32,1024]{1,0:T(8,128)S(1)}, f32[32,1024]{1,0:T(8,128)S(1)}, u32[]{:S(2)}, u32[]{:S(2)}) collective-permute-start(f32[32,1024]{1,0:T(8,128)S(1)} %get-tuple-element.79.xb), channel_id=1, source_target_pairs={{8,16},{24,32},{40,48},{56,64},{72,80},{88,96},{104,112},{120,128}... | collective-permute-start | bytes 393224 | tf_op jit(solution)/shard_map/ppermute | solution.py:393

commit v2 on v1

--- a/solution.py
+++ b/solution.py
@@ -145,73 +145,81 @@
     return mid, up, down
 
 
-def prepare_kernel(recv_ref, table_ref, t_hbm, cap_hbm, soil_hbm, inj_hbm,
-                   fx_ref, fy_ref, fz_ref, w_ref, rhs_ref, tn_ref, ex_ref, ey_ref, t_ref, cond, soil, cap, inj, sems):
+def coef_kernel(table_ref, hya, hyb, t_hbm, cap_hbm, soil_hbm, *refs):
+    outs, (more_ref, halo_ref, ex_ref, ey_ref, half_ref, t_ref, cap, soil), made, (in_sems, out_sems) = (
+        refs[:6], refs[6:14], refs[14:20], refs[20:])
+    fx_ref, fy_ref, fz_ref, rhs_ref, tn_ref, w_ref = made
+    step = CX // PARTS
+    spans = [pl.ds(part * step, step) for part in range(PARTS)]
     copies = []
-    step = CX // PARTS
+    for k, (src, dst) in enumerate(((soil_hbm, soil), (t_hbm, t_ref), (cap_hbm, cap))):
+        copies.append([pltpu.make_async_copy(src.at[span], dst.at[span], in_sems.at[k, part]) for part, span in enumerate(spans)])
+        for copy in copies[k]:
+            copy.start()
+    table = [0.5 * table_ref[k] for k in range(NCLS)]
+    gy = lax.axis_index("gy")
+    halo = split(hya[...], hyb[...], even("gy"))
+    for k, inside in enumerate((gy > 0, gy < NGY - 1)):
+        more_ref[k] = lookup(halo[k][CX:].astype(jnp.int32), table) * jnp.where(inside, F32(1.0), F32(0.0))
+        halo_ref[k] = halo[k][0:CX]
+
+    def fill(x, carry):
+        half_ref[x] = lookup(soil[x], table)
+        return carry
+
     for part in range(PARTS):
-        span = pl.ds(part * step, step)
-        for k, (src, dst) in enumerate(((soil_hbm, soil), (t_hbm, t_ref), (cap_hbm, cap))):
-            copies.append(pltpu.make_async_copy(src.at[span], dst.at[span], sems.at[3 * part + k]))
-    copies.append(pltpu.make_async_copy(inj_hbm, inj, sems.at[3 * PARTS]))
-    for copy in copies:
-        copy.start()
-    table = [table_ref[k] for k in range(NCLS)]
-
-    def fill(x, carry):
-        cond[x] = lookup(soil[x], table)
-        return carry
-
-    copies[-1].wait()
-    add_source(recv_ref, inj, rhs_ref)
-    for part in range(PARTS):
-        copies[3 * part].wait()
+        copies[0][part].wait()
         lax.fori_loop(part * step, (part + 1) * step, fill, 0)
     for part in range(PARTS):
-        copies[3 * part + 1].wait()
-        copies[3 * part + 2].wait()
+        copies[1][part].wait()
+        copies[2][part].wait()
     for side, x in enumerate((0, CX - 1)):
-        ex_ref[side, 0] = cond[x]
+        ex_ref[side, 0] = half_ref[x]
         ex_ref[side, 1] = t_ref[x]
     row = lax.broadcasted_iota(jnp.int32, (YT, NZ), 0)
     lane = lax.broadcasted_iota(jnp.int32, (YT, NZ), 1)
+    at_end = lane == NZ - 1
+    at_ends = jnp.logical_or(at_end, lane == 0)
 
     def plane(x, first, last):
         for yt in range(NT):
             rows = slice(yt * YT, (yt + 1) * YT)
             low, high = yt == 0, yt == NT - 1
-            c, cyp, cym = tile_sides(cond, x, yt)
-            half = 0.5 * c
-            fxp = half if last else 0.5 * (c + cond[x + 1, rows, :])
-            fxm = half if first else 0.5 * (c + cond[x - 1, rows, :])
-            fyp, fym = 0.5 * (c + cyp), 0.5 * (c + cym)
+            c, cyp, cym = tile_sides(half_ref, x, yt)
+            t, typ, tym = tile_sides(t_ref, x, yt)
+            fyp, fym = c + cyp, c + cym
+            fz = jnp.where(at_end, F32(0.0), c + pltpu.roll(c, NZ - 1, 1))
+            cp = cap[x, rows, :]
+            diag = cp + fz + pltpu.roll(fz, 1, 1) + jnp.where(at_ends, c, F32(0.0))
             if high:
-                fyp = jnp.where(row == YT - 1, half, fyp)
+                diag = diag + jnp.where(row == YT - 1, c, fyp)
+                fyp = jnp.where(row == YT - 1, F32(0.0), fyp)
+            else:
+                diag = diag + fyp
             if low:
-                fym = jnp.where(row == 0, half, fym)
-            fzp = jnp.where(lane == NZ - 1, half, 0.5 * (c + pltpu.roll(c, NZ - 1, 1)))
-            fzm = jnp.where(lane == 0, half, 0.5 * (c + pltpu.roll(c, 1, 1)))
-            cp = cap[x, rows, :]
-            diag = cp + fxp + fxm + fyp + fym + fzp + fzm
-            t, typ, tym = tile_sides(t_ref, x, yt)
-            rhs = rhs_ref[x, rows, :] + cp * t
-            rhs_ref[x, rows, :] = rhs
-            total = rhs
-            if not last:
+                diag = diag + jnp.where(row == 0, c, fym)
+                fym = jnp.where(row == 0, F32(0.0), fym)
+            else:
+                diag = diag + fym
+            rhs = cp * t
+            total = rhs + fyp * typ + fym * tym
+            if last:
+                diag = diag + c
+            else:
+                fxp = c + half_ref[x + 1, rows, :]
+                diag = diag + fxp
                 total = total + fxp * t_ref[x + 1, rows, :]
                 fx_ref[x, rows, :] = fxp
-            if not first:
+            if first:
+                diag = diag + c
+            else:
+                fxm = c + half_ref[x - 1, rows, :]
+                diag = diag + fxm
                 total = total + fxm * t_ref[x - 1, rows, :]
-            if high:
-                fyp = jnp.where(row == YT - 1, F32(0.0), fyp)
-            if low:
-                fym = jnp.where(row == 0, F32(0.0), fym)
-            fzp = jnp.where(lane == NZ - 1, F32(0.0), fzp)
-            fzm = jnp.where(lane == 0, F32(0.0), fzm)
+            total = total + fz * pltpu.roll(t, NZ - 1, 1) + pltpu.roll(fz * t, 1, 1)
+            rhs_ref[x, rows, :] = rhs
             fy_ref[x, rows, :] = fyp
-            fz_ref[x, rows, :] = fzp
-            total = total + fyp * typ + fym * tym
-            total = total + fzp * pltpu.roll(t, NZ - 1, 1) + fzm * pltpu.roll(t, 1, 1)
+            fz_ref[x, rows, :] = fz
             if first or last:
                 w_ref[x, rows, :] = diag
                 tn_ref[x, rows, :] = total
@@ -229,9 +237,48 @@
         plane(x, False, False)
         return carry
 
-    plane(0, True, False)
+    leaving = []
+    for part in range(PARTS):
+        if part == 0:
+            plane(0, True, False)
+        lax.fori_loop(max(1, part * step), min(CX - 1, (part + 1) * step), inner, 0)
+        if part == PARTS - 1:
+            fx_ref[CX - 1] = jnp.zeros((CY, NZ), F32)
+            plane(CX - 1, False, True)
+        for k in range(6):
+            leaving.append(pltpu.make_async_copy(made[k].at[spans[part]], outs[k].at[spans[part]], out_sems.at[k, part]))
+            leaving[-1].start()
+    for copy in leaving:
+        copy.wait()
+
+
+def source_kernel(recv_ref, inj_hbm, rhs_hbm, tn_hbm, w_hbm, ey_in, rhs_ref, tn_ref, w_ref, ey_ref, source, inj, sems):
+    pairs = [(inj_hbm, inj), (rhs_hbm, rhs_ref), (tn_hbm, tn_ref), (w_hbm, w_ref)]
+    copies = [pltpu.make_async_copy(src, dst, sems.at[k]) for k, (src, dst) in enumerate(pairs)]
+    for copy in copies:
+        copy.start()
+    copies[0].wait()
+    add_source(recv_ref, inj, source)
+    copies[1].wait()
+    copies[2].wait()
+    copies[3].wait()
+
+    def plane(x, edge):
+        for yt in range(NT):
+            rows = slice(yt * YT, (yt + 1) * YT)
+            src = source[x, rows, :]
+            rhs_ref[x, rows, :] = rhs_ref[x, rows, :] + src
+            tn_ref[x, rows, :] = tn_ref[x, rows, :] + (src if edge else w_ref[x, rows, :] * src)
+        for side, y in enumerate((0, CY - 1)):
+            ey_ref[side, 0, pl.ds(x, 1), :] = ey_in[side, 0, pl.ds(x, 1), :] + source[x, y:y + 1, :]
+
+    def inner(x, carry):
+        plane(x, False)
+        return carry
+
+    plane(0, True)
     lax.fori_loop(1, CX - 1, inner, 0)
-    plane(CX - 1, False, True)
+    plane(CX - 1, True)
 
 
 def at_row(shape, index, value):
@@ -246,30 +293,18 @@
             yhi + at_row(ys, 0, xlo[CY - 1:CY]) + at_row(ys, CX - 1, xhi[CY - 1:CY]))
 
 
-def fix_y_kernel(table_ref, hya, hyb, ey_ref, more_ref, face_ref, term_ref):
-    table = [table_ref[k] for k in range(NCLS)]
-    gy = lax.axis_index("gy")
-    halo = split(hya[...], hyb[...], even("gy"))
-    for k, inside in enumerate((gy > 0, gy < NGY - 1)):
-        inside = jnp.where(inside, F32(1.0), F32(0.0))
-        more = 0.5 * lookup(halo[k][CX:].astype(jnp.int32), table) * inside
-        face = (0.5 * ey_ref[k, 2] + more) * inside
-        more_ref[k] = more
-        face_ref[k] = face
-        term_ref[k] = face * halo[k][0:CX]
-
-
-def fix_kernel(table_ref, hxa, hxb, my_ref, fy_ref, gy_ref, w_ref, tn_ref, ex_ref, ey_ref,
+def fix_kernel(table_ref, hxa, hxb, my_ref, ty_ref, w_ref, tn_ref, ex_ref, ey_ref,
                xa, xb, ya, yb, wx_ref, wy_ref, ax_ref, ay_ref):
-    table = [table_ref[k] for k in range(NCLS)]
-    gx = lax.axis_index("gx")
-    within = [jnp.where(q, F32(1.0), F32(0.0)) for q in (gx > 0, gx < NGX - 1)]
-    t_halo = split(hxa[0:CY, :], hxb[0:CY, :], even("gx"))
+    table = [0.5 * table_ref[k] for k in range(NCLS)]
+    gx, gy = lax.axis_index("gx"), lax.axis_index("gy")
+    within = [jnp.where(q, F32(1.0), F32(0.0)) for q in (gx > 0, gx < NGX - 1, gy > 0, gy < NGY - 1)]
+    t_halo = split(hxa[0:CY, :], hxb[0:CY, :], even("gx")) + (ty_ref[0], ty_ref[1])
     klass = split(hxa[CY:, :], hxb[CY:, :], even("gx"))
-    more = [0.5 * lookup(k.astype(jnp.int32), table) * q for k, q in zip(klass, within)]
-    face = [(0.5 * ex_ref[k, 0] + more[k]) * within[k] for k in range(2)] + [fy_ref[0], fy_ref[1]]
-    diag = with_corners(*more, my_ref[0], my_ref[1])
-    total = with_corners(face[0] * t_halo[0], face[1] * t_halo[1], gy_ref[0], gy_ref[1])
+    more = [lookup(k.astype(jnp.int32), table) * q for k, q in zip(klass, within)] + [my_ref[0], my_ref[1]]
+    conds = (ex_ref[0, 0], ex_ref[1, 0], ey_ref[0, 2], ey_ref[1, 2])
+    face = [(c + m) * q for c, m, q in zip(conds, more, within)]
+    diag = with_corners(*more)
+    total = with_corners(*[f * t for f, t in zip(face, t_halo)])
     total = [a + b for a, b in zip(total, (tn_ref[0], tn_ref[CX - 1], ey_ref[0, 0], ey_ref[1, 0]))]
     w = [0.8 / (a + b) for a, b in zip(diag, (w_ref[0], w_ref[CX - 1], ey_ref[0, 1], ey_ref[1, 1]))]
     old = (ex_ref[0, 1], ex_ref[1, 1], ey_ref[0, 3], ey_ref[1, 3])
@@ -309,7 +344,6 @@
 
 def sweep_plane(x, first, last, t_ref, fx_ref, fy_ref, fz_ref, w_ref, rhs_ref, tn_ref, py_ref):
     row = lax.broadcasted_iota(jnp.int32, (YT, NZ), 0)
-    lane = lax.broadcasted_iota(jnp.int32, (YT, NZ), 1)
     for yt in range(NT):
         rows = slice(yt * YT, (yt + 1) * YT)
         t, typ, tym = tile_sides(t_ref, x, yt)
@@ -323,7 +357,7 @@
         if not first:
             total = total + fx_ref[x - 1, rows, :] * t_ref[x - 1, rows, :]
         total = total + fz * pltpu.roll(t, NZ - 1, 1)
-        total = total + jnp.where(lane == 0, F32(0.0), pltpu.roll(fz * t, 1, 1))
+        total = total + pltpu.roll(fz * t, 1, 1)
         tn = (1.0 - 0.8) * t + w_ref[x, rows, :] * total
         tn_ref[x, rows, :] = tn
         if yt == 0:
@@ -340,10 +374,25 @@
     lax.fori_loop(start, stop, inner, 0)
 
 
-def first_sweep_kernel(fx_ref, fy_ref, fz_ref, rhs_ref, xa, xb, ya, yb, wx_ref, wy_ref, w_in, t_in,
-                       w_ref, t_ref, tn_ref, py_ref):
+def first_sweep_kernel(fx_hbm, fy_hbm, fz_hbm, rhs_ref, xa, xb, ya, yb, wx_ref, wy_ref, w_in, t_in,
+                       w_ref, t_ref, tn_ref, py_ref, fx_ref, fy_ref, fz_ref, sems):
+    step = CX // PARTS
+    pairs = ((fx_hbm, fx_ref), (fy_hbm, fy_ref), (fz_hbm, fz_ref))
+    copies = [[pltpu.make_async_copy(src.at[pl.ds(part * step, step)], dst.at[pl.ds(part * step, step)], sems.at[k, part])
+               for k, (src, dst) in enumerate(pairs)] for part in range(PARTS)]
+    for part in range(PARTS):
+        for copy in copies[part]:
+            copy.start()
     put_edges(w_ref, wx_ref[0], wx_ref[1], wy_ref[0], wy_ref[1])
-    sweep(fx_ref, fy_ref, fz_ref, rhs_ref, w_ref, xa, xb, ya, yb, t_ref, tn_ref, py_ref)
+    put_edges(t_ref, *split(xa[...], xb[...], even("gx")), *split(ya[...], yb[...], even("gy")))
+    refs = (t_ref, fx_ref, fy_ref, fz_ref, w_ref, rhs_ref, tn_ref, py_ref)
+    for part in range(PARTS):
+        for copy in copies[part]:
+            copy.wait()
+        if part == 0:
+            sweep_plane(0, True, False, *refs)
+        sweep_inside(refs, max(1, part * step), min(CX - 1, (part + 1) * step))
+    sweep_plane(CX - 1, False, True, *refs)
 
 
 def sweep(fx_ref, fy_ref, fz_ref, rhs_ref, w_ref, xa, xb, ya, yb, t_ref, tn_ref, py_ref):
@@ -415,6 +464,7 @@
 XX, YY = local(2, CY, NZ), local(2, CX, NZ)
 DMA = pltpu.SemaphoreType.DMA
 I32 = jnp.int32
+FIXY, PREP = 20.0, 0.1
 
 
 def shards(temp_old, capacity, soil_class, cond_table, losses, owner, column, injection):
@@ -426,22 +476,25 @@
         *far(temp_old, soil_class, losses, owner.reshape(1, SEG), column.reshape(1, SEG)))
     recv = lax.all_to_all(send, "gy", 0, 0, tiled=True)
     halo = exchange(*faces)
-    fx, fy, fz, w, rhs, new, ex, ey = call(
-        prepare_kernel, (SLAB,) * 6 + (local(2, 2, CY, NZ), local(2, 4, CX, NZ)), [VM, SM] + [HB] * 4,
-        [SLAB, SLAB, local(CX, CY, NZ, dtype=I32), SLAB, local(LW, NZ), DMA((3 * PARTS + 1,))], mib=16, us=0.1)(
-        *near(recv), cond_table, *far(temp_old, capacity, soil_class, injection))
     hxa, hxb, hya, hyb = halo
-    my, fyh, gy = call(fix_y_kernel, (YY, YY, YY), [SM] + [VM] * 3, us=8.0)(cond_table, hya, hyb, *near(ey))
-    *faces, wx, wy, ax, ay = call(
-        fix_kernel, FACES + (XX, YY, XX, YY), [SM] + [VM] * 9, mib=2)(
-        cond_table, hxa, hxb, *near(my, fyh, gy, w, new, ex, ey))
+    edge_x, edge_y = local(2, 2, CY, NZ), local(2, 4, CX, NZ)
+    *stored, my, ty, ex, ey = call(
+        coef_kernel, (pltpu.HBM((CX, CY, NZ), F32),) * 6 + (YY, YY, edge_x, edge_y), [SM] + [VM] * 2 + [HB] * 3,
+        [SLAB, SLAB, SLAB, local(CX, CY, NZ, dtype=I32)] + [SLAB] * 6 + [DMA((3, PARTS)), DMA((6, PARTS))],
+        mib=24, us=FIXY, out_specs=[HB] * 6 + [VM] * 4)(
+        cond_table, hya, hyb, *far(temp_old, capacity, soil_class))
+    rhs, new, w, ey = call(
+        source_kernel, (SLAB,) * 3 + (edge_y,), [VM] + [HB] * 4 + [VM], [SLAB, local(LW, NZ), DMA((4,))],
+        alias={5: 3}, mib=8, us=PREP)(*near(recv), *far(injection, *stored[3:]), *near(ey))
+    *faces, wx, wy, ax, ay = call(fix_kernel, FACES + (XX, YY, XX, YY), [SM] + [VM] * 8, mib=2)(
+        cond_table, hxa, hxb, *near(my, ty, w, new, ex, ey))
     for number in range(1, SWEEPS):
         halo = exchange(*faces)
-        coefs = near(fx, fy, fz, rhs)
         if number == 1:
-            w, temp, new, py = call(
-                first_sweep_kernel, (SLAB, SLAB, SLAB, YY), [VM] * 12, alias={10: 0, 11: 1}, mib=2)(
-                *coefs, *near(*faces, wx, wy, w, new))
+            w, temp, new, py, fx, fy, fz = call(
+                first_sweep_kernel, (SLAB, SLAB, SLAB, YY, SLAB, SLAB, SLAB), [HB] * 3 + [VM] * 9, [DMA((3, PARTS))],
+                alias={10: 0, 11: 1}, mib=2)(*far(*stored[:3]), *near(rhs, *faces, wx, wy, w, new))
+            coefs = near(fx, fy, fz, rhs)
         elif number < SWEEPS - 1:
             temp, new, py = call(sweep_kernel, (SLAB, SLAB, YY), [VM] * 10, alias={9: 0}, mib=2)(
                 *coefs, *near(w, *faces, new))

time: 91.6 us -> 90.3 us (0.986)
  starting transfers between devices: 49.7 us -> 47.6 us
  Pallas kernels: 24.8 us -> 26.9 us
  waiting for transfers between devices: 16.6 us -> 15.3 us
    all_to_all x1, waiting for transfers between devices: 2.97 us -> 0.01 us  [shards(): recv = lax.all_to_all(send, 'gy', 0, 0, tiled=True)]
    pallas_call x4, Pallas kernels: 15.2 us -> 17.9 us  [the longest x1 9.4 us: shards(): call(coef_kernel, (pltpu.HBM((CX, CY, NZ), F32),) * 6 + (YY, YY, edge_x,...]
    ppermute x16, waiting for transfers between devices: 13.6 us -> 15.3 us  [swaps(): lax.ppermute(v, axis, p + [(j, i) for i, j in p])]
    ppermute x16, starting transfers between devices: 38.2 us -> 36.9 us  [swaps(): lax.ppermute(v, axis, p + [(j, i) for i, j in p])]
  transfers between devices with their start and end apart: 17 -> 17, of which waited for: 9 -> 6; matrix products, arithmetic and copies ran while one was open for 0% -> 0% of each run, Pallas kernels for 22% -> 24%
where the time goes in v2:
time: 90.3 us; the launch traced here: 90.1 us
  starting transfers between devices  47.6 us (53%)
  Pallas kernels  26.9 us (30%)
  waiting for transfers between devices  15.3 us (17%)
    ppermute x16, starting transfers between devices, swaps(): lax.ppermute(v, axis, p + [(j, i) for i, j in p])  36.9 us
    ppermute x16, waiting for transfers between devices, swaps(): lax.ppermute(v, axis, p + [(j, i) for i, j in p])  15.3 us
    all_to_all x1, starting transfers between devices, shards(): recv = lax.all_to_all(send, 'gy', 0, 0, tiled=True)  10.6 us
    pallas_call x1, Pallas kernels, shards(): call(coef_kernel, (pltpu.HBM((CX, CY, NZ), F32),) * 6 + (YY, YY, edge_x,...  9.4 us
    pallas_call x1, Pallas kernels, shards(): call(first_sweep_kernel, (SLAB, SLAB, SLAB, YY, SLAB, SLAB, SLAB), [HB] *...  3.79 us
    pallas_call x1, Pallas kernels, shards(): call(source_kernel, (SLAB,) * 3 + (edge_y,), [VM] + [HB] * 4 + [VM], [SLA...  3.68 us
    pallas_call x1, Pallas kernels, shards(): call(last_sweep_kernel, (SLAB, SLAB, YY, pltpu.HBM((CX, CY, NZ), F32)), [...  2.8 us
    pallas_call x1, Pallas kernels, shards(): call(start_kernel, (local(NGY * CHUNK, LW),) + (local(2 * CY, NZ),) * 2 +...  2.58 us
  transfers between devices with their start and end apart: 17, of which 6 were waited for; matrix products, arithmetic and copies ran while one was open for 0% of the time, Pallas kernels for 24%

profile of v2, /device:TPU:8, one launch (start us, length us, event | category | flops | bytes accessed | tf_op | source)
XLA Modules:
  0.0 90.1 jit_solution(13980823820230900351)
XLA Ops:
  0.0 0.0 copy-start
  0.0 2.6 %shard_map.82 = (f32[576,128]{1,0:T(8,128)}, f32[64,1024]{1,0:T(8,128)S(1)}, f32[64,1024]{1,0:T(8,128)S(1)}, f32[32,1024]{1,0:T(8,128)S(1)}, f32[32,1024]{1,0:T(8,128)S(1)}) custom-call(f32[16,32,1024]{2,1,0:T(8,128)} %t_hbm.3, s32[16,32,1024]{2,1,0:T(8,128)} %soil_hbm.3, f32[256,128]{1,0:T(8,128)} %loss_hbm.1, s32[1,256]{1,0:T(1,128)} %bitcast.5, ...), custom_call_target="tpu_custom_call" | custom-call | flops 100000000 | bytes 300000 | tf_op jit(solution)/shard_map/pallas_call | solution.py:472
  2.6 7.3 %collective-permute-start = (f32[32,1024]{1,0:T(8,128)S(1)}, f32[32,1024]{1,0:T(8,128)S(1)}, u32[]{:S(2)}, u32[]{:S(2)}) collective-permute-start(f32[32,1024]{1,0:T(8,128)S(1)} %get-tuple-element.51), channel_id=1, source_target_pairs={{0,1},{2,3},{4,5},{6,7},{1,0},{3,2},{5,4},{7,6},{8,9},{10,11},{12,... | collective-permute-start | bytes 393224 | tf_op jit(solution)/shard_map/ppermute | solution.py:442
  9.9 0.4 collective-permute-start.1
  10.2 10.6 %all-to-all-start = ((f32[8,72,128]{2,1,0:T(8,128)}), f32[8,72,128]{2,1,0:T(8,128)S(1)}, u32[]{:S(2)}, u32[]{:S(2)}) async-start(f32[8,72,128]{2,1,0:T(8,128)} %bitcast.2), calls=%async_computation | async-start | bytes 589824 | tf_op jit(solution)/shard_map/all_to_all | solution.py:477
  20.9 0.0 collective-permute-start.2
  20.9 4.2 %collective-permute-start.3 = (f32[64,1024]{1,0:T(8,128)S(1)}, f32[64,1024]{1,0:T(8,128)S(1)}, u32[]{:S(2)}, u32[]{:S(2)}) collective-permute-start(f32[64,1024]{1,0:T(8,128)S(1)} %get-tuple-element.63), channel_id=1, source_target_pairs={{8,16},{24,32},{40,48},{56,64},{72,80},{88,96},{104,112},{120,128}... | collective-permute-start | bytes 786440 | tf_op jit(solution)/shard_map/ppermute | solution.py:442
  25.1 0.0 collective-permute-done.hya
  25.1 0.0 collective-permute-done.1.hyb
  25.1 0.0 copy-done
  25.1 9.4 %shard_map.83 = (f32[16,32,1024]{2,1,0:T(8,128)}, f32[16,32,1024]{2,1,0:T(8,128)}, f32[16,32,1024]{2,1,0:T(8,128)}, f32[16,32,1024]{2,1,0:T(8,128)}, f32[16,32,1...) custom-call(f32[8]{0:T(128)S(1)} %copy-done, ...), custom_call_target="tpu_custom_call" | custom-call | flops 20000000000 | bytes 60000000 | tf_op jit(solution)/shard_map/pallas_call | solution.py:481
  34.5 0.0 all-to-all-done
  34.5 3.7 %shard_map.84 = (f32[16,32,1024]{2,1,0:T(8,128)S(1)}, f32[16,32,1024]{2,1,0:T(8,128)S(1)}, f32[16,32,1024]{2,1,0:T(8,128)S(1)}, f32[2,4,16,1024]{3,2,1,0:T(8,128)S(1)}) custom-call(f32[576,128]{1,0:T(8,128)S(1)} %bitcast.4, f32[128,1024]{1,0:T(8,128)} %inj_hbm.1, f32[16,32,1024]{2,1,0:T(8,128)} %get-tuple-element.57.rhs_hbm, ...), custom_call_target="tpu_custom_call", output_to_operand_aliasing={{3}: (5, {})} | custom-call | flops 100000000 | bytes 300000 | tf_op jit(solution)/shard_map/pallas_call | solution.py:486
  38.2 0.0 collective-permute-done.2.hxa
  38.2 0.0 collective-permute-done.3.hxb
  38.2 1.0 %shard_map.85 = (f32[32,1024]{1,0:T(8,128)S(1)}, f32[32,1024]{1,0:T(8,128)S(1)}, f32[16,1024]{1,0:T(8,128)S(1)}, f32[16,1024]{1,0:T(8,128)S(1)}, f32[2,32,1024]{...) custom-call(f32[8]{0:T(128)S(1)} %copy-done, ...), custom_call_target="tpu_custom_call" | custom-call | flops 100000000 | bytes 300000 | tf_op jit(solution)/shard_map/pallas_call | solution.py:489
  39.2 5.5 %collective-permute-start.4 = (f32[16,1024]{1,0:T(8,128)S(1)}, f32[16,1024]{1,0:T(8,128)S(1)}, u32[]{:S(2)}, u32[]{:S(2)}) collective-permute-start(f32[16,1024]{1,0:T(8,128)S(1)} %get-tuple-element.72.ya), channel_id=1, source_target_pairs={{0,1},{2,3},{4,5},{6,7},{1,0},{3,2},{5,4},{7,6},{8,9},{10,11},{12,... | collective-permute-start | bytes 196616 | tf_op jit(solution)/shard_map/ppermute | solution.py:442
  44.7 1.7 %collective-permute-start.5 = (f32[16,1024]{1,0:T(8,128)S(1)}, f32[16,1024]{1,0:T(8,128)S(1)}, u32[]{:S(2)}, u32[]{:S(2)}) collective-permute-start(f32[16,1024]{1,0:T(8,128)S(1)} %get-tuple-element.73.yb), channel_id=1, source_target_pairs={{1,2},{3,4},{5,6},{7,0},{2,1},{4,3},{6,5},{0,7},{9,10},{11,12},{13... | collective-permute-start | bytes 196616 | tf_op jit(solution)/shard_map/ppermute | solution.py:442
  46.4 0.0 collective-permute-start.6
  46.4 2.2 %collective-permute-start.7 = (f32[32,1024]{1,0:T(8,128)S(1)}, f32[32,1024]{1,0:T(8,128)S(1)}, u32[]{:S(2)}, u32[]{:S(2)}) collective-permute-start(f32[32,1024]{1,0:T(8,128)S(1)} %get-tuple-element.71.xb), channel_id=1, source_target_pairs={{8,16},{24,32},{40,48},{56,64},{72,80},{88,96},{104,112},{120,128}... | collective-permute-start | bytes 393224 | tf_op jit(solution)/shard_map/ppermute | solution.py:442
  48.6 3.8 %shard_map.86 = (f32[16,32,1024]{2,1,0:T(8,128)S(1)}, f32[16,32,1024]{2,1,0:T(8,128)S(1)}, f32[16,32,1024]{2,1,0:T(8,128)S(1)}, f32[2,16,1024]{2,1,0:T(8,128)S(1...) custom-call(f32[16,32,1024]{2,1,0:T(8,128)} %get-tuple-element.53.fx, ...), custom_call_target="tpu_custom_call", output_to_operand_aliasing={{0}: (10, {}), {1}: (11, {})} | custom-call | flops 100000000 | bytes 300000 | tf_op jit(solution)/shard_map/pallas_call | solution.py:494
  52.4 0.0 collective-permute-done.4.hya
  52.5 1.8 %collective-permute-done.5.hyb = f32[16,1024]{1,0:T(8,128)S(1)} collective-permute-done((f32[16,1024]{1,0:T(8,128)S(1)}, f32[16,1024]{1,0:T(8,128)S(1)}, u32[]{:S(2)}, u32[]{:S(2)}) %collective-permute-start.5) | collective-permute-done | bytes 65568 | tf_op jit(solution)/shard_map/ppermute | solution.py:442
  54.3 0.0 collective-permute-done.6.hxa
  54.3 1.7 %collective-permute-done.7.hxb = f32[32,1024]{1,0:T(8,128)S(1)} collective-permute-done((f32[32,1024]{1,0:T(8,128)S(1)}, f32[32,1024]{1,0:T(8,128)S(1)}, u32[]{:S(2)}, u32[]{:S(2)}) %collective-permute-start.7) | collective-permute-done | bytes 131104 | tf_op jit(solution)/shard_map/ppermute | solution.py:442
  56.0 0.1 shard_map.88
  56.1 5.0 %collective-permute-start.8 = (f32[16,1024]{1,0:T(8,128)S(1)}, f32[16,1024]{1,0:T(8,128)S(1)}, u32[]{:S(2)}, u32[]{:S(2)}) collective-permute-start(f32[16,1024]{1,0:T(8,128)S(1)} %get-tuple-element.86.ya), channel_id=1, source_target_pairs={{0,1},{2,3},{4,5},{6,7},{1,0},{3,2},{5,4},{7,6},{8,9},{10,11},{12,... | collective-permute-start | bytes 196616 | tf_op jit(solution)/shard_map/ppermute | solution.py:442
  61.1 1.1 %collective-permute-start.9 = (f32[16,1024]{1,0:T(8,128)S(1)}, f32[16,1024]{1,0:T(8,128)S(1)}, u32[]{:S(2)}, u32[]{:S(2)}) collective-permute-start(f32[16,1024]{1,0:T(8,128)S(1)} %get-tuple-element.87.yb), channel_id=1, source_target_pairs={{1,2},{3,4},{5,6},{7,0},{2,1},{4,3},{6,5},{0,7},{9,10},{11,12},{13... | collective-permute-start | bytes 196616 | tf_op jit(solution)/shard_map/ppermute | solution.py:442
  62.2 0.0 collective-permute-start.10
  62.2 1.8 %collective-permute-start.11 = (f32[32,1024]{1,0:T(8,128)S(1)}, f32[32,1024]{1,0:T(8,128)S(1)}, u32[]{:S(2)}, u32[]{:S(2)}) collective-permute-start(f32[32,1024]{1,0:T(8,128)S(1)} %get-tuple-element.85.xb), channel_id=1, source_target_pairs={{8,16},{24,32},{40,48},{56,64},{72,80},{88,96},{104,112},{120,128}... | collective-permute-start | bytes 393224 | tf_op jit(solution)/shard_map/ppermute | solution.py:442
  64.0 2.3 %shard_map.89 = (f32[16,32,1024]{2,1,0:T(8,128)S(1)}, f32[16,32,1024]{2,1,0:T(8,128)S(1)}, f32[2,16,1024]{2,1,0:T(8,128)S(1)}) custom-call(f32[16,32,1024]{2,1,0:T(8,128)S(1)} %get-tuple-element.76.fx_ref, f32[16,32,1024]{2,1,0:T(8,128)S(1)} %get-tuple-element.77.fy_ref, ...), custom_call_target="tpu_custom_call", output_to_operand_aliasing={{0}: (9, {})} | custom-call | flops 100000000 | bytes 300000 | tf_op jit(solution)/shard_map/pallas_call | solution.py:499
  66.4 0.0 collective-permute-done.8.hya
  66.4 4.8 %collective-permute-done.9.hyb = f32[16,1024]{1,0:T(8,128)S(1)} collective-permute-done((f32[16,1024]{1,0:T(8,128)S(1)}, f32[16,1024]{1,0:T(8,128)S(1)}, u32[]{:S(2)}, u32[]{:S(2)}) %collective-permute-start.9) | collective-permute-done | bytes 65568 | tf_op jit(solution)/shard_map/ppermute | solution.py:442
  71.2 0.0 collective-permute-done.10.hxa
  71.2 0.8 collective-permute-done.11.hxb
  72.1 0.1 shard_map.91
  72.2 4.5 %collective-permute-start.12 = (f32[16,1024]{1,0:T(8,128)S(1)}, f32[16,1024]{1,0:T(8,128)S(1)}, u32[]{:S(2)}, u32[]{:S(2)}) collective-permute-start(f32[16,1024]{1,0:T(8,128)S(1)} %get-tuple-element.92.ya), channel_id=1, source_target_pairs={{0,1},{2,3},{4,5},{6,7},{1,0},{3,2},{5,4},{7,6},{8,9},{10,11},{12,... | collective-permute-start | bytes 196616 | tf_op jit(solution)/shard_map/ppermute | solution.py:442
  76.7 2.1 %collective-permute-start.13 = (f32[16,1024]{1,0:T(8,128)S(1)}, f32[16,1024]{1,0:T(8,128)S(1)}, u32[]{:S(2)}, u32[]{:S(2)}) collective-permute-start(f32[16,1024]{1,0:T(8,128)S(1)} %get-tuple-element.93.yb), channel_id=1, source_target_pairs={{1,2},{3,4},{5,6},{7,0},{2,1},{4,3},{6,5},{0,7},{9,10},{11,12},{13... | collective-permute-start | bytes 196616 | tf_op jit(solution)/shard_map/ppermute | solution.py:442
  78.7 0.0 collective-permute-start.14
  78.7 1.2 %collective-permute-start.15 = (f32[32,1024]{1,0:T(8,128)S(1)}, f32[32,1024]{1,0:T(8,128)S(1)}, u32[]{:S(2)}, u32[]{:S(2)}) collective-permute-start(f32[32,1024]{1,0:T(8,128)S(1)} %get-tuple-element.91.xb), channel_id=1, source_target_pairs={{8,16},{24,32},{40,48},{56,64},{72,80},{88,96},{104,112},{120,128}... | collective-permute-start | bytes 393224 | tf_op jit(solution)/shard_map/ppermute | solution.py:442
  79.9 2.8 %shard_map.92 = (f32[16,32,1024]{2,1,0:T(8,128)S(1)}, f32[16,32,1024]{2,1,0:T(8,128)S(1)}, f32[2,16,1024]{2,1,0:T(8,128)S(1)}, f32[16,32,1024]{2,1,0:T(8,128)}) custom-call(f32[16,32,1024]{2,1,0:T(8,128)S(1)} %get-tuple-element.76.fx_ref, f32[16,32,1024]{2,1,0:T(8,128)S(1)} %get-tuple-element.77.fy_ref, ...), custom_call_target="tpu_custom_call", output_to_operand_aliasing={{0}: (9, {})} | custom-call | flops 100000000 | bytes 300000 | tf_op jit(solution)/shard_map/pallas_call | solution.py:502
  82.7 0.0 collective-permute-done.12.hya
  82.7 3.9 %collective-permute-done.13.hyb = f32[16,1024]{1,0:T(8,128)S(1)} collective-permute-done((f32[16,1024]{1,0:T(8,128)S(1)}, f32[16,1024]{1,0:T(8,128)S(1)}, u32[]{:S(2)}, u32[]{:S(2)}) %collective-permute-start.13) | collective-permute-done | bytes 65568 | tf_op jit(solution)/shard_map/ppermute | solution.py:442
  86.6 0.0 collective-permute-done.14.hxa
  86.7 2.2 %collective-permute-done.15.hxb = f32[32,1024]{1,0:T(8,128)S(1)} collective-permute-done((f32[32,1024]{1,0:T(8,128)S(1)}, f32[32,1024]{1,0:T(8,128)S(1)}, u32[]{:S(2)}, u32[]{:S(2)}) %collective-permute-start.15) | collective-permute-done | bytes 131104 | tf_op jit(solution)/shard_map/ppermute | solution.py:442
  88.9 1.1 %shard_map.94 = f32[16,32,1024]{2,1,0:T(8,128)} custom-call(f32[16,32,1024]{2,1,0:T(8,128)S(1)} %get-tuple-element.94.tn_ref, f32[2,16,1024]{2,1,0:T(8,128)S(1)} %get-tuple-element.95.py_ref, f32[2,32,1024]{2,1,0:T(8,128)S(1)} %get-tuple-element.82.ax_ref, f32[2,16,1024]{2,1,0:T(8,128)S(1)} %shard_map.93.gy_ref, ...), custom_call_target="tpu_custom_call", output_to_operand_aliasing={{}: (6, {})} | custom-call | flops 100000000 | bytes 300000 | tf_op jit(solution)/shard_map/pallas_call | solution.py:510
  (3 shorter events, 0.1 us)
Async XLA Ops:
  0.0 25.1 %copy-start = (f32[8]{0:T(128)S(1)}, f32[8]{0:T(128)}, u32[]{:S(2)}) copy-start(f32[8]{0:T(128)} %table_ref.3) | copy-start | bytes 100
  2.6 22.5 %collective-permute-start = (f32[32,1024]{1,0:T(8,128)S(1)}, f32[32,1024]{1,0:T(8,128)S(1)}, u32[]{:S(2)}, u32[]{:S(2)}) collective-permute-start(f32[32,1024]{1,0:T(8,128)S(1)} %get-tuple-element.51), channel_id=1, source_target_pairs={{0,1},{2,3},{4,5},{6,7},{1,0},{3,2},{5,4},{7,6},{8,9},{10,11},{12,... | collective-permute-start | bytes 393224 | tf_op jit(solution)/shard_map/ppermute | solution.py:442
  9.9 15.2 %collective-permute-start.1 = (f32[32,1024]{1,0:T(8,128)S(1)}, f32[32,1024]{1,0:T(8,128)S(1)}, u32[]{:S(2)}, u32[]{:S(2)}) collective-permute-start(f32[32,1024]{1,0:T(8,128)S(1)} %get-tuple-element.52), channel_id=1, source_target_pairs={{1,2},{3,4},{5,6},{7,0},{2,1},{4,3},{6,5},{0,7},{9,10},{11,12},{13... | collective-permute-start | bytes 393224 | tf_op jit(solution)/shard_map/ppermute | solution.py:442
  10.2 24.3 %all-to-all-start = ((f32[8,72,128]{2,1,0:T(8,128)}), f32[8,72,128]{2,1,0:T(8,128)S(1)}, u32[]{:S(2)}, u32[]{:S(2)}) async-start(f32[8,72,128]{2,1,0:T(8,128)} %bitcast.2), calls=%async_computation | async-start | bytes 589824 | tf_op jit(solution)/shard_map/all_to_all | solution.py:477
  20.9 17.4 %collective-permute-start.2 = (f32[64,1024]{1,0:T(8,128)S(1)}, f32[64,1024]{1,0:T(8,128)S(1)}, u32[]{:S(2)}, u32[]{:S(2)}) collective-permute-start(f32[64,1024]{1,0:T(8,128)S(1)} %get-tuple-element.62), channel_id=1, source_target_pairs={{0,8},{16,24},{32,40},{48,56},{64,72},{80,88},{96,104},{112,120},{... | collective-permute-start | bytes 786440 | tf_op jit(solution)/shard_map/ppermute | solution.py:442
  20.9 17.4 %collective-permute-start.3 = (f32[64,1024]{1,0:T(8,128)S(1)}, f32[64,1024]{1,0:T(8,128)S(1)}, u32[]{:S(2)}, u32[]{:S(2)}) collective-permute-start(f32[64,1024]{1,0:T(8,128)S(1)} %get-tuple-element.63), channel_id=1, source_target_pairs={{8,16},{24,32},{40,48},{56,64},{72,80},{88,96},{104,112},{120,128}... | collective-permute-start | bytes 786440 | tf_op jit(solution)/shard_map/ppermute | solution.py:442
  39.2 13.2 %collective-permute-start.4 = (f32[16,1024]{1,0:T(8,128)S(1)}, f32[16,1024]{1,0:T(8,128)S(1)}, u32[]{:S(2)}, u32[]{:S(2)}) collective-permute-start(f32[16,1024]{1,0:T(8,128)S(1)} %get-tuple-element.72.ya), channel_id=1, source_target_pairs={{0,1},{2,3},{4,5},{6,7},{1,0},{3,2},{5,4},{7,6},{8,9},{10,11},{12,... | collective-permute-start | bytes 196616 | tf_op jit(solution)/shard_map/ppermute | solution.py:442
  44.7 9.6 %collective-permute-start.5 = (f32[16,1024]{1,0:T(8,128)S(1)}, f32[16,1024]{1,0:T(8,128)S(1)}, u32[]{:S(2)}, u32[]{:S(2)}) collective-permute-start(f32[16,1024]{1,0:T(8,128)S(1)} %get-tuple-element.73.yb), channel_id=1, source_target_pairs={{1,2},{3,4},{5,6},{7,0},{2,1},{4,3},{6,5},{0,7},{9,10},{11,12},{13... | collective-permute-start | bytes 196616 | tf_op jit(solution)/shard_map/ppermute | solution.py:442
  46.4 7.9 %collective-permute-start.6 = (f32[32,1024]{1,0:T(8,128)S(1)}, f32[32,1024]{1,0:T(8,128)S(1)}, u32[]{:S(2)}, u32[]{:S(2)}) collective-permute-start(f32[32,1024]{1,0:T(8,128)S(1)} %get-tuple-element.70.xa), channel_id=1, source_target_pairs={{0,8},{16,24},{32,40},{48,56},{64,72},{80,88},{96,104},{112,120},{... | collective-permute-start | bytes 393224 | tf_op jit(solution)/shard_map/ppermute | solution.py:442
  46.4 9.6 %collective-permute-start.7 = (f32[32,1024]{1,0:T(8,128)S(1)}, f32[32,1024]{1,0:T(8,128)S(1)}, u32[]{:S(2)}, u32[]{:S(2)}) collective-permute-start(f32[32,1024]{1,0:T(8,128)S(1)} %get-tuple-element.71.xb), channel_id=1, source_target_pairs={{8,16},{24,32},{40,48},{56,64},{72,80},{88,96},{104,112},{120,128}... | collective-permute-start | bytes 393224 | tf_op jit(solution)/shard_map/ppermute | solution.py:442
  56.1 10.3 %collective-permute-start.8 = (f32[16,1024]{1,0:T(8,128)S(1)}, f32[16,1024]{1,0:T(8,128)S(1)}, u32[]{:S(2)}, u32[]{:S(2)}) collective-permute-start(f32[16,1024]{1,0:T(8,128)S(1)} %get-tuple-element.86.ya), channel_id=1, source_target_pairs={{0,1},{2,3},{4,5},{6,7},{1,0},{3,2},{5,4},{7,6},{8,9},{10,11},{12,... | collective-permute-start | bytes 196616 | tf_op jit(solution)/shard_map/ppermute | solution.py:442
  61.1 10.0 %collective-permute-start.9 = (f32[16,1024]{1,0:T(8,128)S(1)}, f32[16,1024]{1,0:T(8,128)S(1)}, u32[]{:S(2)}, u32[]{:S(2)}) collective-permute-start(f32[16,1024]{1,0:T(8,128)S(1)} %get-tuple-element.87.yb), channel_id=1, source_target_pairs={{1,2},{3,4},{5,6},{7,0},{2,1},{4,3},{6,5},{0,7},{9,10},{11,12},{13... | collective-permute-start | bytes 196616 | tf_op jit(solution)/shard_map/ppermute | solution.py:442
  62.2 9.0 %collective-permute-start.10 = (f32[32,1024]{1,0:T(8,128)S(1)}, f32[32,1024]{1,0:T(8,128)S(1)}, u32[]{:S(2)}, u32[]{:S(2)}) collective-permute-start(f32[32,1024]{1,0:T(8,128)S(1)} %get-tuple-element.84.xa), channel_id=1, source_target_pairs={{0,8},{16,24},{32,40},{48,56},{64,72},{80,88},{96,104},{112,120},{... | collective-permute-start | bytes 393224 | tf_op jit(solution)/shard_map/ppermute | solution.py:442
  62.2 9.9 %collective-permute-start.11 = (f32[32,1024]{1,0:T(8,128)S(1)}, f32[32,1024]{1,0:T(8,128)S(1)}, u32[]{:S(2)}, u32[]{:S(2)}) collective-permute-start(f32[32,1024]{1,0:T(8,128)S(1)} %get-tuple-element.85.xb), channel_id=1, source_target_pairs={{8,16},{24,32},{40,48},{56,64},{72,80},{88,96},{104,112},{120,128}... | collective-permute-start | bytes 393224 | tf_op jit(solution)/shard_map/ppermute | solution.py:442
  72.2 10.5 %collective-permute-start.12 = (f32[16,1024]{1,0:T(8,128)S(1)}, f32[16,1024]{1,0:T(8,128)S(1)}, u32[]{:S(2)}, u32[]{:S(2)}) collective-permute-start(f32[16,1024]{1,0:T(8,128)S(1)} %get-tuple-element.92.ya), channel_id=1, source_target_pairs={{0,1},{2,3},{4,5},{6,7},{1,0},{3,2},{5,4},{7,6},{8,9},{10,11},{12,... | collective-permute-start | bytes 196616 | tf_op jit(solution)/shard_map/ppermute | solution.py:442
  76.7 10.0 %collective-permute-start.13 = (f32[16,1024]{1,0:T(8,128)S(1)}, f32[16,1024]{1,0:T(8,128)S(1)}, u32[]{:S(2)}, u32[]{:S(2)}) collective-permute-start(f32[16,1024]{1,0:T(8,128)S(1)} %get-tuple-element.93.yb), channel_id=1, source_target_pairs={{1,2},{3,4},{5,6},{7,0},{2,1},{4,3},{6,5},{0,7},{9,10},{11,12},{13... | collective-permute-start | bytes 196616 | tf_op jit(solution)/shard_map/ppermute | solution.py:442
  78.7 7.9 %collective-permute-start.14 = (f32[32,1024]{1,0:T(8,128)S(1)}, f32[32,1024]{1,0:T(8,128)S(1)}, u32[]{:S(2)}, u32[]{:S(2)}) collective-permute-start(f32[32,1024]{1,0:T(8,128)S(1)} %get-tuple-element.90.xa), channel_id=1, source_target_pairs={{0,8},{16,24},{32,40},{48,56},{64,72},{80,88},{96,104},{112,120},{... | collective-permute-start | bytes 393224 | tf_op jit(solution)/shard_map/ppermute | solution.py:442
  78.7 10.1 %collective-permute-start.15 = (f32[32,1024]{1,0:T(8,128)S(1)}, f32[32,1024]{1,0:T(8,128)S(1)}, u32[]{:S(2)}, u32[]{:S(2)}) collective-permute-start(f32[32,1024]{1,0:T(8,128)S(1)} %get-tuple-element.91.xb), channel_id=1, source_target_pairs={{8,16},{24,32},{40,48},{56,64},{72,80},{88,96},{104,112},{120,128}... | collective-permute-start | bytes 393224 | tf_op jit(solution)/shard_map/ppermute | solution.py:442

commit v3 on v2

--- a/solution.py
+++ b/solution.py
@@ -436,14 +436,27 @@
           (lo_out, out_ref.at[inside, 0:YT]), (hi_out, out_ref.at[inside, CY - YT:CY])], sems)
 
 
-def swaps(axis, count, a, b):
-    one = [(i, i + 1) for i in range(0, count, 2)]
-    two = [(i, (i + 1) % count) for i in range(1, count, 2)]
-    return [lax.ppermute(v, axis, p + [(j, i) for i, j in p]) for v, p in ((a, one), (b, two))]
+def swap(value, partner):
+    there = [partner(gx, gy) for gx in range(NGX) for gy in range(NGY)]
+    return lax.ppermute(value, ("gx", "gy"), [(i, x * NGY + y) for i, (x, y) in enumerate(there)])
+
+
+def odd_x(gx, gy):
+    if gx in (0, NGX - 1):
+        return gx, gy ^ 2
+    return (gx + 1 if gx % 2 else gx - 1), gy
+
+
+def odd_y(gx, gy):
+    if gy in (0, NGY - 1):
+        return gx ^ 1, gy
+    return gx, (gy + 1 if gy % 2 else gy - 1)
 
 
 def exchange(xa, xb, ya, yb):
-    return near(*swaps("gx", NGX, xa, xb), *swaps("gy", NGY, ya, yb))
+    xa, xb = swap(xa, lambda gx, gy: (gx ^ 1, gy)), swap(xb, odd_x)
+    ya, yb = swap(ya, lambda gx, gy: (gx, gy ^ 1)), swap(yb, odd_y)
+    return near(xa, xb, ya, yb)
 
 
 def call(kernel, outs, specs, scratch=(), alias={}, mib=1, us=0.1, out_specs=None):

time: 90.3 us -> 85.5 us (0.947)
  the two profiles are of different devices: /device:TPU:8 before, /device:TPU:22 now
where the time goes in v3:
time: 85.5 us; the launch traced here: 85.3 us
  starting transfers between devices  42.5 us (50%)
  Pallas kernels  26.9 us (31%)
  waiting for transfers between devices  15.5 us (18%)
    ppermute x16, starting transfers between devices, swap(): lax.ppermute(value, ('gx', 'gy'), [(i, x * NGY + y) for i, (x, y) in enum...  31.6 us
    ppermute x16, waiting for transfers between devices, swap(): lax.ppermute(value, ('gx', 'gy'), [(i, x * NGY + y) for i, (x, y) in enum...  14.4 us
    all_to_all x1, starting transfers between devices, shards(): recv = lax.all_to_all(send, 'gy', 0, 0, tiled=True)  10.9 us
    pallas_call x1, Pallas kernels, shards(): call(coef_kernel, (pltpu.HBM((CX, CY, NZ), F32),) * 6 + (YY, YY, edge_x,...  9.4 us
    pallas_call x1, Pallas kernels, shards(): call(first_sweep_kernel, (SLAB, SLAB, SLAB, YY, SLAB, SLAB, SLAB), [HB] *...  3.79 us
    pallas_call x1, Pallas kernels, shards(): call(source_kernel, (SLAB,) * 3 + (edge_y,), [VM] + [HB] * 4 + [VM], [SLA...  3.67 us
    pallas_call x1, Pallas kernels, shards(): call(last_sweep_kernel, (SLAB, SLAB, YY, pltpu.HBM((CX, CY, NZ), F32)), [...  2.8 us
    pallas_call x1, Pallas kernels, shards(): call(start_kernel, (local(NGY * CHUNK, LW),) + (local(2 * CY, NZ),) * 2 +...  2.58 us
  transfers between devices with their start and end apart: 17, of which 7 were waited for; matrix products, arithmetic and copies ran while one was open for 0% of the time, Pallas kernels for 26%

profile of v3, /device:TPU:22, one launch (start us, length us, event | category | flops | bytes accessed | tf_op | source)
XLA Modules:
  0.0 85.3 jit_solution(2968793840100013535)
XLA Ops:
  0.0 0.0 copy-start
  0.0 2.6 %shard_map.82 = (f32[576,128]{1,0:T(8,128)}, f32[64,1024]{1,0:T(8,128)S(1)}, f32[64,1024]{1,0:T(8,128)S(1)}, f32[32,1024]{1,0:T(8,128)S(1)}, f32[32,1024]{1,0:T(8,128)S(1)}) custom-call(f32[16,32,1024]{2,1,0:T(8,128)} %t_hbm.3, s32[16,32,1024]{2,1,0:T(8,128)} %soil_hbm.3, f32[256,128]{1,0:T(8,128)} %loss_hbm.1, s32[1,256]{1,0:T(1,128)} %bitcast.5, ...), custom_call_target="tpu_custom_call" | custom-call | flops 100000000 | bytes 300000 | tf_op jit(solution)/shard_map/pallas_call | solution.py:485
  2.6 7.3 %collective-permute-start = (f32[32,1024]{1,0:T(8,128)S(1)}, f32[32,1024]{1,0:T(8,128)S(1)}, u32[]{:S(2)}, u32[]{:S(2)}) collective-permute-start(f32[32,1024]{1,0:T(8,128)S(1)} %get-tuple-element.51), channel_id=1, source_target_pairs={{0,1},{1,0},{2,3},{3,2},{4,5},{5,4},{6,7},{7,6},{8,9},{9,8},{10,11... | collective-permute-start | bytes 393224 | tf_op jit(solution)/shard_map/ppermute | solution.py:441
  9.9 0.0 collective-permute-start.1
  9.9 10.9 %all-to-all-start = ((f32[8,72,128]{2,1,0:T(8,128)}), f32[8,72,128]{2,1,0:T(8,128)S(1)}, u32[]{:S(2)}, u32[]{:S(2)}) async-start(f32[8,72,128]{2,1,0:T(8,128)} %bitcast.2), calls=%async_computation | async-start | bytes 589824 | tf_op jit(solution)/shard_map/all_to_all | solution.py:490
  20.8 0.0 collective-permute-start.2
  20.8 2.3 %collective-permute-start.3 = (f32[64,1024]{1,0:T(8,128)S(1)}, f32[64,1024]{1,0:T(8,128)S(1)}, u32[]{:S(2)}, u32[]{:S(2)}) collective-permute-start(f32[64,1024]{1,0:T(8,128)S(1)} %get-tuple-element.63), channel_id=1, source_target_pairs={{0,2},{1,3},{2,0},{3,1},{4,6},{5,7},{6,4},{7,5},{8,16},{9,17},{10,... | collective-permute-start | bytes 786440 | tf_op jit(solution)/shard_map/ppermute | solution.py:441
  23.1 0.0 collective-permute-done.hya
  23.1 0.0 collective-permute-done.1.hyb
  23.1 0.0 copy-done
  23.1 9.4 %shard_map.83 = (f32[16,32,1024]{2,1,0:T(8,128)}, f32[16,32,1024]{2,1,0:T(8,128)}, f32[16,32,1024]{2,1,0:T(8,128)}, f32[16,32,1024]{2,1,0:T(8,128)}, f32[16,32,1...) custom-call(f32[8]{0:T(128)S(1)} %copy-done, ...), custom_call_target="tpu_custom_call" | custom-call | flops 20000000000 | bytes 60000000 | tf_op jit(solution)/shard_map/pallas_call | solution.py:494
  32.5 1.1 %all-to-all-done = f32[8,72,128]{2,1,0:T(8,128)S(1)} async-done(((f32[8,72,128]{2,1,0:T(8,128)}), f32[8,72,128]{2,1,0:T(8,128)S(1)}, u32[]{:S(2)}, u32[]{:S(2)}) %all-to-all-start) | async-done | bytes 294944 | tf_op jit(solution)/shard_map/all_to_all | solution.py:490
  33.6 3.7 %shard_map.84 = (f32[16,32,1024]{2,1,0:T(8,128)S(1)}, f32[16,32,1024]{2,1,0:T(8,128)S(1)}, f32[16,32,1024]{2,1,0:T(8,128)S(1)}, f32[2,4,16,1024]{3,2,1,0:T(8,128)S(1)}) custom-call(f32[576,128]{1,0:T(8,128)S(1)} %bitcast.4, f32[128,1024]{1,0:T(8,128)} %inj_hbm.1, f32[16,32,1024]{2,1,0:T(8,128)} %get-tuple-element.57.rhs_hbm, ...), custom_call_target="tpu_custom_call", output_to_operand_aliasing={{3}: (5, {})} | custom-call | flops 100000000 | bytes 300000 | tf_op jit(solution)/shard_map/pallas_call | solution.py:499
  37.2 0.0 collective-permute-done.2.hxa
  37.2 0.0 collective-permute-done.3.hxb
  37.3 1.0 %shard_map.85 = (f32[32,1024]{1,0:T(8,128)S(1)}, f32[32,1024]{1,0:T(8,128)S(1)}, f32[16,1024]{1,0:T(8,128)S(1)}, f32[16,1024]{1,0:T(8,128)S(1)}, f32[2,32,1024]{...) custom-call(f32[8]{0:T(128)S(1)} %copy-done, ...), custom_call_target="tpu_custom_call" | custom-call | flops 100000000 | bytes 300000 | tf_op jit(solution)/shard_map/pallas_call | solution.py:502
  38.2 4.4 %collective-permute-start.4 = (f32[16,1024]{1,0:T(8,128)S(1)}, f32[16,1024]{1,0:T(8,128)S(1)}, u32[]{:S(2)}, u32[]{:S(2)}) collective-permute-start(f32[16,1024]{1,0:T(8,128)S(1)} %get-tuple-element.72.ya), channel_id=1, source_target_pairs={{0,1},{1,0},{2,3},{3,2},{4,5},{5,4},{6,7},{7,6},{8,9},{9,8},{10,11... | collective-permute-start | bytes 196616 | tf_op jit(solution)/shard_map/ppermute | solution.py:441
  42.7 1.8 %collective-permute-start.5 = (f32[16,1024]{1,0:T(8,128)S(1)}, f32[16,1024]{1,0:T(8,128)S(1)}, u32[]{:S(2)}, u32[]{:S(2)}) collective-permute-start(f32[16,1024]{1,0:T(8,128)S(1)} %get-tuple-element.73.yb), channel_id=1, source_target_pairs={{0,8},{1,2},{2,1},{3,4},{4,3},{5,6},{6,5},{7,15},{8,0},{9,10},{10,... | collective-permute-start | bytes 196616 | tf_op jit(solution)/shard_map/ppermute | solution.py:441
  44.4 0.0 collective-permute-start.6
  44.4 0.4 collective-permute-start.7
  44.8 3.8 %shard_map.86 = (f32[16,32,1024]{2,1,0:T(8,128)S(1)}, f32[16,32,1024]{2,1,0:T(8,128)S(1)}, f32[16,32,1024]{2,1,0:T(8,128)S(1)}, f32[2,16,1024]{2,1,0:T(8,128)S(1...) custom-call(f32[16,32,1024]{2,1,0:T(8,128)} %get-tuple-element.53.fx, ...), custom_call_target="tpu_custom_call", output_to_operand_aliasing={{0}: (10, {}), {1}: (11, {})} | custom-call | flops 100000000 | bytes 300000 | tf_op jit(solution)/shard_map/pallas_call | solution.py:507
  48.6 0.0 collective-permute-done.4.hya
  48.6 3.4 %collective-permute-done.5.hyb = f32[16,1024]{1,0:T(8,128)S(1)} collective-permute-done((f32[16,1024]{1,0:T(8,128)S(1)}, f32[16,1024]{1,0:T(8,128)S(1)}, u32[]{:S(2)}, u32[]{:S(2)}) %collective-permute-start.5) | collective-permute-done | bytes 65568 | tf_op jit(solution)/shard_map/ppermute | solution.py:441
  52.0 0.0 collective-permute-done.6.hxa
  52.0 1.8 %collective-permute-done.7.hxb = f32[32,1024]{1,0:T(8,128)S(1)} collective-permute-done((f32[32,1024]{1,0:T(8,128)S(1)}, f32[32,1024]{1,0:T(8,128)S(1)}, u32[]{:S(2)}, u32[]{:S(2)}) %collective-permute-start.7) | collective-permute-done | bytes 131104 | tf_op jit(solution)/shard_map/ppermute | solution.py:441
  53.8 0.1 shard_map.88
  53.9 4.0 %collective-permute-start.8 = (f32[16,1024]{1,0:T(8,128)S(1)}, f32[16,1024]{1,0:T(8,128)S(1)}, u32[]{:S(2)}, u32[]{:S(2)}) collective-permute-start(f32[16,1024]{1,0:T(8,128)S(1)} %get-tuple-element.86.ya), channel_id=1, source_target_pairs={{0,1},{1,0},{2,3},{3,2},{4,5},{5,4},{6,7},{7,6},{8,9},{9,8},{10,11... | collective-permute-start | bytes 196616 | tf_op jit(solution)/shard_map/ppermute | solution.py:441
  57.9 2.1 %collective-permute-start.9 = (f32[16,1024]{1,0:T(8,128)S(1)}, f32[16,1024]{1,0:T(8,128)S(1)}, u32[]{:S(2)}, u32[]{:S(2)}) collective-permute-start(f32[16,1024]{1,0:T(8,128)S(1)} %get-tuple-element.87.yb), channel_id=1, source_target_pairs={{0,8},{1,2},{2,1},{3,4},{4,3},{5,6},{6,5},{7,15},{8,0},{9,10},{10,... | collective-permute-start | bytes 196616 | tf_op jit(solution)/shard_map/ppermute | solution.py:441
  59.9 0.0 collective-permute-start.10
  59.9 1.4 %collective-permute-start.11 = (f32[32,1024]{1,0:T(8,128)S(1)}, f32[32,1024]{1,0:T(8,128)S(1)}, u32[]{:S(2)}, u32[]{:S(2)}) collective-permute-start(f32[32,1024]{1,0:T(8,128)S(1)} %get-tuple-element.85.xb), channel_id=1, source_target_pairs={{0,2},{1,3},{2,0},{3,1},{4,6},{5,7},{6,4},{7,5},{8,16},{9,17},{10,... | collective-permute-start | bytes 393224 | tf_op jit(solution)/shard_map/ppermute | solution.py:441
  61.4 2.3 %shard_map.89 = (f32[16,32,1024]{2,1,0:T(8,128)S(1)}, f32[16,32,1024]{2,1,0:T(8,128)S(1)}, f32[2,16,1024]{2,1,0:T(8,128)S(1)}) custom-call(f32[16,32,1024]{2,1,0:T(8,128)S(1)} %get-tuple-element.76.fx_ref, f32[16,32,1024]{2,1,0:T(8,128)S(1)} %get-tuple-element.77.fy_ref, ...), custom_call_target="tpu_custom_call", output_to_operand_aliasing={{0}: (9, {})} | custom-call | flops 100000000 | bytes 300000 | tf_op jit(solution)/shard_map/pallas_call | solution.py:512
  63.7 0.0 collective-permute-done.8.hya
  63.7 4.2 %collective-permute-done.9.hyb = f32[16,1024]{1,0:T(8,128)S(1)} collective-permute-done((f32[16,1024]{1,0:T(8,128)S(1)}, f32[16,1024]{1,0:T(8,128)S(1)}, u32[]{:S(2)}, u32[]{:S(2)}) %collective-permute-start.9) | collective-permute-done | bytes 65568 | tf_op jit(solution)/shard_map/ppermute | solution.py:441
  67.9 0.0 collective-permute-done.10.hxa
  67.9 0.6 collective-permute-done.11.hxb
  68.5 0.1 shard_map.91
  68.6 1.5 %collective-permute-start.12 = (f32[16,1024]{1,0:T(8,128)S(1)}, f32[16,1024]{1,0:T(8,128)S(1)}, u32[]{:S(2)}, u32[]{:S(2)}) collective-permute-start(f32[16,1024]{1,0:T(8,128)S(1)} %get-tuple-element.92.ya), channel_id=1, source_target_pairs={{0,1},{1,0},{2,3},{3,2},{4,5},{5,4},{6,7},{7,6},{8,9},{9,8},{10,11... | collective-permute-start | bytes 196616 | tf_op jit(solution)/shard_map/ppermute | solution.py:441
  70.1 4.4 %collective-permute-start.13 = (f32[16,1024]{1,0:T(8,128)S(1)}, f32[16,1024]{1,0:T(8,128)S(1)}, u32[]{:S(2)}, u32[]{:S(2)}) collective-permute-start(f32[16,1024]{1,0:T(8,128)S(1)} %get-tuple-element.93.yb), channel_id=1, source_target_pairs={{0,8},{1,2},{2,1},{3,4},{4,3},{5,6},{6,5},{7,15},{8,0},{9,10},{10,... | collective-permute-start | bytes 196616 | tf_op jit(solution)/shard_map/ppermute | solution.py:441
  74.5 0.0 collective-permute-start.14
  74.5 2.2 %collective-permute-start.15 = (f32[32,1024]{1,0:T(8,128)S(1)}, f32[32,1024]{1,0:T(8,128)S(1)}, u32[]{:S(2)}, u32[]{:S(2)}) collective-permute-start(f32[32,1024]{1,0:T(8,128)S(1)} %get-tuple-element.91.xb), channel_id=1, source_target_pairs={{0,2},{1,3},{2,0},{3,1},{4,6},{5,7},{6,4},{7,5},{8,16},{9,17},{10,... | collective-permute-start | bytes 393224 | tf_op jit(solution)/shard_map/ppermute | solution.py:441
  76.6 2.8 %shard_map.92 = (f32[16,32,1024]{2,1,0:T(8,128)S(1)}, f32[16,32,1024]{2,1,0:T(8,128)S(1)}, f32[2,16,1024]{2,1,0:T(8,128)S(1)}, f32[16,32,1024]{2,1,0:T(8,128)}) custom-call(f32[16,32,1024]{2,1,0:T(8,128)S(1)} %get-tuple-element.76.fx_ref, f32[16,32,1024]{2,1,0:T(8,128)S(1)} %get-tuple-element.77.fy_ref, ...), custom_call_target="tpu_custom_call", output_to_operand_aliasing={{0}: (9, {})} | custom-call | flops 100000000 | bytes 300000 | tf_op jit(solution)/shard_map/pallas_call | solution.py:515
  79.5 0.0 collective-permute-done.12.hya
  79.5 0.5 collective-permute-done.13.hyb
  80.0 0.0 collective-permute-done.14.hxa
  80.0 4.0 %collective-permute-done.15.hxb = f32[32,1024]{1,0:T(8,128)S(1)} collective-permute-done((f32[32,1024]{1,0:T(8,128)S(1)}, f32[32,1024]{1,0:T(8,128)S(1)}, u32[]{:S(2)}, u32[]{:S(2)}) %collective-permute-start.15) | collective-permute-done | bytes 131104 | tf_op jit(solution)/shard_map/ppermute | solution.py:441
  84.0 1.1 %shard_map.94 = f32[16,32,1024]{2,1,0:T(8,128)} custom-call(f32[16,32,1024]{2,1,0:T(8,128)S(1)} %get-tuple-element.94.tn_ref, f32[2,16,1024]{2,1,0:T(8,128)S(1)} %get-tuple-element.95.py_ref, f32[2,32,1024]{2,1,0:T(8,128)S(1)} %get-tuple-element.82.ax_ref, f32[2,16,1024]{2,1,0:T(8,128)S(1)} %shard_map.93.gy_ref, ...), custom_call_target="tpu_custom_call", output_to_operand_aliasing={{}: (6, {})} | custom-call | flops 100000000 | bytes 300000 | tf_op jit(solution)/shard_map/pallas_call | solution.py:523
  (3 shorter events, 0.1 us)
Async XLA Ops:
  0.0 23.1 %copy-start = (f32[8]{0:T(128)S(1)}, f32[8]{0:T(128)}, u32[]{:S(2)}) copy-start(f32[8]{0:T(128)} %table_ref.3) | copy-start | bytes 100
  2.6 20.5 %collective-permute-start = (f32[32,1024]{1,0:T(8,128)S(1)}, f32[32,1024]{1,0:T(8,128)S(1)}, u32[]{:S(2)}, u32[]{:S(2)}) collective-permute-start(f32[32,1024]{1,0:T(8,128)S(1)} %get-tuple-element.51), channel_id=1, source_target_pairs={{0,1},{1,0},{2,3},{3,2},{4,5},{5,4},{6,7},{7,6},{8,9},{9,8},{10,11... | collective-permute-start | bytes 393224 | tf_op jit(solution)/shard_map/ppermute | solution.py:441
  9.9 13.2 %collective-permute-start.1 = (f32[32,1024]{1,0:T(8,128)S(1)}, f32[32,1024]{1,0:T(8,128)S(1)}, u32[]{:S(2)}, u32[]{:S(2)}) collective-permute-start(f32[32,1024]{1,0:T(8,128)S(1)} %get-tuple-element.52), channel_id=1, source_target_pairs={{0,8},{1,2},{2,1},{3,4},{4,3},{5,6},{6,5},{7,15},{8,0},{9,10},{10,... | collective-permute-start | bytes 393224 | tf_op jit(solution)/shard_map/ppermute | solution.py:441
  9.9 23.7 %all-to-all-start = ((f32[8,72,128]{2,1,0:T(8,128)}), f32[8,72,128]{2,1,0:T(8,128)S(1)}, u32[]{:S(2)}, u32[]{:S(2)}) async-start(f32[8,72,128]{2,1,0:T(8,128)} %bitcast.2), calls=%async_computation | async-start | bytes 589824 | tf_op jit(solution)/shard_map/all_to_all | solution.py:490
  20.8 16.5 %collective-permute-start.2 = (f32[64,1024]{1,0:T(8,128)S(1)}, f32[64,1024]{1,0:T(8,128)S(1)}, u32[]{:S(2)}, u32[]{:S(2)}) collective-permute-start(f32[64,1024]{1,0:T(8,128)S(1)} %get-tuple-element.62), channel_id=1, source_target_pairs={{0,8},{1,9},{2,10},{3,11},{4,12},{5,13},{6,14},{7,15},{8,0},{9,1},... | collective-permute-start | bytes 786440 | tf_op jit(solution)/shard_map/ppermute | solution.py:441
  20.8 16.5 %collective-permute-start.3 = (f32[64,1024]{1,0:T(8,128)S(1)}, f32[64,1024]{1,0:T(8,128)S(1)}, u32[]{:S(2)}, u32[]{:S(2)}) collective-permute-start(f32[64,1024]{1,0:T(8,128)S(1)} %get-tuple-element.63), channel_id=1, source_target_pairs={{0,2},{1,3},{2,0},{3,1},{4,6},{5,7},{6,4},{7,5},{8,16},{9,17},{10,... | collective-permute-start | bytes 786440 | tf_op jit(solution)/shard_map/ppermute | solution.py:441
  38.2 10.3 %collective-permute-start.4 = (f32[16,1024]{1,0:T(8,128)S(1)}, f32[16,1024]{1,0:T(8,128)S(1)}, u32[]{:S(2)}, u32[]{:S(2)}) collective-permute-start(f32[16,1024]{1,0:T(8,128)S(1)} %get-tuple-element.72.ya), channel_id=1, source_target_pairs={{0,1},{1,0},{2,3},{3,2},{4,5},{5,4},{6,7},{7,6},{8,9},{9,8},{10,11... | collective-permute-start | bytes 196616 | tf_op jit(solution)/shard_map/ppermute | solution.py:441
  42.7 9.3 %collective-permute-start.5 = (f32[16,1024]{1,0:T(8,128)S(1)}, f32[16,1024]{1,0:T(8,128)S(1)}, u32[]{:S(2)}, u32[]{:S(2)}) collective-permute-start(f32[16,1024]{1,0:T(8,128)S(1)} %get-tuple-element.73.yb), channel_id=1, source_target_pairs={{0,8},{1,2},{2,1},{3,4},{4,3},{5,6},{6,5},{7,15},{8,0},{9,10},{10,... | collective-permute-start | bytes 196616 | tf_op jit(solution)/shard_map/ppermute | solution.py:441
  44.4 7.6 %collective-permute-start.6 = (f32[32,1024]{1,0:T(8,128)S(1)}, f32[32,1024]{1,0:T(8,128)S(1)}, u32[]{:S(2)}, u32[]{:S(2)}) collective-permute-start(f32[32,1024]{1,0:T(8,128)S(1)} %get-tuple-element.70.xa), channel_id=1, source_target_pairs={{0,8},{1,9},{2,10},{3,11},{4,12},{5,13},{6,14},{7,15},{8,0},{9,1},... | collective-permute-start | bytes 393224 | tf_op jit(solution)/shard_map/ppermute | solution.py:441
  44.4 9.4 %collective-permute-start.7 = (f32[32,1024]{1,0:T(8,128)S(1)}, f32[32,1024]{1,0:T(8,128)S(1)}, u32[]{:S(2)}, u32[]{:S(2)}) collective-permute-start(f32[32,1024]{1,0:T(8,128)S(1)} %get-tuple-element.71.xb), channel_id=1, source_target_pairs={{0,2},{1,3},{2,0},{3,1},{4,6},{5,7},{6,4},{7,5},{8,16},{9,17},{10,... | collective-permute-start | bytes 393224 | tf_op jit(solution)/shard_map/ppermute | solution.py:441
  53.9 9.8 %collective-permute-start.8 = (f32[16,1024]{1,0:T(8,128)S(1)}, f32[16,1024]{1,0:T(8,128)S(1)}, u32[]{:S(2)}, u32[]{:S(2)}) collective-permute-start(f32[16,1024]{1,0:T(8,128)S(1)} %get-tuple-element.86.ya), channel_id=1, source_target_pairs={{0,1},{1,0},{2,3},{3,2},{4,5},{5,4},{6,7},{7,6},{8,9},{9,8},{10,11... | collective-permute-start | bytes 196616 | tf_op jit(solution)/shard_map/ppermute | solution.py:441
  57.9 10.0 %collective-permute-start.9 = (f32[16,1024]{1,0:T(8,128)S(1)}, f32[16,1024]{1,0:T(8,128)S(1)}, u32[]{:S(2)}, u32[]{:S(2)}) collective-permute-start(f32[16,1024]{1,0:T(8,128)S(1)} %get-tuple-element.87.yb), channel_id=1, source_target_pairs={{0,8},{1,2},{2,1},{3,4},{4,3},{5,6},{6,5},{7,15},{8,0},{9,10},{10,... | collective-permute-start | bytes 196616 | tf_op jit(solution)/shard_map/ppermute | solution.py:441
  59.9 8.0 %collective-permute-start.10 = (f32[32,1024]{1,0:T(8,128)S(1)}, f32[32,1024]{1,0:T(8,128)S(1)}, u32[]{:S(2)}, u32[]{:S(2)}) collective-permute-start(f32[32,1024]{1,0:T(8,128)S(1)} %get-tuple-element.84.xa), channel_id=1, source_target_pairs={{0,8},{1,9},{2,10},{3,11},{4,12},{5,13},{6,14},{7,15},{8,0},{9,1},... | collective-permute-start | bytes 393224 | tf_op jit(solution)/shard_map/ppermute | solution.py:441
  59.9 8.6 %collective-permute-start.11 = (f32[32,1024]{1,0:T(8,128)S(1)}, f32[32,1024]{1,0:T(8,128)S(1)}, u32[]{:S(2)}, u32[]{:S(2)}) collective-permute-start(f32[32,1024]{1,0:T(8,128)S(1)} %get-tuple-element.85.xb), channel_id=1, source_target_pairs={{0,2},{1,3},{2,0},{3,1},{4,6},{5,7},{6,4},{7,5},{8,16},{9,17},{10,... | collective-permute-start | bytes 393224 | tf_op jit(solution)/shard_map/ppermute | solution.py:441
  68.6 10.8 %collective-permute-start.12 = (f32[16,1024]{1,0:T(8,128)S(1)}, f32[16,1024]{1,0:T(8,128)S(1)}, u32[]{:S(2)}, u32[]{:S(2)}) collective-permute-start(f32[16,1024]{1,0:T(8,128)S(1)} %get-tuple-element.92.ya), channel_id=1, source_target_pairs={{0,1},{1,0},{2,3},{3,2},{4,5},{5,4},{6,7},{7,6},{8,9},{9,8},{10,11... | collective-permute-start | bytes 196616 | tf_op jit(solution)/shard_map/ppermute | solution.py:441
  70.1 9.8 %collective-permute-start.13 = (f32[16,1024]{1,0:T(8,128)S(1)}, f32[16,1024]{1,0:T(8,128)S(1)}, u32[]{:S(2)}, u32[]{:S(2)}) collective-permute-start(f32[16,1024]{1,0:T(8,128)S(1)} %get-tuple-element.93.yb), channel_id=1, source_target_pairs={{0,8},{1,2},{2,1},{3,4},{4,3},{5,6},{6,5},{7,15},{8,0},{9,10},{10,... | collective-permute-start | bytes 196616 | tf_op jit(solution)/shard_map/ppermute | solution.py:441
  74.5 5.5 %collective-permute-start.14 = (f32[32,1024]{1,0:T(8,128)S(1)}, f32[32,1024]{1,0:T(8,128)S(1)}, u32[]{:S(2)}, u32[]{:S(2)}) collective-permute-start(f32[32,1024]{1,0:T(8,128)S(1)} %get-tuple-element.90.xa), channel_id=1, source_target_pairs={{0,8},{1,9},{2,10},{3,11},{4,12},{5,13},{6,14},{7,15},{8,0},{9,1},... | collective-permute-start | bytes 393224 | tf_op jit(solution)/shard_map/ppermute | solution.py:441
  74.5 9.5 %collective-permute-start.15 = (f32[32,1024]{1,0:T(8,128)S(1)}, f32[32,1024]{1,0:T(8,128)S(1)}, u32[]{:S(2)}, u32[]{:S(2)}) collective-permute-start(f32[32,1024]{1,0:T(8,128)S(1)} %get-tuple-element.91.xb), channel_id=1, source_target_pairs={{0,2},{1,3},{2,0},{3,1},{4,6},{5,7},{6,4},{7,5},{8,16},{9,17},{10,... | collective-permute-start | bytes 393224 | tf_op jit(solution)/shard_map/ppermute | solution.py:441

commit v4 on v3

--- a/solution.py
+++ b/solution.py
@@ -15,7 +15,7 @@
 CHUNK = CAP + 8
 YT = 8
 NT = CY // YT
-PARTS = 4
+PARTS = 8
 F32, BF16 = jnp.float32, jnp.bfloat16
 HIGH = lax.Precision.HIGHEST
 VM = pl.BlockSpec(memory_space=pltpu.VMEM)
@@ -145,7 +145,7 @@
     return mid, up, down
 
 
-def coef_kernel(table_ref, hya, hyb, t_hbm, cap_hbm, soil_hbm, *refs):
+def coef_kernel(table_ref, hyb, hya, t_hbm, cap_hbm, soil_hbm, *refs):
     outs, (more_ref, halo_ref, ex_ref, ey_ref, half_ref, t_ref, cap, soil), made, (in_sems, out_sems) = (
         refs[:6], refs[6:14], refs[14:20], refs[20:])
     fx_ref, fy_ref, fz_ref, rhs_ref, tn_ref, w_ref = made
@@ -252,16 +252,15 @@
         copy.wait()
 
 
-def source_kernel(recv_ref, inj_hbm, rhs_hbm, tn_hbm, w_hbm, ey_in, rhs_ref, tn_ref, w_ref, ey_ref, source, inj, sems):
-    pairs = [(inj_hbm, inj), (rhs_hbm, rhs_ref), (tn_hbm, tn_ref), (w_hbm, w_ref)]
-    copies = [pltpu.make_async_copy(src, dst, sems.at[k]) for k, (src, dst) in enumerate(pairs)]
-    for copy in copies:
-        copy.start()
-    copies[0].wait()
-    add_source(recv_ref, inj, source)
-    copies[1].wait()
-    copies[2].wait()
-    copies[3].wait()
+def source_kernel(recv_ref, inj_ref, rhs_hbm, tn_hbm, w_hbm, ey_in, rhs_ref, tn_ref, w_ref, ey_ref, source, sems):
+    step = CX // 4
+    pairs = ((rhs_hbm, rhs_ref), (w_hbm, w_ref), (tn_hbm, tn_ref))
+    copies = [[pltpu.make_async_copy(src.at[pl.ds(part * step, step)], dst.at[pl.ds(part * step, step)], sems.at[k, part])
+               for k, (src, dst) in enumerate(pairs)] for part in range(4)]
+    for part in copies:
+        for copy in part:
+            copy.start()
+    add_source(recv_ref, inj_ref, source)
 
     def plane(x, edge):
         for yt in range(NT):
@@ -276,8 +275,12 @@
         plane(x, False)
         return carry
 
-    plane(0, True)
-    lax.fori_loop(1, CX - 1, inner, 0)
+    for part in range(4):
+        for copy in copies[part]:
+            copy.wait()
+        if part == 0:
+            plane(0, True)
+        lax.fori_loop(max(1, part * step), min(CX - 1, (part + 1) * step), inner, 0)
     plane(CX - 1, True)
 
 
@@ -293,7 +296,7 @@
             yhi + at_row(ys, 0, xlo[CY - 1:CY]) + at_row(ys, CX - 1, xhi[CY - 1:CY]))
 
 
-def fix_kernel(table_ref, hxa, hxb, my_ref, ty_ref, w_ref, tn_ref, ex_ref, ey_ref,
+def fix_kernel(table_ref, hxb, hxa, my_ref, ty_ref, w_ref, tn_ref, ex_ref, ey_ref,
                xa, xb, ya, yb, wx_ref, wy_ref, ax_ref, ay_ref):
     table = [0.5 * table_ref[k] for k in range(NCLS)]
     gx, gy = lax.axis_index("gx"), lax.axis_index("gy")
@@ -316,20 +319,20 @@
         ax_ref[k], ay_ref[k] = w[k] * face[k], w[2 + k] * face[2 + k]
 
 
-def y_term_kernel(ay_ref, hya, hyb, gy_ref):
+def y_term_kernel(ay_ref, hyb, hya, gy_ref):
     lo, hi = split(hya[...], hyb[...], even("gy"))
     gy_ref[0] = ay_ref[0] * lo
     gy_ref[1] = ay_ref[1] * hi
 
 
-def faces_of(tn_ref, py_ref, ax_ref, gy_ref, hxa, hxb):
+def faces_of(tn_ref, py_ref, ax_ref, gy_ref, hxb, hxa):
     lo, hi = split(hxa[...], hxb[...], even("gx"))
     terms = with_corners(ax_ref[0] * lo, ax_ref[1] * hi, gy_ref[0], gy_ref[1])
     return [a + b for a, b in zip(terms, (tn_ref[0], tn_ref[CX - 1], py_ref[0], py_ref[1]))]
 
 
-def edge_kernel(tn_ref, py_ref, ax_ref, gy_ref, hxa, hxb, xa, xb, ya, yb):
-    new = faces_of(tn_ref, py_ref, ax_ref, gy_ref, hxa, hxb)
+def edge_kernel(tn_ref, py_ref, ax_ref, gy_ref, hxb, hxa, xa, xb, ya, yb):
+    new = faces_of(tn_ref, py_ref, ax_ref, gy_ref, hxb, hxa)
     xa[...], xb[...] = split(new[0], new[1], even("gx"))
     ya[...], yb[...] = split(new[2], new[3], even("gy"))
 
@@ -423,8 +426,8 @@
         copy.wait()
 
 
-def finish_kernel(tn_ref, py_ref, ax_ref, gy_ref, hxa, hxb, out_in, out_ref, x_out, lo_out, hi_out, sems):
-    xlo, xhi, ylo, yhi = faces_of(tn_ref, py_ref, ax_ref, gy_ref, hxa, hxb)
+def finish_kernel(tn_ref, py_ref, ax_ref, gy_ref, hxb, hxa, out_in, out_ref, x_out, lo_out, hi_out, sems):
+    xlo, xhi, ylo, yhi = faces_of(tn_ref, py_ref, ax_ref, gy_ref, hxb, hxa)
     x_out[0] = xlo
     x_out[1] = xhi
     row = lax.broadcasted_iota(jnp.int32, (YT, NZ), 0)
@@ -454,8 +457,8 @@
 
 
 def exchange(xa, xb, ya, yb):
-    xa, xb = swap(xa, lambda gx, gy: (gx ^ 1, gy)), swap(xb, odd_x)
-    ya, yb = swap(ya, lambda gx, gy: (gx, gy ^ 1)), swap(yb, odd_y)
+    xb, xa = swap(xb, odd_x), swap(xa, lambda gx, gy: (gx ^ 1, gy))
+    yb, ya = swap(yb, odd_y), swap(ya, lambda gx, gy: (gx, gy ^ 1))
     return near(xa, xb, ya, yb)
 
 
@@ -495,12 +498,12 @@
         coef_kernel, (pltpu.HBM((CX, CY, NZ), F32),) * 6 + (YY, YY, edge_x, edge_y), [SM] + [VM] * 2 + [HB] * 3,
         [SLAB, SLAB, SLAB, local(CX, CY, NZ, dtype=I32)] + [SLAB] * 6 + [DMA((3, PARTS)), DMA((6, PARTS))],
         mib=24, us=FIXY, out_specs=[HB] * 6 + [VM] * 4)(
-        cond_table, hya, hyb, *far(temp_old, capacity, soil_class))
+        cond_table, hyb, hya, *far(temp_old, capacity, soil_class))
     rhs, new, w, ey = call(
-        source_kernel, (SLAB,) * 3 + (edge_y,), [VM] + [HB] * 4 + [VM], [SLAB, local(LW, NZ), DMA((4,))],
-        alias={5: 3}, mib=8, us=PREP)(*near(recv), *far(injection, *stored[3:]), *near(ey))
+        source_kernel, (SLAB,) * 3 + (edge_y,), [VM] * 2 + [HB] * 3 + [VM], [SLAB, DMA((3, 4))],
+        alias={5: 3}, mib=8, us=PREP)(*near(recv, injection), *far(*stored[3:]), *near(ey))
     *faces, wx, wy, ax, ay = call(fix_kernel, FACES + (XX, YY, XX, YY), [SM] + [VM] * 8, mib=2)(
-        cond_table, hxa, hxb, *near(my, ty, w, new, ex, ey))
+        cond_table, hxb, hxa, *near(my, ty, w, new, ex, ey))
     for number in range(1, SWEEPS):
         halo = exchange(*faces)
         if number == 1:
@@ -516,8 +519,8 @@
                 last_sweep_kernel, (SLAB, SLAB, YY, pltpu.HBM((CX, CY, NZ), F32)), [VM] * 10, [DMA((4,))],
                 alias={9: 0}, mib=2, out_specs=[VM] * 3 + [HB])(*coefs, *near(w, *faces, new))
         hxa, hxb, hya, hyb = halo
-        (gy,) = call(y_term_kernel, (YY,), [VM] * 3, us=8.0)(*near(ay), hya, hyb)
-        args = near(new, py, ax, gy) + [hxa, hxb]
+        (gy,) = call(y_term_kernel, (YY,), [VM] * 3, us=8.0)(*near(ay), hyb, hya)
+        args = near(new, py, ax, gy) + [hxb, hxa]
         if number < SWEEPS - 1:
             faces = call(edge_kernel, FACES, [VM] * 6, mib=2)(*args)
     return call(finish_kernel, (pltpu.HBM((CX, CY, NZ), F32),), [VM] * 6 + [HB],

time: 85.5 us -> 83.5 us (0.977)
  the two profiles are of different devices: /device:TPU:22 before, /device:TPU:14 now
where the time goes in v4:
time: 83.5 us; the launch traced here: 83.3 us
  starting transfers between devices  41.7 us (50%)
  Pallas kernels  26.2 us (31%)
  waiting for transfers between devices  15 us (18%)
    ppermute x16, starting transfers between devices, swap(): lax.ppermute(value, ('gx', 'gy'), [(i, x * NGY + y) for i, (x, y) in enum...  31.5 us
    ppermute x16, waiting for transfers between devices, swap(): lax.ppermute(value, ('gx', 'gy'), [(i, x * NGY + y) for i, (x, y) in enum...  12.7 us
    all_to_all x1, starting transfers between devices, shards(): recv = lax.all_to_all(send, 'gy', 0, 0, tiled=True)  10.2 us
    pallas_call x1, Pallas kernels, shards(): call(coef_kernel, (pltpu.HBM((CX, CY, NZ), F32),) * 6 + (YY, YY, edge_x,...  9.39 us
    pallas_call x1, Pallas kernels, shards(): call(first_sweep_kernel, (SLAB, SLAB, SLAB, YY, SLAB, SLAB, SLAB), [HB] *...  3.57 us
    pallas_call x1, Pallas kernels, shards(): call(source_kernel, (SLAB,) * 3 + (edge_y,), [VM] * 2 + [HB] * 3 + [VM],...  3.23 us
    pallas_call x1, Pallas kernels, shards(): call(last_sweep_kernel, (SLAB, SLAB, YY, pltpu.HBM((CX, CY, NZ), F32)), [...  2.8 us
    pallas_call x1, Pallas kernels, shards(): call(start_kernel, (local(NGY * CHUNK, LW),) + (local(2 * CY, NZ),) * 2 +...  2.59 us
  transfers between devices with their start and end apart: 17, of which 8 were waited for; matrix products, arithmetic and copies ran while one was open for 0% of the time, Pallas kernels for 26%

profile of v4, /device:TPU:14, one launch (start us, length us, event | category | flops | bytes accessed | tf_op | source)
XLA Modules:
  0.0 83.3 jit_solution(3770425167762343481)
XLA Ops:
  0.0 0.0 copy-start.1
  0.0 2.6 %shard_map.82 = (f32[576,128]{1,0:T(8,128)}, f32[64,1024]{1,0:T(8,128)S(1)}, f32[64,1024]{1,0:T(8,128)S(1)}, f32[32,1024]{1,0:T(8,128)S(1)}, f32[32,1024]{1,0:T(8,128)S(1)}) custom-call(f32[16,32,1024]{2,1,0:T(8,128)} %t_hbm.3, s32[16,32,1024]{2,1,0:T(8,128)} %soil_hbm.3, f32[256,128]{1,0:T(8,128)} %loss_hbm.1, s32[1,256]{1,0:T(1,128)} %bitcast.5, ...), custom_call_target="tpu_custom_call" | custom-call | flops 100000000 | bytes 300000 | tf_op jit(solution)/shard_map/pallas_call | solution.py:488
  2.6 7.2 %collective-permute-start = (f32[32,1024]{1,0:T(8,128)S(1)}, f32[32,1024]{1,0:T(8,128)S(1)}, u32[]{:S(2)}, u32[]{:S(2)}) collective-permute-start(f32[32,1024]{1,0:T(8,128)S(1)} %get-tuple-element.51), channel_id=1, source_target_pairs={{0,8},{1,2},{2,1},{3,4},{4,3},{5,6},{6,5},{7,15},{8,0},{9,10},{10,... | collective-permute-start | bytes 393224 | tf_op jit(solution)/shard_map/ppermute | solution.py:444
  9.8 0.2 collective-permute-start.1
  10.0 10.2 %all-to-all-start = ((f32[8,72,128]{2,1,0:T(8,128)}), f32[8,72,128]{2,1,0:T(8,128)S(1)}, u32[]{:S(2)}, u32[]{:S(2)}) async-start(f32[8,72,128]{2,1,0:T(8,128)} %bitcast.2), calls=%async_computation | async-start | bytes 589824 | tf_op jit(solution)/shard_map/all_to_all | solution.py:493
  20.2 0.5 collective-permute-start.2
  20.7 0.0 copy-start
  20.7 0.6 collective-permute-start.3
  21.3 0.0 collective-permute-done.hyb
  21.3 0.0 collective-permute-done.1.hya
  21.3 0.0 copy-done.1
  21.3 9.4 %shard_map.83 = (f32[16,32,1024]{2,1,0:T(8,128)}, f32[16,32,1024]{2,1,0:T(8,128)}, f32[16,32,1024]{2,1,0:T(8,128)}, f32[16,32,1024]{2,1,0:T(8,128)}, f32[16,32,1...) custom-call(f32[8]{0:T(128)S(1)} %copy-done.1, ...), custom_call_target="tpu_custom_call" | custom-call | flops 20000000000 | bytes 60000000 | tf_op jit(solution)/shard_map/pallas_call | solution.py:497
  30.7 2.4 %all-to-all-done = f32[8,72,128]{2,1,0:T(8,128)S(1)} async-done(((f32[8,72,128]{2,1,0:T(8,128)}), f32[8,72,128]{2,1,0:T(8,128)S(1)}, u32[]{:S(2)}, u32[]{:S(2)}) %all-to-all-start) | async-done | bytes 294944 | tf_op jit(solution)/shard_map/all_to_all | solution.py:493
  33.1 0.0 copy-done
  33.1 3.2 %shard_map.84 = (f32[16,32,1024]{2,1,0:T(8,128)S(1)}, f32[16,32,1024]{2,1,0:T(8,128)S(1)}, f32[16,32,1024]{2,1,0:T(8,128)S(1)}, f32[2,4,16,1024]{3,2,1,0:T(8,128)S(1)}) custom-call(f32[576,128]{1,0:T(8,128)S(1)} %bitcast.4, f32[128,1024]{1,0:T(8,128)S(1)} %copy-done, f32[16,32,1024]{2,1,0:T(8,128)} %get-tuple-element.57.rhs_hbm, ...), custom_call_target="tpu_custom_call", output_to_operand_aliasing={{3}: (5, {})} | custom-call | flops 100000000 | bytes 300000 | tf_op jit(solution)/shard_map/pallas_call | solution.py:502
  36.3 0.0 collective-permute-done.2.hxb
  36.3 0.0 collective-permute-done.3.hxa
  36.3 1.0 %shard_map.85 = (f32[32,1024]{1,0:T(8,128)S(1)}, f32[32,1024]{1,0:T(8,128)S(1)}, f32[16,1024]{1,0:T(8,128)S(1)}, f32[16,1024]{1,0:T(8,128)S(1)}, f32[2,32,1024]{...) custom-call(f32[8]{0:T(128)S(1)} %copy-done.1, ...), custom_call_target="tpu_custom_call" | custom-call | flops 100000000 | bytes 300000 | tf_op jit(solution)/shard_map/pallas_call | solution.py:505
  37.3 3.1 %collective-permute-start.4 = (f32[16,1024]{1,0:T(8,128)S(1)}, f32[16,1024]{1,0:T(8,128)S(1)}, u32[]{:S(2)}, u32[]{:S(2)}) collective-permute-start(f32[16,1024]{1,0:T(8,128)S(1)} %get-tuple-element.73.yb), channel_id=1, source_target_pairs={{0,8},{1,2},{2,1},{3,4},{4,3},{5,6},{6,5},{7,15},{8,0},{9,10},{10,... | collective-permute-start | bytes 196616 | tf_op jit(solution)/shard_map/ppermute | solution.py:444
  40.4 4.0 %collective-permute-start.5 = (f32[16,1024]{1,0:T(8,128)S(1)}, f32[16,1024]{1,0:T(8,128)S(1)}, u32[]{:S(2)}, u32[]{:S(2)}) collective-permute-start(f32[16,1024]{1,0:T(8,128)S(1)} %get-tuple-element.72.ya), channel_id=1, source_target_pairs={{0,1},{1,0},{2,3},{3,2},{4,5},{5,4},{6,7},{7,6},{8,9},{9,8},{10,11... | collective-permute-start | bytes 196616 | tf_op jit(solution)/shard_map/ppermute | solution.py:444
  44.4 0.8 collective-permute-start.6
  45.2 0.0 collective-permute-start.7
  45.2 3.6 %shard_map.86 = (f32[16,32,1024]{2,1,0:T(8,128)S(1)}, f32[16,32,1024]{2,1,0:T(8,128)S(1)}, f32[16,32,1024]{2,1,0:T(8,128)S(1)}, f32[2,16,1024]{2,1,0:T(8,128)S(1...) custom-call(f32[16,32,1024]{2,1,0:T(8,128)} %get-tuple-element.53.fx, ...), custom_call_target="tpu_custom_call", output_to_operand_aliasing={{0}: (10, {}), {1}: (11, {})} | custom-call | flops 100000000 | bytes 300000 | tf_op jit(solution)/shard_map/pallas_call | solution.py:510
  48.8 0.0 collective-permute-done.4.hyb
  48.8 1.5 %collective-permute-done.5.hya = f32[16,1024]{1,0:T(8,128)S(1)} collective-permute-done((f32[16,1024]{1,0:T(8,128)S(1)}, f32[16,1024]{1,0:T(8,128)S(1)}, u32[]{:S(2)}, u32[]{:S(2)}) %collective-permute-start.5) | collective-permute-done | bytes 65568 | tf_op jit(solution)/shard_map/ppermute | solution.py:444
  50.3 2.4 %collective-permute-done.6.hxb = f32[32,1024]{1,0:T(8,128)S(1)} collective-permute-done((f32[32,1024]{1,0:T(8,128)S(1)}, f32[32,1024]{1,0:T(8,128)S(1)}, u32[]{:S(2)}, u32[]{:S(2)}) %collective-permute-start.6) | collective-permute-done | bytes 131104 | tf_op jit(solution)/shard_map/ppermute | solution.py:444
  52.7 0.0 collective-permute-done.7.hxa
  52.7 0.1 shard_map.88
  52.8 1.6 %collective-permute-start.8 = (f32[16,1024]{1,0:T(8,128)S(1)}, f32[16,1024]{1,0:T(8,128)S(1)}, u32[]{:S(2)}, u32[]{:S(2)}) collective-permute-start(f32[16,1024]{1,0:T(8,128)S(1)} %get-tuple-element.87.yb), channel_id=1, source_target_pairs={{0,8},{1,2},{2,1},{3,4},{4,3},{5,6},{6,5},{7,15},{8,0},{9,10},{10,... | collective-permute-start | bytes 196616 | tf_op jit(solution)/shard_map/ppermute | solution.py:444
  54.4 5.3 %collective-permute-start.9 = (f32[16,1024]{1,0:T(8,128)S(1)}, f32[16,1024]{1,0:T(8,128)S(1)}, u32[]{:S(2)}, u32[]{:S(2)}) collective-permute-start(f32[16,1024]{1,0:T(8,128)S(1)} %get-tuple-element.86.ya), channel_id=1, source_target_pairs={{0,1},{1,0},{2,3},{3,2},{4,5},{5,4},{6,7},{7,6},{8,9},{9,8},{10,11... | collective-permute-start | bytes 196616 | tf_op jit(solution)/shard_map/ppermute | solution.py:444
  59.7 0.7 collective-permute-start.10
  60.4 0.0 collective-permute-start.11
  60.4 2.3 %shard_map.89 = (f32[16,32,1024]{2,1,0:T(8,128)S(1)}, f32[16,32,1024]{2,1,0:T(8,128)S(1)}, f32[2,16,1024]{2,1,0:T(8,128)S(1)}) custom-call(f32[16,32,1024]{2,1,0:T(8,128)S(1)} %get-tuple-element.76.fx_ref, f32[16,32,1024]{2,1,0:T(8,128)S(1)} %get-tuple-element.77.fy_ref, ...), custom_call_target="tpu_custom_call", output_to_operand_aliasing={{0}: (9, {})} | custom-call | flops 100000000 | bytes 300000 | tf_op jit(solution)/shard_map/pallas_call | solution.py:515
  62.7 0.1 collective-permute-done.8.hyb
  62.8 2.7 %collective-permute-done.9.hya = f32[16,1024]{1,0:T(8,128)S(1)} collective-permute-done((f32[16,1024]{1,0:T(8,128)S(1)}, f32[16,1024]{1,0:T(8,128)S(1)}, u32[]{:S(2)}, u32[]{:S(2)}) %collective-permute-start.9) | collective-permute-done | bytes 65568 | tf_op jit(solution)/shard_map/ppermute | solution.py:444
  65.5 2.0 %collective-permute-done.10.hxb = f32[32,1024]{1,0:T(8,128)S(1)} collective-permute-done((f32[32,1024]{1,0:T(8,128)S(1)}, f32[32,1024]{1,0:T(8,128)S(1)}, u32[]{:S(2)}, u32[]{:S(2)}) %collective-permute-start.10) | collective-permute-done | bytes 131104 | tf_op jit(solution)/shard_map/ppermute | solution.py:444
  67.5 0.0 collective-permute-done.11.hxa
  67.5 0.1 shard_map.91
  67.6 1.3 %collective-permute-start.12 = (f32[16,1024]{1,0:T(8,128)S(1)}, f32[16,1024]{1,0:T(8,128)S(1)}, u32[]{:S(2)}, u32[]{:S(2)}) collective-permute-start(f32[16,1024]{1,0:T(8,128)S(1)} %get-tuple-element.93.yb), channel_id=1, source_target_pairs={{0,8},{1,2},{2,1},{3,4},{4,3},{5,6},{6,5},{7,15},{8,0},{9,10},{10,... | collective-permute-start | bytes 196616 | tf_op jit(solution)/shard_map/ppermute | solution.py:444
  68.9 5.0 %collective-permute-start.13 = (f32[16,1024]{1,0:T(8,128)S(1)}, f32[16,1024]{1,0:T(8,128)S(1)}, u32[]{:S(2)}, u32[]{:S(2)}) collective-permute-start(f32[16,1024]{1,0:T(8,128)S(1)} %get-tuple-element.92.ya), channel_id=1, source_target_pairs={{0,1},{1,0},{2,3},{3,2},{4,5},{5,4},{6,7},{7,6},{8,9},{9,8},{10,11... | collective-permute-start | bytes 196616 | tf_op jit(solution)/shard_map/ppermute | solution.py:444
  73.9 1.2 %collective-permute-start.14 = (f32[32,1024]{1,0:T(8,128)S(1)}, f32[32,1024]{1,0:T(8,128)S(1)}, u32[]{:S(2)}, u32[]{:S(2)}) collective-permute-start(f32[32,1024]{1,0:T(8,128)S(1)} %get-tuple-element.91.xb), channel_id=1, source_target_pairs={{0,2},{1,3},{2,0},{3,1},{4,6},{5,7},{6,4},{7,5},{8,16},{9,17},{10,... | collective-permute-start | bytes 393224 | tf_op jit(solution)/shard_map/ppermute | solution.py:444
  75.1 0.0 collective-permute-start.15
  75.1 2.8 %shard_map.92 = (f32[16,32,1024]{2,1,0:T(8,128)S(1)}, f32[16,32,1024]{2,1,0:T(8,128)S(1)}, f32[2,16,1024]{2,1,0:T(8,128)S(1)}, f32[16,32,1024]{2,1,0:T(8,128)}) custom-call(f32[16,32,1024]{2,1,0:T(8,128)S(1)} %get-tuple-element.76.fx_ref, f32[16,32,1024]{2,1,0:T(8,128)S(1)} %get-tuple-element.77.fy_ref, ...), custom_call_target="tpu_custom_call", output_to_operand_aliasing={{0}: (9, {})} | custom-call | flops 100000000 | bytes 300000 | tf_op jit(solution)/shard_map/pallas_call | solution.py:518
  78.0 0.0 collective-permute-done.12.hyb
  78.0 0.5 collective-permute-done.13.hya
  78.5 3.5 %collective-permute-done.14.hxb = f32[32,1024]{1,0:T(8,128)S(1)} collective-permute-done((f32[32,1024]{1,0:T(8,128)S(1)}, f32[32,1024]{1,0:T(8,128)S(1)}, u32[]{:S(2)}, u32[]{:S(2)}) %collective-permute-start.14) | collective-permute-done | bytes 131104 | tf_op jit(solution)/shard_map/ppermute | solution.py:444
  82.0 0.0 collective-permute-done.15.hxa
  82.0 1.1 %shard_map.94 = f32[16,32,1024]{2,1,0:T(8,128)} custom-call(f32[16,32,1024]{2,1,0:T(8,128)S(1)} %get-tuple-element.94.tn_ref, f32[2,16,1024]{2,1,0:T(8,128)S(1)} %get-tuple-element.95.py_ref, f32[2,32,1024]{2,1,0:T(8,128)S(1)} %get-tuple-element.82.ax_ref, f32[2,16,1024]{2,1,0:T(8,128)S(1)} %shard_map.93.gy_ref, ...), custom_call_target="tpu_custom_call", output_to_operand_aliasing={{}: (6, {})} | custom-call | flops 100000000 | bytes 300000 | tf_op jit(solution)/shard_map/pallas_call | solution.py:526
  (3 shorter events, 0.1 us)
Async XLA Ops:
  0.0 21.3 %copy-start.1 = (f32[8]{0:T(128)S(1)}, f32[8]{0:T(128)}, u32[]{:S(2)}) copy-start(f32[8]{0:T(128)} %table_ref.3) | copy-start | bytes 100
  2.6 18.7 %collective-permute-start = (f32[32,1024]{1,0:T(8,128)S(1)}, f32[32,1024]{1,0:T(8,128)S(1)}, u32[]{:S(2)}, u32[]{:S(2)}) collective-permute-start(f32[32,1024]{1,0:T(8,128)S(1)} %get-tuple-element.51), channel_id=1, source_target_pairs={{0,8},{1,2},{2,1},{3,4},{4,3},{5,6},{6,5},{7,15},{8,0},{9,10},{10,... | collective-permute-start | bytes 393224 | tf_op jit(solution)/shard_map/ppermute | solution.py:444
  9.8 11.5 %collective-permute-start.1 = (f32[32,1024]{1,0:T(8,128)S(1)}, f32[32,1024]{1,0:T(8,128)S(1)}, u32[]{:S(2)}, u32[]{:S(2)}) collective-permute-start(f32[32,1024]{1,0:T(8,128)S(1)} %get-tuple-element.52), channel_id=1, source_target_pairs={{0,1},{1,0},{2,3},{3,2},{4,5},{5,4},{6,7},{7,6},{8,9},{9,8},{10,11... | collective-permute-start | bytes 393224 | tf_op jit(solution)/shard_map/ppermute | solution.py:444
  10.0 23.1 %all-to-all-start = ((f32[8,72,128]{2,1,0:T(8,128)}), f32[8,72,128]{2,1,0:T(8,128)S(1)}, u32[]{:S(2)}, u32[]{:S(2)}) async-start(f32[8,72,128]{2,1,0:T(8,128)} %bitcast.2), calls=%async_computation | async-start | bytes 589824 | tf_op jit(solution)/shard_map/all_to_all | solution.py:493
  20.2 16.1 %collective-permute-start.2 = (f32[64,1024]{1,0:T(8,128)S(1)}, f32[64,1024]{1,0:T(8,128)S(1)}, u32[]{:S(2)}, u32[]{:S(2)}) collective-permute-start(f32[64,1024]{1,0:T(8,128)S(1)} %get-tuple-element.62), channel_id=1, source_target_pairs={{0,2},{1,3},{2,0},{3,1},{4,6},{5,7},{6,4},{7,5},{8,16},{9,17},{10,... | collective-permute-start | bytes 786440 | tf_op jit(solution)/shard_map/ppermute | solution.py:444
  20.7 12.4 %copy-start = (f32[128,1024]{1,0:T(8,128)S(1)}, f32[128,1024]{1,0:T(8,128)}, u32[]{:S(2)}) copy-start(f32[128,1024]{1,0:T(8,128)} %inj_ref.1) | copy-start | bytes 1572868
  20.7 15.6 %collective-permute-start.3 = (f32[64,1024]{1,0:T(8,128)S(1)}, f32[64,1024]{1,0:T(8,128)S(1)}, u32[]{:S(2)}, u32[]{:S(2)}) collective-permute-start(f32[64,1024]{1,0:T(8,128)S(1)} %get-tuple-element.63), channel_id=1, source_target_pairs={{0,8},{1,9},{2,10},{3,11},{4,12},{5,13},{6,14},{7,15},{8,0},{9,1},... | collective-permute-start | bytes 786440 | tf_op jit(solution)/shard_map/ppermute | solution.py:444
  37.3 11.5 %collective-permute-start.4 = (f32[16,1024]{1,0:T(8,128)S(1)}, f32[16,1024]{1,0:T(8,128)S(1)}, u32[]{:S(2)}, u32[]{:S(2)}) collective-permute-start(f32[16,1024]{1,0:T(8,128)S(1)} %get-tuple-element.73.yb), channel_id=1, source_target_pairs={{0,8},{1,2},{2,1},{3,4},{4,3},{5,6},{6,5},{7,15},{8,0},{9,10},{10,... | collective-permute-start | bytes 196616 | tf_op jit(solution)/shard_map/ppermute | solution.py:444
  40.4 9.8 %collective-permute-start.5 = (f32[16,1024]{1,0:T(8,128)S(1)}, f32[16,1024]{1,0:T(8,128)S(1)}, u32[]{:S(2)}, u32[]{:S(2)}) collective-permute-start(f32[16,1024]{1,0:T(8,128)S(1)} %get-tuple-element.72.ya), channel_id=1, source_target_pairs={{0,1},{1,0},{2,3},{3,2},{4,5},{5,4},{6,7},{7,6},{8,9},{9,8},{10,11... | collective-permute-start | bytes 196616 | tf_op jit(solution)/shard_map/ppermute | solution.py:444
  44.4 8.3 %collective-permute-start.6 = (f32[32,1024]{1,0:T(8,128)S(1)}, f32[32,1024]{1,0:T(8,128)S(1)}, u32[]{:S(2)}, u32[]{:S(2)}) collective-permute-start(f32[32,1024]{1,0:T(8,128)S(1)} %get-tuple-element.71.xb), channel_id=1, source_target_pairs={{0,2},{1,3},{2,0},{3,1},{4,6},{5,7},{6,4},{7,5},{8,16},{9,17},{10,... | collective-permute-start | bytes 393224 | tf_op jit(solution)/shard_map/ppermute | solution.py:444
  45.2 7.5 %collective-permute-start.7 = (f32[32,1024]{1,0:T(8,128)S(1)}, f32[32,1024]{1,0:T(8,128)S(1)}, u32[]{:S(2)}, u32[]{:S(2)}) collective-permute-start(f32[32,1024]{1,0:T(8,128)S(1)} %get-tuple-element.70.xa), channel_id=1, source_target_pairs={{0,8},{1,9},{2,10},{3,11},{4,12},{5,13},{6,14},{7,15},{8,0},{9,1},... | collective-permute-start | bytes 393224 | tf_op jit(solution)/shard_map/ppermute | solution.py:444
  52.8 9.9 %collective-permute-start.8 = (f32[16,1024]{1,0:T(8,128)S(1)}, f32[16,1024]{1,0:T(8,128)S(1)}, u32[]{:S(2)}, u32[]{:S(2)}) collective-permute-start(f32[16,1024]{1,0:T(8,128)S(1)} %get-tuple-element.87.yb), channel_id=1, source_target_pairs={{0,8},{1,2},{2,1},{3,4},{4,3},{5,6},{6,5},{7,15},{8,0},{9,10},{10,... | collective-permute-start | bytes 196616 | tf_op jit(solution)/shard_map/ppermute | solution.py:444
  54.4 11.1 %collective-permute-start.9 = (f32[16,1024]{1,0:T(8,128)S(1)}, f32[16,1024]{1,0:T(8,128)S(1)}, u32[]{:S(2)}, u32[]{:S(2)}) collective-permute-start(f32[16,1024]{1,0:T(8,128)S(1)} %get-tuple-element.86.ya), channel_id=1, source_target_pairs={{0,1},{1,0},{2,3},{3,2},{4,5},{5,4},{6,7},{7,6},{8,9},{9,8},{10,11... | collective-permute-start | bytes 196616 | tf_op jit(solution)/shard_map/ppermute | solution.py:444
  59.7 7.8 %collective-permute-start.10 = (f32[32,1024]{1,0:T(8,128)S(1)}, f32[32,1024]{1,0:T(8,128)S(1)}, u32[]{:S(2)}, u32[]{:S(2)}) collective-permute-start(f32[32,1024]{1,0:T(8,128)S(1)} %get-tuple-element.85.xb), channel_id=1, source_target_pairs={{0,2},{1,3},{2,0},{3,1},{4,6},{5,7},{6,4},{7,5},{8,16},{9,17},{10,... | collective-permute-start | bytes 393224 | tf_op jit(solution)/shard_map/ppermute | solution.py:444
  60.4 7.1 %collective-permute-start.11 = (f32[32,1024]{1,0:T(8,128)S(1)}, f32[32,1024]{1,0:T(8,128)S(1)}, u32[]{:S(2)}, u32[]{:S(2)}) collective-permute-start(f32[32,1024]{1,0:T(8,128)S(1)} %get-tuple-element.84.xa), channel_id=1, source_target_pairs={{0,8},{1,9},{2,10},{3,11},{4,12},{5,13},{6,14},{7,15},{8,0},{9,1},... | collective-permute-start | bytes 393224 | tf_op jit(solution)/shard_map/ppermute | solution.py:444
  67.6 10.4 %collective-permute-start.12 = (f32[16,1024]{1,0:T(8,128)S(1)}, f32[16,1024]{1,0:T(8,128)S(1)}, u32[]{:S(2)}, u32[]{:S(2)}) collective-permute-start(f32[16,1024]{1,0:T(8,128)S(1)} %get-tuple-element.93.yb), channel_id=1, source_target_pairs={{0,8},{1,2},{2,1},{3,4},{4,3},{5,6},{6,5},{7,15},{8,0},{9,10},{10,... | collective-permute-start | bytes 196616 | tf_op jit(solution)/shard_map/ppermute | solution.py:444
  68.9 9.6 %collective-permute-start.13 = (f32[16,1024]{1,0:T(8,128)S(1)}, f32[16,1024]{1,0:T(8,128)S(1)}, u32[]{:S(2)}, u32[]{:S(2)}) collective-permute-start(f32[16,1024]{1,0:T(8,128)S(1)} %get-tuple-element.92.ya), channel_id=1, source_target_pairs={{0,1},{1,0},{2,3},{3,2},{4,5},{5,4},{6,7},{7,6},{8,9},{9,8},{10,11... | collective-permute-start | bytes 196616 | tf_op jit(solution)/shard_map/ppermute | solution.py:444
  73.9 8.1 %collective-permute-start.14 = (f32[32,1024]{1,0:T(8,128)S(1)}, f32[32,1024]{1,0:T(8,128)S(1)}, u32[]{:S(2)}, u32[]{:S(2)}) collective-permute-start(f32[32,1024]{1,0:T(8,128)S(1)} %get-tuple-element.91.xb), channel_id=1, source_target_pairs={{0,2},{1,3},{2,0},{3,1},{4,6},{5,7},{6,4},{7,5},{8,16},{9,17},{10,... | collective-permute-start | bytes 393224 | tf_op jit(solution)/shard_map/ppermute | solution.py:444
  75.1 6.8 %collective-permute-start.15 = (f32[32,1024]{1,0:T(8,128)S(1)}, f32[32,1024]{1,0:T(8,128)S(1)}, u32[]{:S(2)}, u32[]{:S(2)}) collective-permute-start(f32[32,1024]{1,0:T(8,128)S(1)} %get-tuple-element.90.xa), channel_id=1, source_target_pairs={{0,8},{1,9},{2,10},{3,11},{4,12},{5,13},{6,14},{7,15},{8,0},{9,1},... | collective-permute-start | bytes 393224 | tf_op jit(solution)/shard_map/ppermute | solution.py:444

commit v5 on v4

--- a/solution.py
+++ b/solution.py
@@ -377,25 +377,10 @@
     lax.fori_loop(start, stop, inner, 0)
 
 
-def first_sweep_kernel(fx_hbm, fy_hbm, fz_hbm, rhs_ref, xa, xb, ya, yb, wx_ref, wy_ref, w_in, t_in,
-                       w_ref, t_ref, tn_ref, py_ref, fx_ref, fy_ref, fz_ref, sems):
-    step = CX // PARTS
-    pairs = ((fx_hbm, fx_ref), (fy_hbm, fy_ref), (fz_hbm, fz_ref))
-    copies = [[pltpu.make_async_copy(src.at[pl.ds(part * step, step)], dst.at[pl.ds(part * step, step)], sems.at[k, part])
-               for k, (src, dst) in enumerate(pairs)] for part in range(PARTS)]
-    for part in range(PARTS):
-        for copy in copies[part]:
-            copy.start()
+def first_sweep_kernel(fx_ref, fy_ref, fz_ref, rhs_ref, xa, xb, ya, yb, wx_ref, wy_ref, w_in, t_in,
+                       w_ref, t_ref, tn_ref, py_ref):
     put_edges(w_ref, wx_ref[0], wx_ref[1], wy_ref[0], wy_ref[1])
-    put_edges(t_ref, *split(xa[...], xb[...], even("gx")), *split(ya[...], yb[...], even("gy")))
-    refs = (t_ref, fx_ref, fy_ref, fz_ref, w_ref, rhs_ref, tn_ref, py_ref)
-    for part in range(PARTS):
-        for copy in copies[part]:
-            copy.wait()
-        if part == 0:
-            sweep_plane(0, True, False, *refs)
-        sweep_inside(refs, max(1, part * step), min(CX - 1, (part + 1) * step))
-    sweep_plane(CX - 1, False, True, *refs)
+    sweep(fx_ref, fy_ref, fz_ref, rhs_ref, w_ref, xa, xb, ya, yb, t_ref, tn_ref, py_ref)
 
 
 def sweep(fx_ref, fy_ref, fz_ref, rhs_ref, w_ref, xa, xb, ya, yb, t_ref, tn_ref, py_ref):
@@ -507,10 +492,10 @@
     for number in range(1, SWEEPS):
         halo = exchange(*faces)
         if number == 1:
-            w, temp, new, py, fx, fy, fz = call(
-                first_sweep_kernel, (SLAB, SLAB, SLAB, YY, SLAB, SLAB, SLAB), [HB] * 3 + [VM] * 9, [DMA((3, PARTS))],
-                alias={10: 0, 11: 1}, mib=2)(*far(*stored[:3]), *near(rhs, *faces, wx, wy, w, new))
-            coefs = near(fx, fy, fz, rhs)
+            coefs = near(*stored[:3], rhs)
+            w, temp, new, py = call(
+                first_sweep_kernel, (SLAB, SLAB, SLAB, YY), [VM] * 12, alias={10: 0, 11: 1}, mib=2)(
+                *coefs, *near(*faces, wx, wy, w, new))
         elif number < SWEEPS - 1:
             temp, new, py = call(sweep_kernel, (SLAB, SLAB, YY), [VM] * 10, alias={9: 0}, mib=2)(
                 *coefs, *near(w, *faces, new))

time: 83.5 us -> 84.4 us (1.011)
  the two profiles are of different devices: /device:TPU:14 before, /device:TPU:28 now
where the time goes in v5:
time: 84.4 us; the launch traced here: 84.2 us
  starting transfers between devices  44.3 us (52%)
  Pallas kernels  25.3 us (30%)
  waiting for transfers between devices  14.3 us (17%)
    ppermute x16, starting transfers between devices, swap(): lax.ppermute(value, ('gx', 'gy'), [(i, x * NGY + y) for i, (x, y) in enum...  34.4 us
    ppermute x16, waiting for transfers between devices, swap(): lax.ppermute(value, ('gx', 'gy'), [(i, x * NGY + y) for i, (x, y) in enum...  12.4 us
    all_to_all x1, starting transfers between devices, shards(): recv = lax.all_to_all(send, 'gy', 0, 0, tiled=True)  9.88 us
    pallas_call x1, Pallas kernels, shards(): call(coef_kernel, (pltpu.HBM((CX, CY, NZ), F32),) * 6 + (YY, YY, edge_x,...  9.39 us
    pallas_call x1, Pallas kernels, shards(): call(source_kernel, (SLAB,) * 3 + (edge_y,), [VM] * 2 + [HB] * 3 + [VM],...  3.38 us
    pallas_call x1, Pallas kernels, shards(): call(last_sweep_kernel, (SLAB, SLAB, YY, pltpu.HBM((CX, CY, NZ), F32)), [...  2.8 us
    pallas_call x1, Pallas kernels, shards(): call(start_kernel, (local(NGY * CHUNK, LW),) + (local(2 * CY, NZ),) * 2 +...  2.6 us
    pallas_call x1, Pallas kernels, shards(): call(first_sweep_kernel, (SLAB, SLAB, SLAB, YY), [VM] * 12, alias={10: 0,...  2.4 us
  transfers between devices with their start and end apart: 17, of which 6 were waited for; matrix products, arithmetic and copies ran while one was open for 0% of the time, Pallas kernels for 24%

profile of v5, /device:TPU:28, one launch (start us, length us, event | category | flops | bytes accessed | tf_op | source)
XLA Modules:
  0.0 84.2 jit_solution(7279097423619399449)
XLA Ops:
  0.0 0.0 copy-start.4
  0.0 2.6 %shard_map.82 = (f32[576,128]{1,0:T(8,128)}, f32[64,1024]{1,0:T(8,128)S(1)}, f32[64,1024]{1,0:T(8,128)S(1)}, f32[32,1024]{1,0:T(8,128)S(1)}, f32[32,1024]{1,0:T(8,128)S(1)}) custom-call(f32[16,32,1024]{2,1,0:T(8,128)} %t_hbm.3, s32[16,32,1024]{2,1,0:T(8,128)} %soil_hbm.3, f32[256,128]{1,0:T(8,128)} %loss_hbm.1, s32[1,256]{1,0:T(1,128)} %bitcast.5, ...), custom_call_target="tpu_custom_call" | custom-call | flops 100000000 | bytes 300000 | tf_op jit(solution)/shard_map/pallas_call | solution.py:473
  2.6 7.5 %collective-permute-start = (f32[32,1024]{1,0:T(8,128)S(1)}, f32[32,1024]{1,0:T(8,128)S(1)}, u32[]{:S(2)}, u32[]{:S(2)}) collective-permute-start(f32[32,1024]{1,0:T(8,128)S(1)} %get-tuple-element.48), channel_id=1, source_target_pairs={{0,8},{1,2},{2,1},{3,4},{4,3},{5,6},{6,5},{7,15},{8,0},{9,10},{10,... | collective-permute-start | bytes 393224 | tf_op jit(solution)/shard_map/ppermute | solution.py:429
  10.1 0.0 collective-permute-start.1
  10.1 9.9 %all-to-all-start = ((f32[8,72,128]{2,1,0:T(8,128)}), f32[8,72,128]{2,1,0:T(8,128)S(1)}, u32[]{:S(2)}, u32[]{:S(2)}) async-start(f32[8,72,128]{2,1,0:T(8,128)} %bitcast.2), calls=%async_computation | async-start | bytes 589824 | tf_op jit(solution)/shard_map/all_to_all | solution.py:478
  19.9 0.2 collective-permute-start.2
  20.2 0.0 copy-start.3
  20.2 0.9 %collective-permute-start.3 = (f32[64,1024]{1,0:T(8,128)S(1)}, f32[64,1024]{1,0:T(8,128)S(1)}, u32[]{:S(2)}, u32[]{:S(2)}) collective-permute-start(f32[64,1024]{1,0:T(8,128)S(1)} %get-tuple-element.60), channel_id=1, source_target_pairs={{0,8},{1,9},{2,10},{3,11},{4,12},{5,13},{6,14},{7,15},{8,0},{9,1},... | collective-permute-start | bytes 786440 | tf_op jit(solution)/shard_map/ppermute | solution.py:429
  21.1 0.0 collective-permute-done.hyb
  21.1 0.0 collective-permute-done.1.hya
  21.1 0.0 copy-done.4
  21.1 9.4 %shard_map.83 = (f32[16,32,1024]{2,1,0:T(8,128)}, f32[16,32,1024]{2,1,0:T(8,128)}, f32[16,32,1024]{2,1,0:T(8,128)}, f32[16,32,1024]{2,1,0:T(8,128)}, f32[16,32,1...) custom-call(f32[8]{0:T(128)S(1)} %copy-done.4, ...), custom_call_target="tpu_custom_call" | custom-call | flops 20000000000 | bytes 60000000 | tf_op jit(solution)/shard_map/pallas_call | solution.py:482
  30.5 1.9 %all-to-all-done = f32[8,72,128]{2,1,0:T(8,128)S(1)} async-done(((f32[8,72,128]{2,1,0:T(8,128)}), f32[8,72,128]{2,1,0:T(8,128)S(1)}, u32[]{:S(2)}, u32[]{:S(2)}) %all-to-all-start) | async-done | bytes 294944 | tf_op jit(solution)/shard_map/all_to_all | solution.py:478
  32.4 0.0 copy-done.3
  32.4 0.0 copy-start.2
  32.4 3.4 %shard_map.84 = (f32[16,32,1024]{2,1,0:T(8,128)S(1)}, f32[16,32,1024]{2,1,0:T(8,128)S(1)}, f32[16,32,1024]{2,1,0:T(8,128)S(1)}, f32[2,4,16,1024]{3,2,1,0:T(8,128)S(1)}) custom-call(f32[576,128]{1,0:T(8,128)S(1)} %bitcast.4, f32[128,1024]{1,0:T(8,128)S(1)} %copy-done.3, f32[16,32,1024]{2,1,0:T(8,128)} %get-tuple-element.54.rhs_hbm, ...), custom_call_target="tpu_custom_call", output_to_operand_aliasing={{3}: (5, {})} | custom-call | flops 100000000 | bytes 300000 | tf_op jit(solution)/shard_map/pallas_call | solution.py:487
  35.8 0.0 collective-permute-done.2.hxb
  35.8 0.0 collective-permute-done.3.hxa
  35.8 0.0 copy-start
  35.8 0.0 copy-start.1
  35.8 1.0 %shard_map.85 = (f32[32,1024]{1,0:T(8,128)S(1)}, f32[32,1024]{1,0:T(8,128)S(1)}, f32[16,1024]{1,0:T(8,128)S(1)}, f32[16,1024]{1,0:T(8,128)S(1)}, f32[2,32,1024]{...) custom-call(f32[8]{0:T(128)S(1)} %copy-done.4, ...), custom_call_target="tpu_custom_call" | custom-call | flops 100000000 | bytes 300000 | tf_op jit(solution)/shard_map/pallas_call | solution.py:490
  36.8 4.3 %collective-permute-start.5 = (f32[16,1024]{1,0:T(8,128)S(1)}, f32[16,1024]{1,0:T(8,128)S(1)}, u32[]{:S(2)}, u32[]{:S(2)}) collective-permute-start(f32[16,1024]{1,0:T(8,128)S(1)} %get-tuple-element.69.ya), channel_id=1, source_target_pairs={{0,1},{1,0},{2,3},{3,2},{4,5},{5,4},{6,7},{7,6},{8,9},{9,8},{10,11... | collective-permute-start | bytes 196616 | tf_op jit(solution)/shard_map/ppermute | solution.py:429
  41.1 2.6 %collective-permute-start.4 = (f32[16,1024]{1,0:T(8,128)S(1)}, f32[16,1024]{1,0:T(8,128)S(1)}, u32[]{:S(2)}, u32[]{:S(2)}) collective-permute-start(f32[16,1024]{1,0:T(8,128)S(1)} %get-tuple-element.70.yb), channel_id=1, source_target_pairs={{0,8},{1,2},{2,1},{3,4},{4,3},{5,6},{6,5},{7,15},{8,0},{9,10},{10,... | collective-permute-start | bytes 196616 | tf_op jit(solution)/shard_map/ppermute | solution.py:429
  43.8 0.0 collective-permute-start.7
  43.8 2.0 %collective-permute-start.6 = (f32[32,1024]{1,0:T(8,128)S(1)}, f32[32,1024]{1,0:T(8,128)S(1)}, u32[]{:S(2)}, u32[]{:S(2)}) collective-permute-start(f32[32,1024]{1,0:T(8,128)S(1)} %get-tuple-element.68.xb), channel_id=1, source_target_pairs={{0,2},{1,3},{2,0},{3,1},{4,6},{5,7},{6,4},{7,5},{8,16},{9,17},{10,... | collective-permute-start | bytes 393224 | tf_op jit(solution)/shard_map/ppermute | solution.py:429
  45.7 0.0 copy-done.2
  45.7 0.0 copy-done
  45.7 0.0 copy-done.1
  45.7 2.4 %shard_map.86 = (f32[16,32,1024]{2,1,0:T(8,128)S(1)}, f32[16,32,1024]{2,1,0:T(8,128)S(1)}, f32[16,32,1024]{2,1,0:T(8,128)S(1)}, f32[2,16,1024]{2,1,0:T(8,128)S(1)}) custom-call(f32[16,32,1024]{2,1,0:T(8,128)S(1)} %copy-done, f32[16,32,1024]{2,1,0:T(8,128)S(1)} %copy-done.1, ...), custom_call_target="tpu_custom_call", output_to_operand_aliasing={{0}: (10, {}), {1}: (11, {})} | custom-call | flops 100000000 | bytes 300000 | tf_op jit(solution)/shard_map/pallas_call | solution.py:496
  48.1 0.0 collective-permute-done.5.hya
  48.1 2.7 %collective-permute-done.4.hyb = f32[16,1024]{1,0:T(8,128)S(1)} collective-permute-done((f32[16,1024]{1,0:T(8,128)S(1)}, f32[16,1024]{1,0:T(8,128)S(1)}, u32[]{:S(2)}, u32[]{:S(2)}) %collective-permute-start.4) | collective-permute-done | bytes 65568 | tf_op jit(solution)/shard_map/ppermute | solution.py:429
  50.9 0.0 collective-permute-done.7.hxa
  50.9 1.1 %collective-permute-done.6.hxb = f32[32,1024]{1,0:T(8,128)S(1)} collective-permute-done((f32[32,1024]{1,0:T(8,128)S(1)}, f32[32,1024]{1,0:T(8,128)S(1)}, u32[]{:S(2)}, u32[]{:S(2)}) %collective-permute-start.6) | collective-permute-done | bytes 131104 | tf_op jit(solution)/shard_map/ppermute | solution.py:429
  52.0 0.1 shard_map.88
  52.1 0.1 collective-permute-start.9
  52.2 5.8 %collective-permute-start.8 = (f32[16,1024]{1,0:T(8,128)S(1)}, f32[16,1024]{1,0:T(8,128)S(1)}, u32[]{:S(2)}, u32[]{:S(2)}) collective-permute-start(f32[16,1024]{1,0:T(8,128)S(1)} %get-tuple-element.81.yb), channel_id=1, source_target_pairs={{0,8},{1,2},{2,1},{3,4},{4,3},{5,6},{6,5},{7,15},{8,0},{9,10},{10,... | collective-permute-start | bytes 196616 | tf_op jit(solution)/shard_map/ppermute | solution.py:429
  58.0 0.0 collective-permute-start.11
  58.0 2.5 %collective-permute-start.10 = (f32[32,1024]{1,0:T(8,128)S(1)}, f32[32,1024]{1,0:T(8,128)S(1)}, u32[]{:S(2)}, u32[]{:S(2)}) collective-permute-start(f32[32,1024]{1,0:T(8,128)S(1)} %get-tuple-element.79.xb), channel_id=1, source_target_pairs={{0,2},{1,3},{2,0},{3,1},{4,6},{5,7},{6,4},{7,5},{8,16},{9,17},{10,... | collective-permute-start | bytes 393224 | tf_op jit(solution)/shard_map/ppermute | solution.py:429
  60.4 2.3 %shard_map.89 = (f32[16,32,1024]{2,1,0:T(8,128)S(1)}, f32[16,32,1024]{2,1,0:T(8,128)S(1)}, f32[2,16,1024]{2,1,0:T(8,128)S(1)}) custom-call(f32[16,32,1024]{2,1,0:T(8,128)S(1)} %copy-done, f32[16,32,1024]{2,1,0:T(8,128)S(1)} %copy-done.1, f32[16,32,1024]{2,1,0:T(8,128)S(1)} %copy-done.2, ...), custom_call_target="tpu_custom_call", output_to_operand_aliasing={{0}: (9, {})} | custom-call | flops 100000000 | bytes 300000 | tf_op jit(solution)/shard_map/pallas_call | solution.py:500
  62.8 0.0 collective-permute-done.9.hya
  62.8 0.0 collective-permute-done.8.hyb
  62.8 0.0 collective-permute-done.11.hxa
  62.8 4.3 %collective-permute-done.10.hxb = f32[32,1024]{1,0:T(8,128)S(1)} collective-permute-done((f32[32,1024]{1,0:T(8,128)S(1)}, f32[32,1024]{1,0:T(8,128)S(1)}, u32[]{:S(2)}, u32[]{:S(2)}) %collective-permute-start.10) | collective-permute-done | bytes 131104 | tf_op jit(solution)/shard_map/ppermute | solution.py:429
  67.1 0.1 shard_map.91
  67.2 0.1 collective-permute-start.13
  67.3 7.1 %collective-permute-start.12 = (f32[16,1024]{1,0:T(8,128)S(1)}, f32[16,1024]{1,0:T(8,128)S(1)}, u32[]{:S(2)}, u32[]{:S(2)}) collective-permute-start(f32[16,1024]{1,0:T(8,128)S(1)} %get-tuple-element.87.yb), channel_id=1, source_target_pairs={{0,8},{1,2},{2,1},{3,4},{4,3},{5,6},{6,5},{7,15},{8,0},{9,10},{10,... | collective-permute-start | bytes 196616 | tf_op jit(solution)/shard_map/ppermute | solution.py:429
  74.5 0.0 collective-permute-start.15
  74.5 1.4 %collective-permute-start.14 = (f32[32,1024]{1,0:T(8,128)S(1)}, f32[32,1024]{1,0:T(8,128)S(1)}, u32[]{:S(2)}, u32[]{:S(2)}) collective-permute-start(f32[32,1024]{1,0:T(8,128)S(1)} %get-tuple-element.85.xb), channel_id=1, source_target_pairs={{0,2},{1,3},{2,0},{3,1},{4,6},{5,7},{6,4},{7,5},{8,16},{9,17},{10,... | collective-permute-start | bytes 393224 | tf_op jit(solution)/shard_map/ppermute | solution.py:429
  75.8 2.8 %shard_map.92 = (f32[16,32,1024]{2,1,0:T(8,128)S(1)}, f32[16,32,1024]{2,1,0:T(8,128)S(1)}, f32[2,16,1024]{2,1,0:T(8,128)S(1)}, f32[16,32,1024]{2,1,0:T(8,128)}) custom-call(f32[16,32,1024]{2,1,0:T(8,128)S(1)} %copy-done, f32[16,32,1024]{2,1,0:T(8,128)S(1)} %copy-done.1, f32[16,32,1024]{2,1,0:T(8,128)S(1)} %copy-done.2, ...), custom_call_target="tpu_custom_call", output_to_operand_aliasing={{0}: (9, {})} | custom-call | flops 100000000 | bytes 300000 | tf_op jit(solution)/shard_map/pallas_call | solution.py:503
  78.6 0.0 collective-permute-done.13.hya
  78.7 2.4 %collective-permute-done.12.hyb = f32[16,1024]{1,0:T(8,128)S(1)} collective-permute-done((f32[16,1024]{1,0:T(8,128)S(1)}, f32[16,1024]{1,0:T(8,128)S(1)}, u32[]{:S(2)}, u32[]{:S(2)}) %collective-permute-start.12) | collective-permute-done | bytes 65568 | tf_op jit(solution)/shard_map/ppermute | solution.py:429
  81.1 0.0 collective-permute-done.15.hxa
  81.1 1.8 %collective-permute-done.14.hxb = f32[32,1024]{1,0:T(8,128)S(1)} collective-permute-done((f32[32,1024]{1,0:T(8,128)S(1)}, f32[32,1024]{1,0:T(8,128)S(1)}, u32[]{:S(2)}, u32[]{:S(2)}) %collective-permute-start.14) | collective-permute-done | bytes 131104 | tf_op jit(solution)/shard_map/ppermute | solution.py:429
  82.9 1.1 %shard_map.94 = f32[16,32,1024]{2,1,0:T(8,128)} custom-call(f32[16,32,1024]{2,1,0:T(8,128)S(1)} %get-tuple-element.88.tn_ref, f32[2,16,1024]{2,1,0:T(8,128)S(1)} %get-tuple-element.89.py_ref, f32[2,32,1024]{2,1,0:T(8,128)S(1)} %get-tuple-element.76.ax_ref, f32[2,16,1024]{2,1,0:T(8,128)S(1)} %shard_map.93.gy_ref, ...), custom_call_target="tpu_custom_call", output_to_operand_aliasing={{}: (6, {})} | custom-call | flops 100000000 | bytes 300000 | tf_op jit(solution)/shard_map/pallas_call | solution.py:511
  (3 shorter events, 0.1 us)
Async XLA Ops:
  0.0 21.1 %copy-start.4 = (f32[8]{0:T(128)S(1)}, f32[8]{0:T(128)}, u32[]{:S(2)}) copy-start(f32[8]{0:T(128)} %table_ref.3) | copy-start | bytes 100
  2.6 18.5 %collective-permute-start = (f32[32,1024]{1,0:T(8,128)S(1)}, f32[32,1024]{1,0:T(8,128)S(1)}, u32[]{:S(2)}, u32[]{:S(2)}) collective-permute-start(f32[32,1024]{1,0:T(8,128)S(1)} %get-tuple-element.48), channel_id=1, source_target_pairs={{0,8},{1,2},{2,1},{3,4},{4,3},{5,6},{6,5},{7,15},{8,0},{9,10},{10,... | collective-permute-start | bytes 393224 | tf_op jit(solution)/shard_map/ppermute | solution.py:429
  10.1 11.0 %collective-permute-start.1 = (f32[32,1024]{1,0:T(8,128)S(1)}, f32[32,1024]{1,0:T(8,128)S(1)}, u32[]{:S(2)}, u32[]{:S(2)}) collective-permute-start(f32[32,1024]{1,0:T(8,128)S(1)} %get-tuple-element.49), channel_id=1, source_target_pairs={{0,1},{1,0},{2,3},{3,2},{4,5},{5,4},{6,7},{7,6},{8,9},{9,8},{10,11... | collective-permute-start | bytes 393224 | tf_op jit(solution)/shard_map/ppermute | solution.py:429
  10.1 22.3 %all-to-all-start = ((f32[8,72,128]{2,1,0:T(8,128)}), f32[8,72,128]{2,1,0:T(8,128)S(1)}, u32[]{:S(2)}, u32[]{:S(2)}) async-start(f32[8,72,128]{2,1,0:T(8,128)} %bitcast.2), calls=%async_computation | async-start | bytes 589824 | tf_op jit(solution)/shard_map/all_to_all | solution.py:478
  19.9 15.9 %collective-permute-start.2 = (f32[64,1024]{1,0:T(8,128)S(1)}, f32[64,1024]{1,0:T(8,128)S(1)}, u32[]{:S(2)}, u32[]{:S(2)}) collective-permute-start(f32[64,1024]{1,0:T(8,128)S(1)} %get-tuple-element.59), channel_id=1, source_target_pairs={{0,2},{1,3},{2,0},{3,1},{4,6},{5,7},{6,4},{7,5},{8,16},{9,17},{10,... | collective-permute-start | bytes 786440 | tf_op jit(solution)/shard_map/ppermute | solution.py:429
  20.2 12.2 %copy-start.3 = (f32[128,1024]{1,0:T(8,128)S(1)}, f32[128,1024]{1,0:T(8,128)}, u32[]{:S(2)}) copy-start(f32[128,1024]{1,0:T(8,128)} %inj_ref.1) | copy-start | bytes 1572868
  20.2 15.7 %collective-permute-start.3 = (f32[64,1024]{1,0:T(8,128)S(1)}, f32[64,1024]{1,0:T(8,128)S(1)}, u32[]{:S(2)}, u32[]{:S(2)}) collective-permute-start(f32[64,1024]{1,0:T(8,128)S(1)} %get-tuple-element.60), channel_id=1, source_target_pairs={{0,8},{1,9},{2,10},{3,11},{4,12},{5,13},{6,14},{7,15},{8,0},{9,1},... | collective-permute-start | bytes 786440 | tf_op jit(solution)/shard_map/ppermute | solution.py:429
  32.4 13.3 %copy-start.2 = (f32[16,32,1024]{2,1,0:T(8,128)S(1)}, f32[16,32,1024]{2,1,0:T(8,128)}, u32[]{:S(2)}) copy-start(f32[16,32,1024]{2,1,0:T(8,128)} %get-tuple-element.52.fz_ref) | copy-start | bytes 6291460
  35.8 9.9 %copy-start = (f32[16,32,1024]{2,1,0:T(8,128)S(1)}, f32[16,32,1024]{2,1,0:T(8,128)}, u32[]{:S(2)}) copy-start(f32[16,32,1024]{2,1,0:T(8,128)} %get-tuple-element.50.fx_ref) | copy-start | bytes 6291460
  35.8 9.9 %copy-start.1 = (f32[16,32,1024]{2,1,0:T(8,128)S(1)}, f32[16,32,1024]{2,1,0:T(8,128)}, u32[]{:S(2)}) copy-start(f32[16,32,1024]{2,1,0:T(8,128)} %get-tuple-element.51.fy_ref) | copy-start | bytes 6291460
  36.8 11.3 %collective-permute-start.5 = (f32[16,1024]{1,0:T(8,128)S(1)}, f32[16,1024]{1,0:T(8,128)S(1)}, u32[]{:S(2)}, u32[]{:S(2)}) collective-permute-start(f32[16,1024]{1,0:T(8,128)S(1)} %get-tuple-element.69.ya), channel_id=1, source_target_pairs={{0,1},{1,0},{2,3},{3,2},{4,5},{5,4},{6,7},{7,6},{8,9},{9,8},{10,11... | collective-permute-start | bytes 196616 | tf_op jit(solution)/shard_map/ppermute | solution.py:429
  41.1 9.7 %collective-permute-start.4 = (f32[16,1024]{1,0:T(8,128)S(1)}, f32[16,1024]{1,0:T(8,128)S(1)}, u32[]{:S(2)}, u32[]{:S(2)}) collective-permute-start(f32[16,1024]{1,0:T(8,128)S(1)} %get-tuple-element.70.yb), channel_id=1, source_target_pairs={{0,8},{1,2},{2,1},{3,4},{4,3},{5,6},{6,5},{7,15},{8,0},{9,10},{10,... | collective-permute-start | bytes 196616 | tf_op jit(solution)/shard_map/ppermute | solution.py:429
  43.8 7.1 %collective-permute-start.7 = (f32[32,1024]{1,0:T(8,128)S(1)}, f32[32,1024]{1,0:T(8,128)S(1)}, u32[]{:S(2)}, u32[]{:S(2)}) collective-permute-start(f32[32,1024]{1,0:T(8,128)S(1)} %get-tuple-element.67.xa), channel_id=1, source_target_pairs={{0,8},{1,9},{2,10},{3,11},{4,12},{5,13},{6,14},{7,15},{8,0},{9,1},... | collective-permute-start | bytes 393224 | tf_op jit(solution)/shard_map/ppermute | solution.py:429
  43.8 8.2 %collective-permute-start.6 = (f32[32,1024]{1,0:T(8,128)S(1)}, f32[32,1024]{1,0:T(8,128)S(1)}, u32[]{:S(2)}, u32[]{:S(2)}) collective-permute-start(f32[32,1024]{1,0:T(8,128)S(1)} %get-tuple-element.68.xb), channel_id=1, source_target_pairs={{0,2},{1,3},{2,0},{3,1},{4,6},{5,7},{6,4},{7,5},{8,16},{9,17},{10,... | collective-permute-start | bytes 393224 | tf_op jit(solution)/shard_map/ppermute | solution.py:429
  52.1 10.7 %collective-permute-start.9 = (f32[16,1024]{1,0:T(8,128)S(1)}, f32[16,1024]{1,0:T(8,128)S(1)}, u32[]{:S(2)}, u32[]{:S(2)}) collective-permute-start(f32[16,1024]{1,0:T(8,128)S(1)} %get-tuple-element.80.ya), channel_id=1, source_target_pairs={{0,1},{1,0},{2,3},{3,2},{4,5},{5,4},{6,7},{7,6},{8,9},{9,8},{10,11... | collective-permute-start | bytes 196616 | tf_op jit(solution)/shard_map/ppermute | solution.py:429
  52.2 10.6 %collective-permute-start.8 = (f32[16,1024]{1,0:T(8,128)S(1)}, f32[16,1024]{1,0:T(8,128)S(1)}, u32[]{:S(2)}, u32[]{:S(2)}) collective-permute-start(f32[16,1024]{1,0:T(8,128)S(1)} %get-tuple-element.81.yb), channel_id=1, source_target_pairs={{0,8},{1,2},{2,1},{3,4},{4,3},{5,6},{6,5},{7,15},{8,0},{9,10},{10,... | collective-permute-start | bytes 196616 | tf_op jit(solution)/shard_map/ppermute | solution.py:429
  58.0 4.8 %collective-permute-start.11 = (f32[32,1024]{1,0:T(8,128)S(1)}, f32[32,1024]{1,0:T(8,128)S(1)}, u32[]{:S(2)}, u32[]{:S(2)}) collective-permute-start(f32[32,1024]{1,0:T(8,128)S(1)} %get-tuple-element.78.xa), channel_id=1, source_target_pairs={{0,8},{1,9},{2,10},{3,11},{4,12},{5,13},{6,14},{7,15},{8,0},{9,1},... | collective-permute-start | bytes 393224 | tf_op jit(solution)/shard_map/ppermute | solution.py:429
  58.0 9.2 %collective-permute-start.10 = (f32[32,1024]{1,0:T(8,128)S(1)}, f32[32,1024]{1,0:T(8,128)S(1)}, u32[]{:S(2)}, u32[]{:S(2)}) collective-permute-start(f32[32,1024]{1,0:T(8,128)S(1)} %get-tuple-element.79.xb), channel_id=1, source_target_pairs={{0,2},{1,3},{2,0},{3,1},{4,6},{5,7},{6,4},{7,5},{8,16},{9,17},{10,... | collective-permute-start | bytes 393224 | tf_op jit(solution)/shard_map/ppermute | solution.py:429
  67.2 11.4 %collective-permute-start.13 = (f32[16,1024]{1,0:T(8,128)S(1)}, f32[16,1024]{1,0:T(8,128)S(1)}, u32[]{:S(2)}, u32[]{:S(2)}) collective-permute-start(f32[16,1024]{1,0:T(8,128)S(1)} %get-tuple-element.86.ya), channel_id=1, source_target_pairs={{0,1},{1,0},{2,3},{3,2},{4,5},{5,4},{6,7},{7,6},{8,9},{9,8},{10,11... | collective-permute-start | bytes 196616 | tf_op jit(solution)/shard_map/ppermute | solution.py:429
  67.3 13.7 %collective-permute-start.12 = (f32[16,1024]{1,0:T(8,128)S(1)}, f32[16,1024]{1,0:T(8,128)S(1)}, u32[]{:S(2)}, u32[]{:S(2)}) collective-permute-start(f32[16,1024]{1,0:T(8,128)S(1)} %get-tuple-element.87.yb), channel_id=1, source_target_pairs={{0,8},{1,2},{2,1},{3,4},{4,3},{5,6},{6,5},{7,15},{8,0},{9,10},{10,... | collective-permute-start | bytes 196616 | tf_op jit(solution)/shard_map/ppermute | solution.py:429
  74.5 6.6 %collective-permute-start.15 = (f32[32,1024]{1,0:T(8,128)S(1)}, f32[32,1024]{1,0:T(8,128)S(1)}, u32[]{:S(2)}, u32[]{:S(2)}) collective-permute-start(f32[32,1024]{1,0:T(8,128)S(1)} %get-tuple-element.84.xa), channel_id=1, source_target_pairs={{0,8},{1,9},{2,10},{3,11},{4,12},{5,13},{6,14},{7,15},{8,0},{9,1},... | collective-permute-start | bytes 393224 | tf_op jit(solution)/shard_map/ppermute | solution.py:429
  74.5 8.4 %collective-permute-start.14 = (f32[32,1024]{1,0:T(8,128)S(1)}, f32[32,1024]{1,0:T(8,128)S(1)}, u32[]{:S(2)}, u32[]{:S(2)}) collective-permute-start(f32[32,1024]{1,0:T(8,128)S(1)} %get-tuple-element.85.xb), channel_id=1, source_target_pairs={{0,2},{1,3},{2,0},{3,1},{4,6},{5,7},{6,4},{7,5},{8,16},{9,17},{10,... | collective-permute-start | bytes 393224 | tf_op jit(solution)/shard_map/ppermute | solution.py:429
